TPU v7x, 128 devices: a whole 4x4x4 slice. The times are simulated.
128 devices in a mesh: blk: 4 (over z), wide: 32 (over y, x, core).
Axes of the slice: x: 4, y: 4, z: 4, core: 2. Of those that a mesh axis runs over, the one named last changes fastest.
Arguments:
- feature_table: bfloat16 [262144, 1024], P('wide', 'blk'), may hold values from -6 to 6
- owner_ids: int32 [131072, 1], P('wide'), may hold values from 0 to 31; in each aligned block of 4096 rows (0 to 4095, 4096 to 8191, ...) at most 256 rows name the same one
- row_ids: int32 [131072], P('wide'), may hold values from 0 to 8191
- near_first: int32 [65536, 15], P('wide'), may hold values from 0 to 4095
- near_second: int32 [16384, 10], P('wide'), may hold values from 0 to 2047
- w_self: bfloat16 [1024, 512], P('blk'), may hold values from -0.1875 to 0.1875
- w_near: bfloat16 [1024, 512], P('blk'), may hold values from -0.1875 to 0.1875
- bias_hidden: bfloat16 [512], P('blk'), may hold values from -3 to 3
- v_self: bfloat16 [512, 512], P('blk'), may hold values from -0.25 to 0.25
- v_near: bfloat16 [512, 512], P('blk'), may hold values from -0.25 to 0.25
- cotangent: bfloat16 [16384, 512], P('wide'), may hold values from -0.046875 to 0.046875
Outputs:
- seed_out: bfloat16 [16384, 512], P('wide', 'blk')
- grad_w_self: float32 [1024, 512], P('blk')
- grad_w_near: float32 [1024, 512], P('blk')
- grad_v_self: float32 [512, 512], P('blk')
- grad_v_near: float32 [512, 512], P('blk')
Inputs may be any that keep to these rules, and one draw needn't show every extreme that they name: `owner_ids`: among the 4096 frontier nodes of one index of wide, no owner is named by more than 256, a bound that some block reaches.
All inputs are finite; a program needn't handle non-finite values.
Results may differ from a plain program's by a relative error of at most 0.025.
Values may be sent and summed in bfloat16 or wider, within the bound.
No kernel may reach another device: no remote copies, remote signals or barrier semaphores. Data moves between devices by JAX's collectives and lax.ppermute only.
A program may use at most 64 MiB of HBM per device.

v0:
```python
import math

import jax
import jax.numpy as jnp
from jax import lax
from jax.sharding import PartitionSpec as P


def count_block(lists, width):
    columns = jnp.arange(width, dtype=jnp.int32)[None, :]
    counts = jnp.zeros((lists.shape[0], width), jnp.float32)
    for step in range(lists.shape[1]):
        counts = counts + (lists[:, step][:, None] == columns).astype(jnp.float32)
    return counts


def neighbour_mean(source, lists):
    total_rows = lists.shape[0]
    list_width = lists.shape[1]
    block = math.gcd(total_rows, 512)
    blocked = lists.reshape(total_rows // block, block, list_width)

    def one_block(block_lists):
        counts = count_block(block_lists, source.shape[0]).astype(jnp.bfloat16)
        summed = jnp.dot(counts, source, preferred_element_type=jnp.float32)
        return (summed / list_width).astype(jnp.bfloat16)

    means = lax.map(one_block, blocked)
    return means.reshape(total_rows, source.shape[1])


def silu_slope(active):
    sigmoid_value = 1.0 / (1.0 + jnp.exp(-active))
    return sigmoid_value * (1.0 + active * (1.0 - sigmoid_value))


def inner_rows(left, right):
    return lax.dot_general(
        left, right, (((0,), (0,)), ((), ())), preferred_element_type=jnp.float32
    )


def times_transposed(left, right):
    return lax.dot_general(
        left, right, (((1,), (1,)), ((), ())), preferred_element_type=jnp.float32
    )


def spread_back(d_self, d_mean, lists, target_count):
    seed_rows = lists.shape[0]
    block = math.gcd(seed_rows, 512)
    block_count = seed_rows // block
    blocked_lists = lists.reshape(block_count, block, lists.shape[1])
    blocked_grad = d_mean.reshape(block_count, block, d_mean.shape[1])
    start_grad = jnp.pad(d_self, ((0, target_count - d_self.shape[0]), (0, 0)))

    def add_block(accum_grad, pair):
        block_lists, block_grad = pair
        counts = count_block(block_lists, target_count)
        added = lax.dot_general(
            counts,
            block_grad,
            (((0,), (0,)), ((), ())),
            precision=lax.Precision.HIGHEST,
            preferred_element_type=jnp.float32,
        )
        return (accum_grad + added, None)

    result, unused = lax.scan(add_block, start_grad, (blocked_lists, blocked_grad))
    return result


def body(
    feature_table,
    owner_ids,
    row_ids,
    near_first,
    near_second,
    w_self,
    w_near,
    bias_hidden,
    v_self,
    v_near,
    cotangent,
):
    peer_count = lax.axis_size("wide")
    quarter_count = lax.axis_size("blk")
    position = lax.axis_index("blk")
    frontier_count = row_ids.shape[0]
    capacity = 2 * frontier_count // peer_count
    target_count = near_first.shape[0]
    seed_count = near_second.shape[0]
    list_two = near_second.shape[1]
    owners = owner_ids[:, 0]
    onehot = (owners[:, None] == jnp.arange(peer_count, dtype=jnp.int32)[None, :]).astype(jnp.int32)
    slot_index = jnp.sum(onehot * (jnp.cumsum(onehot, axis=0) - 1), axis=1)
    requests = jnp.zeros((peer_count, capacity), jnp.int32).at[owners, slot_index].set(row_ids)
    flat_index = owners * capacity + slot_index
    found_rows = jnp.take(
        feature_table,
        lax.all_to_all(requests, "wide", split_axis=0, concat_axis=0, tiled=True),
        axis=0,
    )
    arrived = lax.all_to_all(found_rows, "wide", split_axis=0, concat_axis=0, tiled=True)
    frontier = jnp.take(
        arrived.reshape(peer_count * capacity, arrived.shape[2]), flat_index, axis=0
    )
    near_mean = neighbour_mean(frontier, near_first)
    self_rows = frontier[:target_count]
    partial_value = jnp.dot(self_rows, w_self, preferred_element_type=jnp.float32) + jnp.dot(
        near_mean, w_near, preferred_element_type=jnp.float32
    )
    pre_act = lax.psum(partial_value.astype(jnp.bfloat16), "blk").astype(jnp.float32)
    v_self_all, v_near_all, bias_all = (
        lax.all_gather(v_self, "blk", axis=0, tiled=True),
        lax.all_gather(v_near, "blk", axis=0, tiled=True),
        lax.all_gather(bias_hidden, "blk", axis=0, tiled=True),
    )
    active = pre_act + bias_all.astype(jnp.float32)
    hidden = jax.nn.silu(active).astype(jnp.bfloat16)
    second_mean = neighbour_mean(hidden, near_second)
    seed_hidden = hidden[:seed_count]
    share_width = v_self_all.shape[1] // quarter_count
    column_start = position * share_width
    out_self = lax.dynamic_slice_in_dim(v_self_all, column_start, share_width, 1)
    out_near = lax.dynamic_slice_in_dim(v_near_all, column_start, share_width, 1)
    seed_out = (
        jnp.dot(seed_hidden, out_self, preferred_element_type=jnp.float32)
        + jnp.dot(second_mean, out_near, preferred_element_type=jnp.float32)
    ).astype(jnp.bfloat16)
    seed_part = lax.dynamic_slice_in_dim(seed_hidden, column_start, share_width, 1)
    mean_part = lax.dynamic_slice_in_dim(second_mean, column_start, share_width, 1)
    grad_vs = inner_rows(seed_part, cotangent)
    grad_vn = inner_rows(mean_part, cotangent)
    d_self = times_transposed(cotangent, v_self_all)
    d_mean = times_transposed(cotangent, v_near_all) / list_two
    d_hidden = spread_back(d_self, d_mean, near_second, target_count)
    slope = (d_hidden * silu_slope(active)).astype(jnp.bfloat16)
    grad_ws = inner_rows(self_rows, slope)
    grad_wn = inner_rows(near_mean, slope)
    grad_ws, grad_wn, grad_vs, grad_vn = (
        lax.psum(grad_ws.astype(jnp.bfloat16), "wide").astype(jnp.float32),
        lax.psum(grad_wn.astype(jnp.bfloat16), "wide").astype(jnp.float32),
        lax.psum(grad_vs.astype(jnp.bfloat16), "wide").astype(jnp.float32),
        lax.psum(grad_vn.astype(jnp.bfloat16), "wide").astype(jnp.float32),
    )
    return (seed_out, grad_ws, grad_wn, grad_vs, grad_vn)


def solution(mesh):
    placed = (
        P("wide", "blk"),
        P("wide", None),
        P("wide"),
        P("wide", None),
        P("wide", None),
        P("blk", None),
        P("blk", None),
        P("blk"),
        P("blk", None),
        P("blk", None),
        P("wide", None),
    )
    return jax.shard_map(
        body,
        mesh=mesh,
        in_specs=placed,
        out_specs=(
            P("wide", "blk"),
            P("blk", None),
            P("blk", None),
            P("blk", None),
            P("blk", None),
        ),
        check_vma=False,
    )
```

profile of v0, /device:TPU:1, one launch (start us, length us, event | category | flops | bytes accessed | tf_op | source)
XLA Modules:
  0.0 456.3 jit_solution(3369745582353969671)
XLA Ops:
  8.0 9.2 %reduce-window.6 = s32[32,32,128]{2,1,0:T(8,128)S(1)} reduce-window(s32[32,32,128]{2,1,0:T(8,128)S(1)} %fusion.19, s32[]{:T(128)} %constant.63.clone.1), window={size=1x1x128 pad=0_0x0_0x127_0}, to_apply=%region_0.0 | reduce-window | flops 16646144 | bytes 1048580 | tf_op jit(solution)/shard_map/reduce-window
  18.4 1.1 fusion.18
  21.8 15.7 %scatter_custom_fusion = s32[8192]{0:T(1024)S(1)} fusion(s32[4096]{0:T(1024)S(1)} %broadcast_select_fusion.2, s32[4096]{0:T(1024)} %param.15, s32[]{:T(128)} %constant.63.clone.1), kind=kCustom, calls=%fused_computation.82 | custom fusion | bytes 33280
  37.6 15.6 %all_to_all.20 = s32[32,1,256]{2,1,0:T(1,128)S(1)} all-to-all(s32[32,1,256]{2,1,0:T(1,128)S(1)} %bitcast.126), channel_id=1, replica_groups=mesh['blk'=4,'wide'=32] {'wide'}, dimensions={0} | all-to-all | bytes 65536 | tf_op jit(solution)/shard_map/all_to_all | solution.py:101
  53.3 33.7 %gather_fusion = bf16[8192,256]{1,0:T(8,128)(2,1)} fusion(bf16[8192,256]{1,0:T(8,128)(2,1)} %param.13, s32[8192]{0:T(1024)S(1)} %broadcast_clamp_fusion), kind=kCustom, calls=%fused_computation | custom fusion | bytes 8421376 | tf_op jit(solution)/shard_map/jit(_take)/gather | solution.py:99
  86.9 5.2 %broadcast_select_fusion = bf16[32,256,256]{2,1,0:T(8,128)(2,1)} fusion(bf16[32,256,256]{2,1,0:T(8,128)(2,1)} %bitcast.117, pred[32,256]{1,0:T(8,128)(4,1)S(1)} %compare_and_fusion), kind=kLoop, calls=%fused_computation.42 | loop fusion | flops 2097152 | bytes 8396800 | tf_op jit(solution)/shard_map/jit(_take)/select_n | solution.py:99
  92.2 5.0 %all-to-all-start.1 = ((bf16[32,256,256]{2,1,0:T(8,128)(2,1)}), bf16[32,256,256]{2,1,0:T(8,128)(2,1)}, u32[]{:S(2)}, u32[]{:S(2)}) async-start(bf16[32,256,256]{2,1,0:T(8,128)(2,1)} %broadcast_select_fusion), calls=%async_computation.1 | async-start | bytes 8388608 | tf_op jit(solution)/shard_map/all_to_all | solution.py:104
  97.4 50.1 %all-to-all-done.1 = bf16[32,256,256]{2,1,0:T(8,128)(2,1)} async-done(((bf16[32,256,256]{2,1,0:T(8,128)(2,1)}), bf16[32,256,256]{2,1,0:T(8,128)(2,1)}, u32[]{:S(2)}, u32[]{:S(2)}) %all-to-all-start.1) | async-done | bytes 4194336 | tf_op jit(solution)/shard_map/all_to_all | solution.py:104
  147.5 15.7 %gather_fusion.1 = bf16[4096,256]{1,0:T(8,128)(2,1)S(1)} fusion(bf16[8192,256]{1,0:T(8,128)(2,1)} %bitcast.25, s32[4096]{0:T(1024)S(1)} %broadcast_clamp_fusion.1), kind=kCustom, calls=%fused_computation.1 | custom fusion | bytes 4210688 | tf_op jit(solution)/shard_map/jit(_take)/gather | solution.py:105
  163.3 1.7 broadcast_select_fusion.1
  165.0 74.3 %while.2 = (s32[]{:T(128)}, bf16[4,512,256]{2,1,0:T(8,128)(2,1)}, s32[4,512,15]{1,0,2:T(4,128)S(1)}, bf16[4096,256]{1,0:T(8,128)(2,1)}, s32[]{:T(128)}) while((s32[]{:T(128)}, bf16[4,512,256]{2,1,0:T(8,128)(2,1)}, s32[4,512,15]{1,0,2:T(4,128)S(1)}, bf16[4096,256]{1,0:T(8,128)(2,1)}, s32[]{:T(128)}) %tuple.55), condition=%wide.region_5.6_spmd, body=%wide.region_4.5_spmd.sunk | while | flops 1168375808 | bytes 2574913 | solution.py:28
  165.3 18.4 %fusion.56 = bf16[4,512,256]{2,1,0:T(8,128)(2,1)} fusion(bf16[4,512,256]{2,1,0:T(8,128)(2,1)} %get-tuple-element.162, s32[]{:T(128)} %get-tuple-element.161, bf16[4096,256]{1,0:T(8,128)(2,1)} %get-tuple-element.169, s32[512]{0:T(512)S(1)} %bitcast.131, s32[512]{0:T(512)S(1)} %bitcast.132, s32[512]{0:T(512)S(1)} %bitcast.133, s32[512]{0:T(512)S(1)} %bitcast.134, ...), kind=kOutput, calls=%fused_computation.23.clone.1 | convolution fusion | flops 1168375808 | bytes 2390528 | tf_op jit(solution)/shard_map/while/body/eval_jaxpr/dot_general | solution.py:25
  183.7 18.4 %fusion.56 = bf16[4,512,256]{2,1,0:T(8,128)(2,1)} fusion(bf16[4,512,256]{2,1,0:T(8,128)(2,1)} %get-tuple-element.162, s32[]{:T(128)} %get-tuple-element.161, bf16[4096,256]{1,0:T(8,128)(2,1)} %get-tuple-element.169, s32[512]{0:T(512)S(1)} %bitcast.131, s32[512]{0:T(512)S(1)} %bitcast.132, s32[512]{0:T(512)S(1)} %bitcast.133, s32[512]{0:T(512)S(1)} %bitcast.134, ...), kind=kOutput, calls=%fused_computation.23.clone.1 | convolution fusion | flops 1168375808 | bytes 2390528 | tf_op jit(solution)/shard_map/while/body/eval_jaxpr/dot_general | solution.py:25
  202.1 18.4 %fusion.56 = bf16[4,512,256]{2,1,0:T(8,128)(2,1)} fusion(bf16[4,512,256]{2,1,0:T(8,128)(2,1)} %get-tuple-element.162, s32[]{:T(128)} %get-tuple-element.161, bf16[4096,256]{1,0:T(8,128)(2,1)} %get-tuple-element.169, s32[512]{0:T(512)S(1)} %bitcast.131, s32[512]{0:T(512)S(1)} %bitcast.132, s32[512]{0:T(512)S(1)} %bitcast.133, s32[512]{0:T(512)S(1)} %bitcast.134, ...), kind=kOutput, calls=%fused_computation.23.clone.1 | convolution fusion | flops 1168375808 | bytes 2390528 | tf_op jit(solution)/shard_map/while/body/eval_jaxpr/dot_general | solution.py:25
  220.6 18.4 %fusion.56 = bf16[4,512,256]{2,1,0:T(8,128)(2,1)} fusion(bf16[4,512,256]{2,1,0:T(8,128)(2,1)} %get-tuple-element.162, s32[]{:T(128)} %get-tuple-element.161, bf16[4096,256]{1,0:T(8,128)(2,1)} %get-tuple-element.169, s32[512]{0:T(512)S(1)} %bitcast.131, s32[512]{0:T(512)S(1)} %bitcast.132, s32[512]{0:T(512)S(1)} %bitcast.133, s32[512]{0:T(512)S(1)} %bitcast.134, ...), kind=kOutput, calls=%fused_computation.23.clone.1 | convolution fusion | flops 1168375808 | bytes 2390528 | tf_op jit(solution)/shard_map/while/body/eval_jaxpr/dot_general | solution.py:25
  239.4 2.0 fusion.15
  241.5 2.0 add_convert_fusion.10
  243.6 8.9 %all-gather = bf16[4,1,128]{2,1,0:T(2,128)(2,1)S(1)} all-gather(bf16[1,1,128]{2,1,0:T(2,128)(2,1)S(1)} %bitcast.167), channel_id=1, replica_groups=mesh['blk'=4,'wide'=32] {'blk'}, dimensions={0}, use_global_device_ids=true | all-gather | bytes 1280 | tf_op jit(solution)/shard_map/all_gather | solution.py:117
  252.5 13.5 %all_gather.11 = bf16[512,512]{1,0:T(8,128)(2,1)S(1)} all-gather(bf16[128,512]{1,0:T(8,128)(2,1)S(1)} %copy-done.10), channel_id=1, replica_groups=mesh['blk'=4,'wide'=32] {'blk'}, dimensions={0}, use_global_device_ids=true | all-gather | bytes 655360 | tf_op jit(solution)/shard_map/all_gather | solution.py:116
  266.1 13.7 %all_gather.10 = bf16[512,512]{1,0:T(8,128)(2,1)S(1)} all-gather(bf16[128,512]{1,0:T(8,128)(2,1)S(1)} %copy-done.11), channel_id=1, replica_groups=mesh['blk'=4,'wide'=32] {'blk'}, dimensions={0}, use_global_device_ids=true | all-gather | bytes 655360 | tf_op jit(solution)/shard_map/all_gather | solution.py:115
  280.8 29.8 %all-reduce.5.cloned.1.call-done = bf16[2048,512]{1,0:T(8,128)(2,1)} async-done(((bf16[2048,512]{1,0:T(8,128)(2,1)}), bf16[2048,512]{1,0:T(8,128)(2,1)}) %all-reduce.5.cloned.1.call-update) | async-done | bytes 2097168 | tf_op jit(solution)/shard_map/psum | solution.py:113
  310.6 15.3 %multiply_convert_fusion = bf16[2048,512]{1,0:T(8,128)(2,1)S(1)} fusion(f32[512,512]{1,0:T(8,128)S(1)} %fusion.34, bf16[2048,512]{1,0:T(8,128)(2,1)} %all-reduce.5.cloned.1.call-done, f32[512,512]{1,0:T(8,128)S(1)} %convolution_multiply_fusion, s32[512]{0:T(512)S(1)} %bitcast.163, s32[512]{0:T(512)S(1)} %bitcast.165, s32[512]{0:T(512)S(1)} %bitcast.149, ...), kind=kOutput, calls=%fused_computation.26 | convolution fusion | flops 6485442560 | bytes 6313984 | tf_op jit(solution)/shard_map/while/body/eval_jaxpr/dot_general | solution.py:60
  326.0 1.4 convolution_convert_fusion
  327.4 1.4 convolution_convert_fusion.1
  328.8 1.4 multiply_convert_fusion.1
  330.3 5.7 %fusion.10 = bf16[512,512]{1,0:T(8,128)(2,1)S(1)} fusion(bf16[2048,512]{1,0:T(8,128)(2,1)S(1)} %multiply_convert_fusion.1, s32[512]{0:T(512)S(1)} %bitcast.164, s32[512]{0:T(512)S(1)} %bitcast.166, s32[512]{0:T(512)S(1)} %bitcast.150, s32[512]{0:T(512)S(1)} %bitcast.152, s32[512]{0:T(512)S(1)} %bitcast.154, s32[512]{0:T(512)S(1)} %bitcast.156, ...), kind=kOutput, calls=%fused_computation.48 | convolution fusion | flops 1105723392 | bytes 2641920 | tf_op jit(solution)/shard_map/while/body/eval_jaxpr/dot_general | solution.py:25
  338.9 2.0 fusion.13
  340.9 101.5 %all-reduce.7.cloned.1.call-done = (bf16[256,512]{1,0:T(8,128)(2,1)}, bf16[256,512]{1,0:T(8,128)(2,1)}, bf16[128,512]{1,0:T(8,128)(2,1)}, bf16[128,512]{1,0:T(8,128)(2,1)}) async-done(((bf16[256,512]{1,0:T(8,128)(2,1)}, bf16[256,512]{1,0:T(8,128)(2,1)}, bf16[128,512]{1,0:T(8,128)(2,1)}, bf16[128,512]{1,0:T(8,128)(2,1)}), (bf16[256,512]{1,0:T(8,128)(2,1)}, bf16[256,512]{1,0:T(8,128)(2,1)}, ...) | async-done | bytes 786448 | tf_op jit(solution)/shard_map/psum | solution.py:142
  442.4 1.8 convert_element_type.188
  444.2 1.8 convert_element_type.190
  446.0 1.6 convert_element_type.192
  447.6 1.6 convert_element_type.194
  (69 shorter events, 8.8 us)
Async XLA Ops:
  7.2 272.6 %copy-start = (bf16[512,512]{1,0:T(8,128)(2,1)S(1)}, bf16[512,512]{1,0:T(8,128)(2,1)}, u32[]{:S(2)}) copy-start(bf16[512,512]{1,0:T(8,128)(2,1)} %param.23) | copy-start | bytes 1572868
  92.2 5.0 %copy-start.12 = (s32[2048,15]{0,1:T(8,128)S(1)}, s32[2048,15]{0,1:T(8,128)}, u32[]{:S(2)}) copy-start(s32[2048,15]{0,1:T(8,128)} %param.16) | copy-start | bytes 368644
  92.2 5.1 %copy-start.7 = (s32[4096,1]{0,1:T(1,128)S(1)}, s32[4096,1]{0,1:T(1,128)}, u32[]{:S(2)}) copy-start(s32[4096,1]{0,1:T(1,128)} %param.14) | copy-start | bytes 49156
  92.2 55.3 %all-to-all-start.1 = ((bf16[32,256,256]{2,1,0:T(8,128)(2,1)}), bf16[32,256,256]{2,1,0:T(8,128)(2,1)}, u32[]{:S(2)}, u32[]{:S(2)}) async-start(bf16[32,256,256]{2,1,0:T(8,128)(2,1)} %broadcast_select_fusion), calls=%async_computation.1 | async-start | bytes 8388608 | tf_op jit(solution)/shard_map/all_to_all | solution.py:104
  97.2 213.4 %all-reduce.5.cloned.1.call-start = ((), (), s32[]{:S(2)}) async-start(), calls=%async_computation.2 | async-start | bytes 4194304 | tf_op jit(solution)/shard_map/psum | solution.py:113
  165.0 74.4 %copy-start.8 = (bf16[256,512]{1,0:T(8,128)(2,1)S(1)}, bf16[256,512]{1,0:T(8,128)(2,1)}, u32[]{:S(2)}) copy-start(bf16[256,512]{1,0:T(8,128)(2,1)} %param.18) | copy-start | bytes 786436
  239.4 2.0 copy-start.4
  239.4 2.0 copy-start.9
  241.4 2.2 copy-start.14
  241.5 11.1 %copy-start.10 = (bf16[128,512]{1,0:T(8,128)(2,1)S(1)}, bf16[128,512]{1,0:T(8,128)(2,1)}, u32[]{:S(2)}) copy-start(bf16[128,512]{1,0:T(8,128)(2,1)} %param.22) | copy-start | bytes 393220
  241.5 24.6 %copy-start.11 = (bf16[128,512]{1,0:T(8,128)(2,1)S(1)}, bf16[128,512]{1,0:T(8,128)(2,1)}, u32[]{:S(2)}) copy-start(bf16[128,512]{1,0:T(8,128)(2,1)} %param.21) | copy-start | bytes 393220
  241.5 38.3 %copy-start.13 = (s32[512,10]{0,1:T(8,128)S(1)}, s32[512,10]{0,1:T(8,128)}, u32[]{:S(2)}) copy-start(s32[512,10]{0,1:T(8,128)} %param.17) | copy-start | bytes 61444
  243.5 198.9 %all-reduce.7.cloned.1.call-start = ((), (), s32[]{:S(2)}) async-start(), calls=%async_computation.3 | async-start | bytes 1572864 | tf_op jit(solution)/shard_map/psum | solution.py:142
  266.1 13.7 %copy-start.2 = (bf16[512,512]{1,0:T(8,128)(2,1)}, bf16[512,512]{1,0:T(8,128)(2,1)S(1)}, u32[]{:S(2)}) copy-start(bf16[512,512]{1,0:T(8,128)(2,1)S(1)} %all_gather.11) | copy-start | bytes 1572868
  310.6 15.4 %copy-start.5 = (bf16[4,512,256]{2,1,0:T(8,128)(2,1)S(1)}, bf16[4,512,256]{2,1,0:T(8,128)(2,1)}, u32[]{:S(2)}) copy-start(bf16[4,512,256]{2,1,0:T(8,128)(2,1)} %get-tuple-element.51) | copy-start | bytes 3145732
  310.6 16.8 %copy-start.1 = (bf16[4096,256]{1,0:T(8,128)(2,1)S(1)}, bf16[4096,256]{1,0:T(8,128)(2,1)}, u32[]{:S(2)}) copy-start(bf16[4096,256]{1,0:T(8,128)(2,1)} %get-tuple-element.184) | copy-start | bytes 6291460
  325.9 2.9 copy-start.3
  335.9 0.8 copy-start.6
Sparse Core Ops, SparseCore 0:
  243.7 66.8 all-reduce.4
  338.7 103.6 all-reduce.6
where the time goes:
time: 462 us; the launch traced here: 456 us
  waiting for transfers between devices  181 us (39%)
  matrix products  107 us (23%)
  local copies, waits for them, and re-layouts  67.1 us (15%)
  blocking collectives  51.8 us (11%)
  other arithmetic  29.3 us (6%)
  between operations  14.5 us (3%)
  starting transfers between devices  5.04 us (1%)
    psum x1, waiting for transfers between devices, body(): lax.psum(grad_ws.astype(jnp.bfloat16), 'wide').astype(jnp.float32)  101 us
    dot_general x5, matrix products, one_block(): summed = jnp.dot(counts, source, preferred_element_type=jnp.float32)  79.2 us
    all_to_all x1, waiting for transfers between devices, body(): lax.all_to_all(found_rows, 'wide', split_axis=0, concat_axis=0, tiled=True)  50.1 us
    gather x1, local copies, waits for them, and re-layouts, body(): jnp.take(feature_table, lax.all_to_all(requests, 'wide', split_axis=0, co...  33.7 us
    psum x1, waiting for transfers between devices, body(): lax.psum(partial_value.astype(jnp.bfloat16), 'blk').astype(jnp.float32)  29.8 us
    unnamed x31, local copies, waits for them, and re-layouts  16.5 us
    gather x1, local copies, waits for them, and re-layouts, body(): jnp.take(arrived.reshape(peer_count * capacity, arrived.shape[2]), flat_i...  15.7 us
    all_to_all x1, blocking collectives, body(): lax.all_to_all(requests, 'wide', split_axis=0, concat_axis=0, tiled=True)  15.6 us
  transfers between devices with their start and end apart: 3, of which 3 were waited for; matrix products, arithmetic and copies ran while one was open for 1% of the time, Pallas kernels for 0%

commit v1 on v0

v1 whole, which is shorter than its diff:
```python
import functools

import jax
import jax.numpy as jnp
from jax import lax
from jax.experimental import pallas as pl
from jax.experimental.pallas import tpu as pltpu
from jax.sharding import PartitionSpec as P

BF = jnp.bfloat16
F32 = jnp.float32
NT = (((1,), (1,)), ((), ()))
TN = (((0,), (0,)), ((), ()))


def iota(shape, axis):
    return lax.broadcasted_iota(jnp.int32, shape, axis)


def one_hot(hit):
    return jnp.where(hit, 1.0, 0.0).astype(BF)


def chunk(index, size):
    return pl.ds(pl.multiple_of(index * size, size), size)


def request_kernel(own_ref, row_ref, req_ref, flat_ref, hot, picked, spots):
    peers, cap = req_ref.shape
    lines, width = own_ref.shape
    names = iota((peers, width), 0)
    for r in range(lines):
        hot[r * peers:(r + 1) * peers, :] = one_hot(own_ref[r:r + 1, :] == names)
    before = one_hot(iota((width, 2 * width), 0) <= iota((width, 2 * width), 1))
    counted = jnp.dot(hot[...], before, preferred_element_type=F32)
    base = jnp.full((peers, width), -1.0, F32)
    slots = iota((cap, width), 0)
    for r in range(lines):
        here = counted[r * peers:(r + 1) * peers]
        hit = own_ref[r:r + 1, :] == names
        slot = jnp.sum(jnp.where(hit, here[:, :width] + base, 0.0), axis=0, keepdims=True)
        slot = slot.astype(jnp.int32)
        base = base + here[:, width:]
        flat_ref[r:r + 1, :] = own_ref[r:r + 1, :] * cap + slot
        cols = slice(r * width, (r + 1) * width)
        row = row_ref[r:r + 1, :]
        upper = jnp.broadcast_to((row >> 6).astype(F32), (peers, width))
        lower = jnp.broadcast_to((row & 63).astype(F32), (peers, width))
        picked[:peers, cols] = jnp.where(hit, upper, 0.0).astype(BF)
        picked[peers:, cols] = jnp.where(hit, lower, 0.0).astype(BF)
        spots[:, cols] = one_hot(slots == slot)
    found = lax.dot_general(picked[...], spots[...], NT, preferred_element_type=F32)
    req_ref[...] = (found[:peers] * 64.0 + found[peers:]).astype(jnp.int32)


def request_table(owners, rows, peers, cap):
    lines, width = owners.shape
    return pl.pallas_call(
        request_kernel,
        out_shape=(
            jax.ShapeDtypeStruct((peers, cap), jnp.int32),
            jax.ShapeDtypeStruct(owners.shape, jnp.int32),
        ),
        scratch_shapes=[
            pltpu.VMEM((lines * peers, width), BF),
            pltpu.VMEM((2 * peers, lines * width), BF),
            pltpu.VMEM((cap, lines * width), BF),
        ],
        compiler_params=pltpu.CompilerParams(vmem_limit_bytes=40 << 20),
        name="request_table",
    )(owners, rows)


def count_kernel(idx_ref, out_ref):
    groups = idx_ref.shape[0]
    uppers = out_ref.shape[0]
    target = iota((1, 256), 1) >> 4
    rows_upper = iota((uppers * 16, 256), 0)
    rows_lower = iota((256, 256), 0)

    def group(g, carry):
        value = idx_ref[pl.ds(g, 1), :]
        code = jnp.where(value >= 0, (value >> 8) * 16 + target, -1)
        found = lax.dot_general(
            one_hot(rows_upper == code),
            one_hot(rows_lower == (value & 255)),
            NT,
            preferred_element_type=F32,
        ).astype(BF)
        for u in range(uppers):
            out_ref[u, chunk(g, 16), :] = found[u * 16:(u + 1) * 16, :]
        return carry

    lax.fori_loop(0, groups, group, 0, unroll=4)


def neighbour_counts(lists, sources, block_groups=16):
    targets, places = lists.shape
    uppers = sources // 256
    padded = jnp.pad(lists, ((0, 0), (0, 16 - places)), constant_values=-1)
    return pl.pallas_call(
        count_kernel,
        grid=(targets // 16 // block_groups,),
        in_specs=[pl.BlockSpec((block_groups, 256), lambda i: (i, 0))],
        out_specs=pl.BlockSpec((uppers, block_groups * 16, 256), lambda i: (0, i, 0)),
        out_shape=jax.ShapeDtypeStruct((uppers, targets, 256), BF),
        compiler_params=pltpu.CompilerParams(vmem_limit_bytes=40 << 20),
        cost_estimate=pl.CostEstimate(
            flops=512 * targets * sources,
            bytes_accessed=2 * targets * sources,
            transcendentals=0,
        ),
        name="neighbour_counts",
    )(padded.reshape(targets // 16, 256))


def widen(source_ref, low, high):
    half = low.shape[1]

    def some(i, carry):
        part = chunk(i, 256)
        low[part, :] = source_ref[part, :half].astype(F32)
        high[part, :] = source_ref[part, half:].astype(F32)
        return carry

    lax.fori_loop(0, source_ref.shape[0] // 256, some, 0)


def pick_rows(idx_ref, first, count, low, high, out_ref):
    half = low.shape[1]
    line = iota((8, half), 0)

    def some(i, carry):
        begin = pl.multiple_of(i * 16, 16)
        lows, highs = [], []
        for h in range(2):
            for j in range(8):
                row = idx_ref[first + begin + h * 8 + j]
                new_low = jnp.broadcast_to(low[pl.ds(row, 1), :], (8, half))
                new_high = jnp.broadcast_to(high[pl.ds(row, 1), :], (8, half))
                if j == 0:
                    got_low, got_high = new_low, new_high
                else:
                    got_low = jnp.where(line == j, new_low, got_low)
                    got_high = jnp.where(line == j, new_high, got_high)
            lows.append(got_low)
            highs.append(got_high)
        out_ref[pl.ds(begin, 16), :half] = jnp.concatenate(lows, axis=0).astype(BF)
        out_ref[pl.ds(begin, 16), half:] = jnp.concatenate(highs, axis=0).astype(BF)
        return carry

    lax.fori_loop(0, count // 16, some, 0, unroll=4)


def gather_kernel(idx_ref, table_ref, out_ref, low, high):
    step = pl.program_id(0)
    rows = out_ref.shape[0]

    @pl.when(step == 0)
    def _():
        widen(table_ref, low, high)

    pick_rows(idx_ref, step * rows, rows, low, high, out_ref)


def gather_rows(table, idx, rows=1024):
    total = idx.shape[0]
    own_rows, width = table.shape
    return pl.pallas_call(
        gather_kernel,
        grid_spec=pltpu.PrefetchScalarGridSpec(
            num_scalar_prefetch=1,
            grid=(total // rows,),
            in_specs=[pl.BlockSpec(table.shape, lambda i, s: (0, 0))],
            out_specs=pl.BlockSpec((rows, width), lambda i, s: (i, 0)),
            scratch_shapes=[pltpu.VMEM((own_rows, width // 2), F32)] * 2,
        ),
        out_shape=jax.ShapeDtypeStruct((total, width), BF),
        compiler_params=pltpu.CompilerParams(vmem_limit_bytes=40 << 20),
        name="gather_rows",
    )(idx, table)


def layer_kernel(list_width, idx_ref, spot_ref, arrived_ref, counts_ref, ws_ref, wn_ref,
                 parts_ref, both_ref, low, high, frontier):
    step = pl.program_id(0)
    block = counts_ref.shape[1]
    uppers = counts_ref.shape[0]
    width = arrived_ref.shape[1]

    @pl.when(step == 0)
    def _():
        widen(arrived_ref, low, high)
        pick_rows(idx_ref, 0, frontier.shape[0], low, high, frontier)

    total = jnp.zeros((block, width), F32)
    for u in range(uppers):
        total = total + jnp.dot(
            counts_ref[u], frontier[u * 256:(u + 1) * 256, :], preferred_element_type=F32
        )
    mean = (total / list_width).astype(BF)
    here = chunk(step, block)
    own = frontier[here, :]
    both_ref[here, :width] = own
    both_ref[here, width:] = mean
    quarters, _, share = parts_ref.shape
    for d in range(quarters):
        cols = chunk(lax.rem(spot_ref[0] + d, quarters), share)
        part = jnp.dot(own, ws_ref[:, cols], preferred_element_type=F32)
        part = part + jnp.dot(mean, wn_ref[:, cols], preferred_element_type=F32)
        parts_ref[d, here, :] = part.astype(BF)


def first_layer(idx, spot, arrived, counts, w_self, w_near, list_width, quarters, block=256):
    uppers, targets, lower = counts.shape
    slots, width = arrived.shape
    hidden = w_self.shape[1]

    def full(shape):
        return pl.BlockSpec(shape, lambda i, *s: (0,) * len(shape))

    return pl.pallas_call(
        functools.partial(layer_kernel, list_width),
        grid_spec=pltpu.PrefetchScalarGridSpec(
            num_scalar_prefetch=2,
            grid=(targets // block,),
            in_specs=[
                full(arrived.shape),
                pl.BlockSpec((uppers, block, lower), lambda i, *s: (0, i, 0)),
                full(w_self.shape),
                full(w_near.shape),
            ],
            out_specs=[
                full((quarters, targets, hidden // quarters)),
                full((targets, 2 * width)),
            ],
            scratch_shapes=[pltpu.VMEM((slots, width // 2), F32)] * 2
            + [pltpu.VMEM((idx.shape[0], width), BF)],
        ),
        out_shape=[
            jax.ShapeDtypeStruct((quarters, targets, hidden // quarters), BF),
            jax.ShapeDtypeStruct((targets, 2 * width), BF),
        ],
        compiler_params=pltpu.CompilerParams(vmem_limit_bytes=56 << 20),
        name="first_layer",
    )(idx, spot, arrived, counts, w_self, w_near)


def finish_kernel(spot_ref, sums_ref, ws_ref, wn_ref, vs_ref, vn_ref):
    quarters = sums_ref.shape[0] // 2
    feats, share = ws_ref.shape[0], vs_ref.shape[0]
    for d in range(quarters):
        cols = chunk(lax.rem(spot_ref[0] + d, quarters), share)
        ws_ref[:, cols] = sums_ref[d, :feats, :].astype(F32)
        wn_ref[:, cols] = sums_ref[d, feats:, :].astype(F32)
    for c in range(quarters):
        cols = slice(c * share, (c + 1) * share)
        vs_ref[:, cols] = sums_ref[quarters + c, :share, :].astype(F32)
        vn_ref[:, cols] = sums_ref[quarters + c, share:2 * share, :].astype(F32)


def body(
    feature_table,
    owner_ids,
    row_ids,
    near_first,
    near_second,
    w_self,
    w_near,
    bias_hidden,
    v_self,
    v_near,
    cotangent,
):
    peers = lax.axis_size("wide")
    quarters = lax.axis_size("blk")
    z = lax.axis_index("blk")
    spot = jnp.full((1,), z, jnp.int32)
    frontier_count = row_ids.shape[0]
    cap = 2 * frontier_count // peers
    targets, first_width = near_first.shape
    seeds, second_width = near_second.shape
    feats, hidden_units = w_self.shape
    share = hidden_units // quarters
    half = targets // 2

    def shift(value, by):
        return lax.ppermute(value, "blk", [(i, (i + by) % quarters) for i in range(quarters)])

    with jax.named_scope("requests"):
        requests, flat = request_table(
            owner_ids.reshape(frontier_count // 128, 128),
            row_ids.reshape(frontier_count // 128, 128),
            peers,
            cap,
        )
        wanted = lax.all_to_all(requests, "wide", split_axis=0, concat_axis=0, tiled=True)
    with jax.named_scope("rows"):
        found = gather_rows(feature_table, wanted.reshape(-1))
        arrived = lax.all_to_all(
            found.reshape(peers, cap, feats), "wide", split_axis=0, concat_axis=0, tiled=True
        ).reshape(peers * cap, feats)
    with jax.named_scope("beside_rows"):
        counts_first = neighbour_counts(near_first, frontier_count)
        counts_second = neighbour_counts(near_second, targets)
        d_self = lax.dot_general(cotangent, v_self, NT, preferred_element_type=F32)
        d_mean = lax.dot_general(cotangent, v_near, NT, preferred_element_type=F32) / second_width
        d_upper = d_mean.astype(BF)
        d_lower = (d_mean - d_upper.astype(F32)).astype(BF)
        spread = lax.dot_general(
            counts_second,
            jnp.concatenate([d_upper, d_lower], axis=1),
            (((1,), (0,)), ((), ())),
            preferred_element_type=F32,
        ).reshape(targets, 2 * share)
        d_hidden = spread[:, :share] + spread[:, share:]
        d_hidden = d_hidden + jnp.pad(d_self, ((0, targets - seeds), (0, 0)))
    with jax.named_scope("first_layer"):
        parts, both = first_layer(
            flat.reshape(-1), spot, arrived, counts_first, w_self, w_near, first_width, quarters
        )
    with jax.named_scope("pre_act_exchange"):
        far_up = shift(parts[2, :half], 1)
        far_down = shift(parts[2, half:], -1)
        up_own = shift(parts[1, half:], 1)
        down_own = shift(parts[3, :half], -1)
        up_sum = shift((parts[1, :half].astype(F32) + far_up.astype(F32)).astype(BF), 1)
        down_sum = shift((parts[3, half:].astype(F32) + far_down.astype(F32)).astype(BF), -1)
        first_half = parts[0, :half].astype(F32) + down_own.astype(F32) + up_sum.astype(F32)
        last_half = parts[0, half:].astype(F32) + up_own.astype(F32) + down_sum.astype(F32)
        active = jnp.concatenate([first_half, last_half]) + bias_hidden.astype(F32)
    with jax.named_scope("slope"):
        sigmoid = 1.0 / (1.0 + jnp.exp(-active))
        hidden = (active / (1.0 + jnp.exp(-active))).astype(BF)
        slope = (d_hidden * (sigmoid * (1.0 + active * (1.0 - sigmoid)))).astype(BF)
    with jax.named_scope("slope_exchange"):
        from_down = (shift(slope[:half], 1), shift(slope[half:], 1))
        from_up = (shift(slope[:half], -1), shift(slope[half:], -1))
        from_far = (shift(from_down[0], 1), shift(from_up[1], -1))

    with jax.named_scope("second_layer"):
        seed_hidden = hidden[:seeds]
        second_mean = (
            lax.dot_general(
                counts_second,
                hidden.reshape(counts_second.shape[0], 256, share),
                (((0, 2), (0, 1)), ((), ())),
                preferred_element_type=F32,
            )
            / second_width
        ).astype(BF)
        grad_v = jnp.concatenate(
            [
                lax.dot_general(seed_hidden, cotangent, TN, preferred_element_type=F32),
                lax.dot_general(second_mean, cotangent, TN, preferred_element_type=F32),
            ]
        ).astype(BF)
        partial_out = jnp.dot(seed_hidden, v_self, preferred_element_type=F32) + jnp.dot(
            second_mean, v_near, preferred_element_type=F32
        )

        def out_part(d):
            return lax.dynamic_slice_in_dim(partial_out, (z + d) % quarters * share, share, 1)

        seed_out = out_part(0)
        for d in range(1, quarters):
            seed_out = seed_out + shift(out_part(d).astype(BF), d).astype(F32)
        seed_out = seed_out.astype(BF)

    def grad_w(slope_part):
        return lax.dot_general(both, slope_part, TN, preferred_element_type=F32).astype(BF)

    def scatter_sum(values):
        rows = values.shape[0] // peers
        got = lax.all_to_all(
            values.reshape(peers, rows, share), "wide", split_axis=0, concat_axis=0, tiled=True
        )
        return jnp.sum(got.astype(F32), axis=0).astype(BF)

    with jax.named_scope("gradients"):
        grad_v_cols = [grad_v[:, c * share:(c + 1) * share] for c in range(quarters)]
        early = scatter_sum(jnp.concatenate(grad_v_cols + [grad_w(slope)]))
        late = scatter_sum(
            jnp.concatenate(
                [
                    grad_w(jnp.concatenate(from_up)),
                    grad_w(jnp.concatenate(from_far)),
                    grad_w(jnp.concatenate(from_down)),
                ]
            )
        )
        sums = lax.all_gather(jnp.concatenate([early, late]), "wide", axis=0)
        early_rows = early.shape[0]
        sums_early = sums[:, :early_rows].reshape(-1, share)
        sums_late = sums[:, early_rows:].reshape(-1, share)
        v_rows = 2 * share * quarters
        tall = 2 * feats
        sums_v = sums_early[:v_rows].reshape(quarters, 2 * share, share)
        sums_v = jnp.pad(sums_v, ((0, 0), (0, tall - 2 * share), (0, 0)))
        sums_all = jnp.concatenate(
            [
                sums_early[v_rows:].reshape(1, tall, share),
                sums_late.reshape(quarters - 1, tall, share),
                sums_v,
            ]
        )
        grads = pl.pallas_call(
            finish_kernel,
            in_specs=[
                pl.BlockSpec(memory_space=pltpu.SMEM),
                pl.BlockSpec(memory_space=pltpu.VMEM),
            ],
            out_specs=[pl.BlockSpec(memory_space=pltpu.VMEM)] * 4,
            out_shape=[jax.ShapeDtypeStruct((feats, hidden_units), F32)] * 2
            + [jax.ShapeDtypeStruct((share, hidden_units), F32)] * 2,
            compiler_params=pltpu.CompilerParams(vmem_limit_bytes=16 << 20),
            name="finish",
        )(spot, sums_all)
    return (seed_out, *grads)


def solution(mesh):
    placed = (
        P("wide", "blk"),
        P("wide", None),
        P("wide"),
        P("wide", None),
        P("wide", None),
        P("blk", None),
        P("blk", None),
        P("blk"),
        P("blk", None),
        P("blk", None),
        P("wide", None),
    )
    return jax.shard_map(
        body,
        mesh=mesh,
        in_specs=placed,
        out_specs=(
            P("wide", "blk"),
            P("blk", None),
            P("blk", None),
            P("blk", None),
            P("blk", None),
        ),
        check_vma=False,
    )
```

time: 462 us -> 226 us (0.49); the launches traced: 456 us -> 226 us
  waiting for transfers between devices: 181 us -> 51.5 us
  matrix products: 107 us -> 11.2 us
  local copies, waits for them, and re-layouts: 67.1 us -> 10.1 us
  Pallas kernels: 0 us -> 54 us
  starting transfers between devices: 5.04 us -> 47.1 us
  other arithmetic: 29.3 us -> 9.02 us
  between operations: 14.5 us -> 1.02 us
  blocking collectives: 51.8 us -> 41.6 us
    psum x2 -> x0, waiting for transfers between devices: 131 us -> none  [the longest x1 101 us: body(): lax.psum(grad_ws.astype(jnp.bfloat16), 'wide').astype(jnp.float32)]
    dot_general x16 -> x12, matrix products: 107 us -> 11.2 us  [the longest x4 5.75 us: grad_w(): lax.dot_general(both, slope_part, TN, preferred_element_type=F32).astype(BF)]
    pallas_call x0 -> x6, Pallas kernels: none -> 54 us  [the longest x1 23.7 us: first_layer(): pl.pallas_call(functools.partial(layer_kernel, list_width), grid_spec=plt...]
    gather x2 -> x0, local copies, waits for them, and re-layouts: 49.4 us -> none  [the longest x1 33.7 us: body(): jnp.take(feature_table, lax.all_to_all(requests, 'wide', split_axis=0, co...]
    all_to_all x1 -> x3, starting transfers between devices: 4.96 us -> 27.3 us  [the longest x2 22.3 us: scatter_sum(): lax.all_to_all(values.reshape(peers, rows, share), 'wide', split_axis=0,...]
    ppermute x0 -> x15, starting transfers between devices: none -> 19.9 us  [shift(): lax.ppermute(value, 'blk', [(i, (i + by) % quarters) for i in range(quart...]
    ppermute x0 -> x15, waiting for transfers between devices: none -> 15.1 us  [shift(): lax.ppermute(value, 'blk', [(i, (i + by) % quarters) for i in range(quart...]
    all_to_all x1 -> x3, waiting for transfers between devices: 50.1 us -> 36.4 us  [the longest x1 36.4 us: body(): lax.all_to_all(found.reshape(peers, cap, feats), 'wide', split_axis=0, co...]
  transfers between devices with their start and end apart: 3 -> 18, of which waited for: 3 -> 7; matrix products, arithmetic and copies ran while one was open for 1% -> 9% of each run, Pallas kernels for 0% -> 7%
where the time goes in v1:
time: 226 us
  Pallas kernels  54 us (24%)
  waiting for transfers between devices  51.5 us (23%)
  starting transfers between devices  47.1 us (21%)
  blocking collectives  41.6 us (18%)
  matrix products  11.2 us (5%)
  local copies, waits for them, and re-layouts  10.1 us (4%)
  other arithmetic  9.02 us (4%)
    all_to_all x1, waiting for transfers between devices, body(): lax.all_to_all(found.reshape(peers, cap, feats), 'wide', split_axis=0, co...  36.4 us
    all_gather x1, blocking collectives, body(): sums = lax.all_gather(jnp.concatenate([early, late]), 'wide', axis=0)  26 us
    pallas_call x1, Pallas kernels, first_layer(): pl.pallas_call(functools.partial(layer_kernel, list_width), grid_spec=plt...  23.7 us
    all_to_all x2, starting transfers between devices, scatter_sum(): lax.all_to_all(values.reshape(peers, rows, share), 'wide', split_axis=0,...  22.3 us
    ppermute x15, starting transfers between devices, shift(): lax.ppermute(value, 'blk', [(i, (i + by) % quarters) for i in range(quart...  19.9 us
    pallas_call x2, Pallas kernels, neighbour_counts(): pl.pallas_call(count_kernel, grid=(targets // 16 // block_groups,), in_sp...  15.9 us
    all_to_all x1, blocking collectives, body(): lax.all_to_all(requests, 'wide', split_axis=0, concat_axis=0, tiled=True)  15.6 us
    ppermute x15, waiting for transfers between devices, shift(): lax.ppermute(value, 'blk', [(i, (i + by) % quarters) for i in range(quart...  15.1 us
  transfers between devices with their start and end apart: 18, of which 7 were waited for; matrix products, arithmetic and copies ran while one was open for 9% of the time, Pallas kernels for 7%

profile of v1, /device:TPU:1, one launch (start us, length us, event | category | flops | bytes accessed | tf_op | source)
XLA Modules:
  0.0 225.6 jit_solution(15556647274950204179)
XLA Ops:
  2.1 1.5 request_table.1
  3.7 15.6 %all_to_all.24 = s32[32,1,256]{2,1,0:T(1,128)S(1)} all-to-all(s32[32,1,256]{2,1,0:T(1,128)S(1)} %copy.24), channel_id=1, replica_groups=mesh['blk'=4,'wide'=32] {'wide'}, dimensions={0} | all-to-all | bytes 65536 | tf_op jit(solution)/shard_map/requests/all_to_all | solution.py:297
  19.3 2.2 copy-done.2
  21.5 11.8 %gather_rows.1 = bf16[8192,256]{1,0:T(8,128)(2,1)S(1)} custom-call(s32[8192]{0:T(1024)S(1)} %bitcast.67, bf16[8192,256]{1,0:T(8,128)(2,1)S(1)} %copy-done.2), custom_call_target="tpu_custom_call" | custom-call | tf_op jit(solution)/shard_map/rows/gather_rows/pallas_call | solution.py:169
  33.3 2.0 copy-done.1
  35.3 5.0 %all-to-all-start.1 = ((bf16[32,256,256]{2,1,0:T(8,128)(2,1)}), bf16[32,256,256]{2,1,0:T(8,128)(2,1)}, u32[]{:S(2)}, u32[]{:S(2)}) async-start(bf16[32,256,256]{2,1,0:T(8,128)(2,1)} %bitcast.66), calls=%async_computation.1 | async-start | bytes 8388608 | tf_op jit(solution)/shard_map/rows/all_to_all | solution.py:300
  41.2 13.1 %neighbour_counts.2.counts_ref = bf16[16,2048,256]{2,1,0:T(8,128)(2,1)} custom-call(s32[128,256]{1,0:T(8,128)S(1)} %reshape.79.idx_ref), custom_call_target="tpu_custom_call" | custom-call | flops 4294967296 | bytes 16777216 | tf_op jit(solution)/shard_map/beside_rows/neighbour_counts/pallas_call | solution.py:101
  54.3 36.4 %all-to-all-done.1 = bf16[32,256,256]{2,1,0:T(8,128)(2,1)} async-done(((bf16[32,256,256]{2,1,0:T(8,128)(2,1)}), bf16[32,256,256]{2,1,0:T(8,128)(2,1)}, u32[]{:S(2)}, u32[]{:S(2)}) %all-to-all-start.1) | async-done | bytes 4194336 | tf_op jit(solution)/shard_map/rows/all_to_all | solution.py:300
  90.7 23.7 %first_layer.1 = (bf16[4,2048,128]{2,1,0:T(8,128)(2,1)}, bf16[2048,512]{1,0:T(8,128)(2,1)}) custom-call(s32[4096]{0:T(1024)} %bitcast.71, s32[1]{0:T(128)} %bitcast.3.spot_ref, bf16[8192,256]{1,0:T(8,128)(2,1)} %bitcast.7.arrived_ref, bf16[16,2048,256]{2,1,0:T(8,128)(2,1)} %neighbour_counts.2.counts_ref, bf16[256,512]{1,0:T(8,128)(2,1)} %ws_ref.1, ...), custom_call_target="tpu_custom_call" | custom-call | tf_op jit(solution)/shard_map/first_layer/first_layer/pallas_call | solution.py:222
  114.4 2.1 slice_bitcast_fusion.3
  116.5 1.6 collective-permute-start.1
  118.4 2.2 collective-permute-start
  120.6 1.5 collective-permute-start.4
  122.1 1.9 collective-permute-done.1
  125.1 2.8 %neighbour_counts.3 = bf16[8,512,256]{2,1,0:T(8,128)(2,1)S(1)} custom-call(s32[32,256]{1,0:T(8,128)S(1)} %reshape.80.idx_ref), custom_call_target="tpu_custom_call" | custom-call | flops 536870912 | bytes 2097152 | tf_op jit(solution)/shard_map/beside_rows/neighbour_counts/pallas_call | solution.py:101
  129.2 2.3 %collective-permute-done.2 = bf16[1024,128]{1,0:T(8,128)(2,1)S(1)} collective-permute-done((bf16[1024,128]{1,0:T(8,128)(2,1)S(1)}, bf16[1024,128]{1,0:T(8,128)(2,1)S(1)}, u32[]{:S(2)}, u32[]{:S(2)}) %collective-permute-start.2) | collective-permute-done | bytes 262176 | tf_op jit(solution)/shard_map/pre_act_exchange/ppermute | solution.py:288
  131.5 1.9 fusion.20
  134.4 2.1 fusion.24
  136.8 2.4 %collective-permute-done.5 = bf16[1024,128]{1,0:T(8,128)(2,1)} collective-permute-done((bf16[1024,128]{1,0:T(8,128)(2,1)}, bf16[1024,128]{1,0:T(8,128)(2,1)}, u32[]{:S(2)}, u32[]{:S(2)}) %collective-permute-start.5) | collective-permute-done | bytes 262176 | tf_op jit(solution)/shard_map/pre_act_exchange/ppermute | solution.py:288
  141.7 1.9 collective-permute-start.9
  143.6 2.7 %collective-permute-start.10 = (bf16[1024,128]{1,0:T(8,128)(2,1)}, bf16[1024,128]{1,0:T(8,128)(2,1)}, u32[]{:S(2)}, u32[]{:S(2)}) collective-permute-start(bf16[1024,128]{1,0:T(8,128)(2,1)} %get-tuple-element.38), channel_id=1, source_target_pairs={{0,96},{32,0},{64,32},{96,64},{1,97},{33,1},{65,33},{97,65},{2,98}... | collective-permute-start | bytes 786440 | tf_op jit(solution)/shard_map/slope_exchange/ppermute | solution.py:288
  151.6 1.4 fusion.3
  153.1 14.5 %all-to-all-start.2 = ((bf16[32,48,128]{2,1,0:T(8,128)(2,1)}), bf16[32,48,128]{2,1,0:T(8,128)(2,1)S(1)}, u32[]{:S(2)}, u32[]{:S(2)}) async-start(bf16[32,48,128]{2,1,0:T(8,128)(2,1)} %bitcast.20), calls=%async_computation.2 | async-start | bytes 786432 | tf_op jit(solution)/shard_map/gradients/all_to_all | solution.py:375
  168.0 3.0 %collective-permute-start.13 = (bf16[1024,128]{1,0:T(8,128)(2,1)}, bf16[1024,128]{1,0:T(8,128)(2,1)S(1)}, u32[]{:S(2)}, u32[]{:S(2)}) collective-permute-start(bf16[1024,128]{1,0:T(8,128)(2,1)} %collective-permute-done.10), channel_id=1, source_target_pairs={{0,96},{32,0},{64,32},{96,64},{1,97},{33,1},{65,33},{97,65},{2,98}... | collective-permute-start | bytes 786440 | tf_op jit(solution)/shard_map/slope_exchange/ppermute | solution.py:288
  171.0 1.8 convolution_convert_fusion.2
  172.8 1.8 convolution_convert_fusion
  174.6 3.0 %collective-permute-done.12 = bf16[1024,128]{1,0:T(8,128)(2,1)S(1)} collective-permute-done((bf16[1024,128]{1,0:T(8,128)(2,1)}, bf16[1024,128]{1,0:T(8,128)(2,1)S(1)}, u32[]{:S(2)}, u32[]{:S(2)}) %collective-permute-start.12) | collective-permute-done | bytes 262176 | tf_op jit(solution)/shard_map/slope_exchange/ppermute | solution.py:288
  179.2 7.8 %all-to-all-start.3 = ((bf16[32,48,128]{2,1,0:T(8,128)(2,1)}), bf16[32,48,128]{2,1,0:T(8,128)(2,1)S(1)}, u32[]{:S(2)}, u32[]{:S(2)}) async-start(bf16[32,48,128]{2,1,0:T(8,128)(2,1)} %bitcast.21), calls=%async_computation.3 | async-start | bytes 786432 | tf_op jit(solution)/shard_map/gradients/all_to_all | solution.py:375
  188.0 3.1 %collective-permute-start.7 = (bf16[512,128]{1,0:T(8,128)(2,1)S(1)}, bf16[512,128]{1,0:T(8,128)(2,1)S(1)}, u32[]{:S(2)}, u32[]{:S(2)}) collective-permute-start(bf16[512,128]{1,0:T(8,128)(2,1)S(1)} %get-tuple-element.33), channel_id=1, source_target_pairs={{0,64},{32,96},{64,0},{96,32},{1,65},{33,97},{65,1},{97,33},{2,66}... | collective-permute-start | bytes 393224 | tf_op jit(solution)/shard_map/second_layer/ppermute | solution.py:288
  191.9 1.5 collective-permute-done.6
  193.4 3.9 %collective-permute-done.7 = bf16[512,128]{1,0:T(8,128)(2,1)S(1)} collective-permute-done((bf16[512,128]{1,0:T(8,128)(2,1)S(1)}, bf16[512,128]{1,0:T(8,128)(2,1)S(1)}, u32[]{:S(2)}, u32[]{:S(2)}) %collective-permute-start.7) | collective-permute-done | bytes 131104 | tf_op jit(solution)/shard_map/second_layer/ppermute | solution.py:288
  198.2 26.0 %all-gather = bf16[3072,128]{1,0:T(8,128)(2,1)S(1)} all-gather(bf16[96,128]{1,0:T(8,128)(2,1)S(1)} %pad_maximum_fusion.3), channel_id=2, replica_groups=mesh['blk'=4,'wide'=32] {'wide'}, dimensions={0}, use_global_device_ids=true | all-gather | bytes 811008 | tf_op jit(solution)/shard_map/gradients/all_gather | solution.py:392
  (84 shorter events, 20.2 us)
Async XLA Ops:
  0.6 127.2 %copy-start = (bf16[512,512]{1,0:T(8,128)(2,1)S(1)}, bf16[512,512]{1,0:T(8,128)(2,1)}, u32[]{:S(2)}) copy-start(bf16[512,512]{1,0:T(8,128)(2,1)} %param.21) | copy-start | bytes 1572868
  0.6 0.8 copy-start.3
  3.6 15.7 %copy-start.5 = (s32[32,128]{1,0:T(8,128)}, s32[32,128]{1,0:T(8,128)S(1)}, u32[]{:S(2)}) copy-start(s32[32,128]{1,0:T(8,128)S(1)} %get-tuple-element.13) | copy-start | bytes 49156
  19.3 2.2 copy-start.2
  33.3 2.0 copy-start.1
  35.3 5.0 %copy-start.10 = (s32[2048,15]{0,1:T(8,128)S(1)}, s32[2048,15]{0,1:T(8,128)}, u32[]{:S(2)}) copy-start(s32[2048,15]{0,1:T(8,128)} %param.14) | copy-start | bytes 368644
  35.3 55.4 %all-to-all-start.1 = ((bf16[32,256,256]{2,1,0:T(8,128)(2,1)}), bf16[32,256,256]{2,1,0:T(8,128)(2,1)}, u32[]{:S(2)}, u32[]{:S(2)}) async-start(bf16[32,256,256]{2,1,0:T(8,128)(2,1)} %bitcast.66), calls=%async_computation.1 | async-start | bytes 8388608 | tf_op jit(solution)/shard_map/rows/all_to_all | solution.py:300
  114.4 3.7 %copy-start.11 = (s32[512,10]{0,1:T(8,128)S(1)}, s32[512,10]{0,1:T(8,128)}, u32[]{:S(2)}) copy-start(s32[512,10]{0,1:T(8,128)} %param.15) | copy-start | bytes 61444
  116.5 11.4 %copy-start.9 = (bf16[128,512]{1,0:T(8,128)(2,1)S(1)}, bf16[128,512]{1,0:T(8,128)(2,1)}, u32[]{:S(2)}) copy-start(bf16[128,512]{1,0:T(8,128)(2,1)} %param.20) | copy-start | bytes 393220
  116.5 7.5 %collective-permute-start.1 = (bf16[1024,128]{1,0:T(8,128)(2,1)S(1)}, bf16[1024,128]{1,0:T(8,128)(2,1)S(1)}, u32[]{:S(2)}, u32[]{:S(2)}) collective-permute-start(bf16[1024,128]{1,0:T(8,128)(2,1)S(1)} %get-tuple-element.30), channel_id=1, source_target_pairs={{0,32},{32,64},{64,96},{96,0},{1,33},{33,65},{65,97},{97,1},{2,34}... | collective-permute-start | bytes 786440 | tf_op jit(solution)/shard_map/pre_act_exchange/ppermute | solution.py:288
  118.4 10.8 %collective-permute-start = (bf16[1024,128]{1,0:T(8,128)(2,1)}, bf16[1024,128]{1,0:T(8,128)(2,1)S(1)}, u32[]{:S(2)}, u32[]{:S(2)}) collective-permute-start(bf16[1024,128]{1,0:T(8,128)(2,1)} %get-tuple-element.27), channel_id=1, source_target_pairs={{0,96},{32,0},{64,32},{96,64},{1,97},{33,1},{65,33},{97,65},{2,98}... | collective-permute-start | bytes 786440 | tf_op jit(solution)/shard_map/pre_act_exchange/ppermute | solution.py:288
  120.6 8.6 %collective-permute-start.4 = (bf16[1024,128]{1,0:T(8,128)(2,1)}, bf16[1024,128]{1,0:T(8,128)(2,1)S(1)}, u32[]{:S(2)}, u32[]{:S(2)}) collective-permute-start(bf16[1024,128]{1,0:T(8,128)(2,1)} %get-tuple-element.28), channel_id=1, source_target_pairs={{0,96},{32,0},{64,32},{96,64},{1,97},{33,1},{65,33},{97,65},{2,98}... | collective-permute-start | bytes 786440 | tf_op jit(solution)/shard_map/pre_act_exchange/ppermute | solution.py:288
  125.0 6.5 %collective-permute-start.2 = (bf16[1024,128]{1,0:T(8,128)(2,1)S(1)}, bf16[1024,128]{1,0:T(8,128)(2,1)S(1)}, u32[]{:S(2)}, u32[]{:S(2)}) collective-permute-start(bf16[1024,128]{1,0:T(8,128)(2,1)S(1)} %fusion.19), channel_id=1, source_target_pairs={{0,32},{32,64},{64,96},{96,0},{1,33},{33,65},{65,97},{97,1},{2,34}... | collective-permute-start | bytes 786440 | tf_op jit(solution)/shard_map/pre_act_exchange/ppermute | solution.py:288
  128.2 8.6 %collective-permute-start.3 = (bf16[1024,128]{1,0:T(8,128)(2,1)}, bf16[1024,128]{1,0:T(8,128)(2,1)}, u32[]{:S(2)}, u32[]{:S(2)}) collective-permute-start(bf16[1024,128]{1,0:T(8,128)(2,1)} %get-tuple-element.29), channel_id=1, source_target_pairs={{0,32},{32,64},{64,96},{96,0},{1,33},{33,65},{65,97},{97,1},{2,34}... | collective-permute-start | bytes 786440 | tf_op jit(solution)/shard_map/pre_act_exchange/ppermute | solution.py:288
  133.4 5.8 %collective-permute-start.5 = (bf16[1024,128]{1,0:T(8,128)(2,1)}, bf16[1024,128]{1,0:T(8,128)(2,1)}, u32[]{:S(2)}, u32[]{:S(2)}) collective-permute-start(bf16[1024,128]{1,0:T(8,128)(2,1)} %get-tuple-element.26), channel_id=1, source_target_pairs={{0,96},{32,0},{64,32},{96,64},{1,97},{33,1},{65,33},{97,65},{2,98}... | collective-permute-start | bytes 786440 | tf_op jit(solution)/shard_map/pre_act_exchange/ppermute | solution.py:288
  134.4 2.1 copy-start.14
  134.4 2.1 copy-start.8
  136.5 3.9 %copy-start.6 = (f32[8,256,256]{2,1,0:T(8,128)S(1)}, f32[8,256,256]{2,1,0:T(8,128)}, u32[]{:S(2)}) copy-start(f32[8,256,256]{2,1,0:T(8,128)} %fusion.24) | copy-start | bytes 6291460
  141.7 29.3 %collective-permute-start.9 = (bf16[1024,128]{1,0:T(8,128)(2,1)}, bf16[1024,128]{1,0:T(8,128)(2,1)}, u32[]{:S(2)}, u32[]{:S(2)}) collective-permute-start(bf16[1024,128]{1,0:T(8,128)(2,1)} %get-tuple-element.37), channel_id=1, source_target_pairs={{0,96},{32,0},{64,32},{96,64},{1,97},{33,1},{65,33},{97,65},{2,98}... | collective-permute-start | bytes 786440 | tf_op jit(solution)/shard_map/slope_exchange/ppermute | solution.py:288
  143.6 24.3 %collective-permute-start.11 = (bf16[1024,128]{1,0:T(8,128)(2,1)}, bf16[1024,128]{1,0:T(8,128)(2,1)}, u32[]{:S(2)}, u32[]{:S(2)}) collective-permute-start(bf16[1024,128]{1,0:T(8,128)(2,1)} %get-tuple-element.37), channel_id=1, source_target_pairs={{0,32},{32,64},{64,96},{96,0},{1,33},{33,65},{65,97},{97,1},{2,34}... | collective-permute-start | bytes 786440 | tf_op jit(solution)/shard_map/slope_exchange/ppermute | solution.py:288
  143.6 24.4 %collective-permute-start.10 = (bf16[1024,128]{1,0:T(8,128)(2,1)}, bf16[1024,128]{1,0:T(8,128)(2,1)}, u32[]{:S(2)}, u32[]{:S(2)}) collective-permute-start(bf16[1024,128]{1,0:T(8,128)(2,1)} %get-tuple-element.38), channel_id=1, source_target_pairs={{0,96},{32,0},{64,32},{96,64},{1,97},{33,1},{65,33},{97,65},{2,98}... | collective-permute-start | bytes 786440 | tf_op jit(solution)/shard_map/slope_exchange/ppermute | solution.py:288
  146.3 26.5 %collective-permute-start.14 = (bf16[1024,128]{1,0:T(8,128)(2,1)}, bf16[1024,128]{1,0:T(8,128)(2,1)}, u32[]{:S(2)}, u32[]{:S(2)}) collective-permute-start(bf16[1024,128]{1,0:T(8,128)(2,1)} %get-tuple-element.38), channel_id=1, source_target_pairs={{0,32},{32,64},{64,96},{96,0},{1,33},{33,65},{65,97},{97,1},{2,34}... | collective-permute-start | bytes 786440 | tf_op jit(solution)/shard_map/slope_exchange/ppermute | solution.py:288
  148.8 2.8 %copy-start.12 = (bf16[2048,512]{1,0:T(8,128)(2,1)S(1)}, bf16[2048,512]{1,0:T(8,128)(2,1)}, u32[]{:S(2)}) copy-start(bf16[2048,512]{1,0:T(8,128)(2,1)} %get-tuple-element.16) | copy-start | bytes 6291460
  150.3 17.2 %copy-start.7 = (f32[512,512]{1,0:T(8,128)S(1)}, f32[512,512]{1,0:T(8,128)}, u32[]{:S(2)}) copy-start(f32[512,512]{1,0:T(8,128)} %fusion.41) | copy-start | bytes 3145732
  153.1 26.1 %all-to-all-start.2 = ((bf16[32,48,128]{2,1,0:T(8,128)(2,1)}), bf16[32,48,128]{2,1,0:T(8,128)(2,1)S(1)}, u32[]{:S(2)}, u32[]{:S(2)}) async-start(bf16[32,48,128]{2,1,0:T(8,128)(2,1)} %bitcast.20), calls=%async_computation.2 | async-start | bytes 786432 | tf_op jit(solution)/shard_map/gradients/all_to_all | solution.py:375
  167.6 3.4 %copy-start.13 = (bf16[2048,512]{1,0:T(8,128)(2,1)S(1)}, bf16[2048,512]{1,0:T(8,128)(2,1)}, u32[]{:S(2)}) copy-start(bf16[2048,512]{1,0:T(8,128)(2,1)} %get-tuple-element.16) | copy-start | bytes 6291460
  167.9 9.8 %collective-permute-start.12 = (bf16[1024,128]{1,0:T(8,128)(2,1)}, bf16[1024,128]{1,0:T(8,128)(2,1)S(1)}, u32[]{:S(2)}, u32[]{:S(2)}) collective-permute-start(bf16[1024,128]{1,0:T(8,128)(2,1)} %collective-permute-done.11), channel_id=1, source_target_pairs={{0,32},{32,64},{64,96},{96,0},{1,33},{33,65},{65,97},{97,1},{2,34}... | collective-permute-start | bytes 786440 | tf_op jit(solution)/shard_map/slope_exchange/ppermute | solution.py:288
  168.0 9.7 %collective-permute-start.13 = (bf16[1024,128]{1,0:T(8,128)(2,1)}, bf16[1024,128]{1,0:T(8,128)(2,1)S(1)}, u32[]{:S(2)}, u32[]{:S(2)}) collective-permute-start(bf16[1024,128]{1,0:T(8,128)(2,1)} %collective-permute-done.10), channel_id=1, source_target_pairs={{0,96},{32,0},{64,32},{96,64},{1,97},{33,1},{65,33},{97,65},{2,98}... | collective-permute-start | bytes 786440 | tf_op jit(solution)/shard_map/slope_exchange/ppermute | solution.py:288
  179.2 18.9 %all-to-all-start.3 = ((bf16[32,48,128]{2,1,0:T(8,128)(2,1)}), bf16[32,48,128]{2,1,0:T(8,128)(2,1)S(1)}, u32[]{:S(2)}, u32[]{:S(2)}) async-start(bf16[32,48,128]{2,1,0:T(8,128)(2,1)} %bitcast.21), calls=%async_computation.3 | async-start | bytes 786432 | tf_op jit(solution)/shard_map/gradients/all_to_all | solution.py:375
  187.1 6.3 %collective-permute-start.6 = (bf16[512,128]{1,0:T(8,128)(2,1)S(1)}, bf16[512,128]{1,0:T(8,128)(2,1)S(1)}, u32[]{:S(2)}, u32[]{:S(2)}) collective-permute-start(bf16[512,128]{1,0:T(8,128)(2,1)S(1)} %get-tuple-element.31), channel_id=1, source_target_pairs={{0,32},{32,64},{64,96},{96,0},{1,33},{33,65},{65,97},{97,1},{2,34}... | collective-permute-start | bytes 393224 | tf_op jit(solution)/shard_map/second_layer/ppermute | solution.py:288
  188.0 9.3 %collective-permute-start.7 = (bf16[512,128]{1,0:T(8,128)(2,1)S(1)}, bf16[512,128]{1,0:T(8,128)(2,1)S(1)}, u32[]{:S(2)}, u32[]{:S(2)}) collective-permute-start(bf16[512,128]{1,0:T(8,128)(2,1)S(1)} %get-tuple-element.33), channel_id=1, source_target_pairs={{0,64},{32,96},{64,0},{96,32},{1,65},{33,97},{65,1},{97,33},{2,66}... | collective-permute-start | bytes 393224 | tf_op jit(solution)/shard_map/second_layer/ppermute | solution.py:288
  191.1 6.2 %collective-permute-start.8 = (bf16[512,128]{1,0:T(8,128)(2,1)S(1)}, bf16[512,128]{1,0:T(8,128)(2,1)S(1)}, u32[]{:S(2)}, u32[]{:S(2)}) collective-permute-start(bf16[512,128]{1,0:T(8,128)(2,1)S(1)} %get-tuple-element.32), channel_id=1, source_target_pairs={{0,96},{32,0},{64,32},{96,64},{1,97},{33,1},{65,33},{97,65},{2,98}... | collective-permute-start | bytes 393224 | tf_op jit(solution)/shard_map/second_layer/ppermute | solution.py:288
  (1 other events, 0.7 us)

commit v2 on v1

v2 whole, which is shorter than its diff:
```python
import functools

import jax
import jax.numpy as jnp
from jax import lax
from jax.experimental import pallas as pl
from jax.experimental.pallas import tpu as pltpu
from jax.sharding import PartitionSpec as P

BF = jnp.bfloat16
F32 = jnp.float32
NT = (((1,), (1,)), ((), ()))
TN = (((0,), (0,)), ((), ()))


def iota(shape, axis):
    return lax.broadcasted_iota(jnp.int32, shape, axis)


def one_hot(hit):
    return jnp.where(hit, 1.0, 0.0).astype(BF)


def chunk(index, size):
    return pl.ds(pl.multiple_of(index * size, size), size)


def request_kernel(own_hbm, row_hbm, req_ref, flat_ref, own_ref, row_ref, hot, picked, spots, sems):
    peers, _, cap = req_ref.shape
    lines, width = own_ref.shape
    copies = [
        pltpu.make_async_copy(own_hbm, own_ref, sems.at[0]),
        pltpu.make_async_copy(row_hbm, row_ref, sems.at[1]),
    ]
    for copy in copies:
        copy.start()
    for copy in copies:
        copy.wait()
    names = iota((peers, width), 0)
    for r in range(lines):
        hot[r * peers:(r + 1) * peers, :] = one_hot(own_ref[r:r + 1, :] == names)
    before = one_hot(iota((width, 2 * width), 0) <= iota((width, 2 * width), 1))
    counted = jnp.dot(hot[...], before, preferred_element_type=F32)
    base = jnp.full((peers, width), -1.0, F32)
    slots = iota((cap, width), 0)
    for r in range(lines):
        here = counted[r * peers:(r + 1) * peers]
        hit = own_ref[r:r + 1, :] == names
        slot = jnp.sum(jnp.where(hit, here[:, :width] + base, 0.0), axis=0, keepdims=True)
        slot = slot.astype(jnp.int32)
        base = base + here[:, width:]
        flat_ref[r:r + 1, :] = own_ref[r:r + 1, :] * cap + slot
        cols = slice(r * width, (r + 1) * width)
        row = row_ref[r:r + 1, :]
        upper = jnp.broadcast_to((row >> 6).astype(F32), (peers, width))
        lower = jnp.broadcast_to((row & 63).astype(F32), (peers, width))
        picked[:peers, cols] = jnp.where(hit, upper, 0.0).astype(BF)
        picked[peers:, cols] = jnp.where(hit, lower, 0.0).astype(BF)
        spots[:, cols] = one_hot(slots == slot)
    found = lax.dot_general(picked[...], spots[...], NT, preferred_element_type=F32)
    req_ref[:, 0, :] = (found[:peers] * 64.0 + found[peers:]).astype(jnp.int32)


def request_table(owners, rows, peers, cap):
    lines, width = owners.shape
    return pl.pallas_call(
        request_kernel,
        out_shape=(
            jax.ShapeDtypeStruct((peers, 1, cap), jnp.int32),
            jax.ShapeDtypeStruct(owners.shape, jnp.int32),
        ),
        in_specs=[pl.BlockSpec(memory_space=pltpu.HBM)] * 2,
        scratch_shapes=[
            pltpu.VMEM(owners.shape, jnp.int32),
            pltpu.VMEM(owners.shape, jnp.int32),
            pltpu.VMEM((lines * peers, width), BF),
            pltpu.VMEM((2 * peers, lines * width), BF),
            pltpu.VMEM((cap, lines * width), BF),
            pltpu.SemaphoreType.DMA((2,)),
        ],
        compiler_params=pltpu.CompilerParams(vmem_limit_bytes=62 << 20),
        name="request_table",
    )(owners, rows)


def count_kernel(idx_ref, out_ref):
    groups = idx_ref.shape[0]
    uppers = out_ref.shape[1] // 256
    target = iota((1, 256), 1) >> 4
    rows_upper = iota((uppers * 16, 256), 0)
    rows_lower = iota((256, 256), 0)

    def group(g, carry):
        value = idx_ref[pl.ds(g, 1), :]
        code = jnp.where(value >= 0, (value >> 8) * 16 + target, -1)
        found = lax.dot_general(
            one_hot(rows_upper == code),
            one_hot(rows_lower == (value & 255)),
            NT,
            preferred_element_type=F32,
        ).astype(BF)
        for u in range(uppers):
            out_ref[chunk(g, 16), u * 256:(u + 1) * 256] = found[u * 16:(u + 1) * 16, :]
        return carry

    lax.fori_loop(0, groups, group, 0, unroll=4)


def neighbour_counts(lists, sources, block_groups=16):
    targets, places = lists.shape
    padded = jnp.pad(lists, ((0, 0), (0, 16 - places)), constant_values=-1)
    return pl.pallas_call(
        count_kernel,
        grid=(targets // 16 // block_groups,),
        in_specs=[pl.BlockSpec((block_groups, 256), lambda i: (i, 0))],
        out_specs=pl.BlockSpec((block_groups * 16, sources), lambda i: (i, 0)),
        out_shape=jax.ShapeDtypeStruct((targets, sources), BF),
        compiler_params=pltpu.CompilerParams(vmem_limit_bytes=40 << 20),
        cost_estimate=pl.CostEstimate(
            flops=512 * targets * sources,
            bytes_accessed=2 * targets * sources,
            transcendentals=0,
        ),
        name="neighbour_counts",
    )(padded.reshape(targets // 16, 256))


def pick_rows(idx_ref, first, count, low, high, out_ref):
    half = low.shape[1]
    line = iota((8, half), 0)

    def some(i, carry):
        begin = pl.multiple_of(i * 16, 16)
        lows, highs = [], []
        for h in range(2):
            for j in range(8):
                row = idx_ref[first + begin + h * 8 + j]
                new_low = jnp.broadcast_to(low[pl.ds(row, 1), :], (8, half))
                new_high = jnp.broadcast_to(high[pl.ds(row, 1), :], (8, half))
                if j == 0:
                    got_low, got_high = new_low, new_high
                else:
                    got_low = jnp.where(line == j, new_low, got_low)
                    got_high = jnp.where(line == j, new_high, got_high)
            lows.append(got_low)
            highs.append(got_high)
        out_ref[pl.ds(begin, 16), :half] = jnp.concatenate(lows, axis=0).astype(BF)
        out_ref[pl.ds(begin, 16), half:] = jnp.concatenate(highs, axis=0).astype(BF)
        return carry

    lax.fori_loop(0, count // 16, some, 0, unroll=4)


def piece_copies(source_ref, held, sems):
    rows = held.shape[0] // sems.shape[0]
    return [
        pltpu.make_async_copy(
            source_ref.at[pl.ds(p * rows, rows), :], held.at[pl.ds(p * rows, rows), :], sems.at[p]
        )
        for p in range(sems.shape[0])
    ]


def widen(held, low, high, copies):
    rows = held.shape[0] // len(copies)
    half = low.shape[1]
    for p, copy in enumerate(copies):
        copy.wait()

        def some(i, carry):
            part = pl.ds(pl.multiple_of(p * rows + i * 128, 128), 128)
            low[part, :] = held[part, :half].astype(F32)
            high[part, :] = held[part, half:].astype(F32)
            return carry

        lax.fori_loop(0, rows // 128, some, 0, unroll=2)


def gather_kernel(idx_ref, table_ref, out_ref, held, low, high, sems):
    step = pl.program_id(0)
    rows = out_ref.shape[0]

    @pl.when(step == 0)
    def _():
        copies = piece_copies(table_ref, held, sems)
        for copy in copies:
            copy.start()
        widen(held, low, high, copies)

    pick_rows(idx_ref, step * rows, rows, low, high, out_ref)


def gather_rows(table, idx, rows=1024):
    total = idx.shape[0]
    own_rows, width = table.shape
    return pl.pallas_call(
        gather_kernel,
        grid_spec=pltpu.PrefetchScalarGridSpec(
            num_scalar_prefetch=1,
            grid=(total // rows,),
            in_specs=[pl.BlockSpec(memory_space=pltpu.HBM)],
            out_specs=pl.BlockSpec((rows, width), lambda i, s: (i, 0)),
            scratch_shapes=[
                pltpu.VMEM((own_rows, width), BF),
                pltpu.VMEM((own_rows, width // 2), F32),
                pltpu.VMEM((own_rows, width // 2), F32),
                pltpu.SemaphoreType.DMA((8,)),
            ],
        ),
        out_shape=pltpu.HBM((total, width), BF),
        compiler_params=pltpu.CompilerParams(vmem_limit_bytes=62 << 20),
        name="gather_rows",
    )(idx, table)


def layer_kernel(list_width, idx_ref, spot_ref, arrived_ref, counts_ref, ws_ref, wn_ref,
                 *refs):
    part_refs, (both_ref, held, low, high, frontier, counts, sems, count_sems) = refs[:-8], refs[-8:]
    step = pl.program_id(0)
    block = both_ref.shape[0]
    width = held.shape[1]

    def count_copy(b):
        return pltpu.make_async_copy(
            counts_ref.at[pl.ds(b * block, block), :],
            counts.at[pl.ds(b * block, block), :],
            count_sems.at[b],
        )

    @pl.when(step == 0)
    def _():
        copies = piece_copies(arrived_ref, held, sems)
        for copy in copies:
            copy.start()
        for b in range(counts.shape[0] // block):
            count_copy(b).start()
        widen(held, low, high, copies)
        pick_rows(idx_ref, 0, frontier.shape[0], low, high, frontier)

    count_copy(step).wait()
    here = chunk(step, block)
    total = jnp.dot(counts[here, :], frontier[...], preferred_element_type=F32)
    own = frontier[here, :]
    mean = (total / list_width).astype(BF)
    both_ref[:, :width] = own
    both_ref[:, width:] = mean
    share = part_refs[0].shape[1]
    quarters = ws_ref.shape[1] // share
    made = jnp.dot(own, ws_ref[...], preferred_element_type=F32)
    made = (made + jnp.dot(mean, wn_ref[...], preferred_element_type=F32)).astype(BF)
    for q in range(quarters):
        d = lax.rem(q + quarters - spot_ref[0], quarters)
        for e in range(quarters):
            for half in range(2):
                @pl.when((d == e) & (step // (pl.num_programs(0) // 2) == half))
                def _():
                    part_refs[2 * e + half][...] = made[:, q * share:(q + 1) * share]


def first_layer(idx, spot, arrived, counts, w_self, w_near, list_width, quarters, block=1024):
    targets, positions = counts.shape
    slots, width = arrived.shape
    share = w_self.shape[1] // quarters
    steps = targets // block
    middle = steps // 2

    def full(shape):
        return pl.BlockSpec(shape, lambda i, *s: (0, 0))

    halves = [
        pl.BlockSpec((block, share), lambda i, *s: (jnp.minimum(i, middle - 1), 0)),
        pl.BlockSpec((block, share), lambda i, *s: (jnp.maximum(i - middle, 0), 0)),
    ]
    return pl.pallas_call(
        functools.partial(layer_kernel, list_width),
        grid_spec=pltpu.PrefetchScalarGridSpec(
            num_scalar_prefetch=2,
            grid=(steps,),
            in_specs=[
                pl.BlockSpec(memory_space=pltpu.HBM),
                pl.BlockSpec(memory_space=pltpu.HBM),
                full(w_self.shape),
                full(w_near.shape),
            ],
            out_specs=halves * quarters + [pl.BlockSpec((block, 2 * width), lambda i, *s: (i, 0))],
            scratch_shapes=[
                pltpu.VMEM((slots, width), BF),
                pltpu.VMEM((slots, width // 2), F32),
                pltpu.VMEM((slots, width // 2), F32),
                pltpu.VMEM((positions, width), BF),
                pltpu.VMEM((targets, positions), BF),
                pltpu.SemaphoreType.DMA((8,)),
                pltpu.SemaphoreType.DMA((steps,)),
            ],
        ),
        out_shape=[jax.ShapeDtypeStruct((targets // 2, share), BF)] * (2 * quarters)
        + [jax.ShapeDtypeStruct((targets, 2 * width), BF)],
        compiler_params=pltpu.CompilerParams(vmem_limit_bytes=62 << 20),
        name="first_layer",
    )(idx, spot, arrived, counts, w_self, w_near)


def slope_kernel(part0, up, down, far, bias_ref, d_ref, hidden_ref, slope_ref):
    active = part0[...].astype(F32) + up[...].astype(F32) + down[...].astype(F32) + far[...].astype(F32)
    active = active + bias_ref[...].astype(F32)
    below = 1.0 + jnp.exp(-active)
    sigmoid = 1.0 / below
    hidden_ref[...] = (active / below).astype(BF)
    slope_ref[...] = (d_ref[...] * (sigmoid * (1.0 + active * (1.0 - sigmoid)))).astype(BF)


def hidden_and_slope(part0, up, down, far, bias, d_hidden, first, block=512):
    rows, share = part0.shape
    place = pl.BlockSpec((block, share), lambda i: (i, 0))
    return pl.pallas_call(
        slope_kernel,
        grid=(rows // block,),
        in_specs=[place] * 4
        + [
            pl.BlockSpec((1, share), lambda i: (0, 0)),
            pl.BlockSpec((block, share), lambda i: (i + first // block, 0)),
        ],
        out_specs=[place, place],
        out_shape=[jax.ShapeDtypeStruct((rows, share), BF)] * 2,
        compiler_params=pltpu.CompilerParams(vmem_limit_bytes=16 << 20),
        name="hidden_and_slope",
    )(part0, up, down, far, bias, d_hidden)


def finish_kernel(spot_ref, mine_ref, other_ref, ws_ref, wn_ref, vs_ref, vn_ref):
    peers, shard, share = mine_ref.shape
    feats = ws_ref.shape[0]
    some = feats // peers
    order = (0, 1, 3, 2)
    v_rows = shard - some * len(order)
    front = spot_ref[1] == 0

    def halves(first, count):
        part = slice(first, first + count)
        mine = mine_ref[:, part, :].astype(F32).reshape(peers * count, share)
        other = other_ref[:, part, :].astype(F32).reshape(peers * count, share)
        return jnp.where(front, mine, other), jnp.where(front, other, mine)

    for place, d in enumerate(order):
        cols = chunk(lax.rem(spot_ref[0] + d, len(order)), share)
        ws_ref[:, cols], wn_ref[:, cols] = halves(v_rows + place * some, some)
    for half, block in enumerate(halves(0, v_rows)):
        for e in range(len(order) // 2):
            cols = slice((2 * half + e) * share, (2 * half + e + 1) * share)
            vs_ref[:, cols] = block[2 * e * share:(2 * e + 1) * share]
            vn_ref[:, cols] = block[(2 * e + 1) * share:(2 * e + 2) * share]


def body(
    feature_table,
    owner_ids,
    row_ids,
    near_first,
    near_second,
    w_self,
    w_near,
    bias_hidden,
    v_self,
    v_near,
    cotangent,
):
    peers = lax.axis_size("wide")
    quarters = lax.axis_size("blk")
    z = lax.axis_index("blk")
    core = lax.axis_index("wide") % 2
    frontier_count = row_ids.shape[0]
    cap = 2 * frontier_count // peers
    targets, first_width = near_first.shape
    seeds, second_width = near_second.shape
    feats, hidden_units = w_self.shape
    share = hidden_units // quarters

    def shift(value, by):
        return lax.ppermute(value, "blk", [(i, (i + by) % quarters) for i in range(quarters)])

    def exchange(value):
        return lax.all_to_all(value, "wide", split_axis=0, concat_axis=0, tiled=True)

    with jax.named_scope("requests"):
        requests, flat = request_table(
            owner_ids.reshape(frontier_count // 128, 128),
            row_ids.reshape(frontier_count // 128, 128),
            peers,
            cap,
        )
        wanted = exchange(requests).reshape(-1)
        flat = flat.reshape(-1)
    with jax.named_scope("rows"):
        found = gather_rows(feature_table, wanted)
        arrived = exchange(found.reshape(peers, cap, feats)).reshape(peers * cap, feats)
    with jax.named_scope("beside_rows"):
        counts_first = neighbour_counts(near_first, frontier_count)
        counts_second = neighbour_counts(near_second, targets)
        d_self = lax.dot_general(cotangent, v_self, NT, preferred_element_type=F32)
        d_mean = lax.dot_general(cotangent, v_near, NT, preferred_element_type=F32) / second_width
        d_upper = d_mean.astype(BF)
        d_lower = (d_mean - d_upper.astype(F32)).astype(BF)
        spread = lax.dot_general(
            counts_second,
            jnp.concatenate([d_upper, d_lower], axis=1),
            TN,
            preferred_element_type=F32,
        )
        d_hidden = spread[:, :share] + spread[:, share:]
        d_hidden = d_hidden + jnp.pad(d_self, ((0, targets - seeds), (0, 0)))
        arrived, counts_first, counts_second, d_hidden = lax.optimization_barrier(
            (arrived, counts_first, counts_second, d_hidden)
        )
    with jax.named_scope("first_layer"):
        *parts, both = first_layer(
            flat,
            jnp.full((1,), z, jnp.int32),
            arrived,
            counts_first,
            w_self,
            w_near,
            first_width,
            quarters,
        )
    with jax.named_scope("pre_act_exchange"):
        hiddens, slopes = [], []
        for half in range(2):
            far = shift(parts[2 * 2 + half], 2)
            up = shift(parts[2 * 1 + half], 1)
            down = shift(parts[2 * 3 + half], -1)
            hidden, slope = hidden_and_slope(
                parts[half], up, down, far, bias_hidden.reshape(1, share), d_hidden, half * targets // 2
            )
            hiddens.append(hidden)
            slopes.append(slope)
    with jax.named_scope("slope_exchange"):
        from_far = jnp.concatenate([shift(slope, 2) for slope in slopes])
        from_down = jnp.concatenate([shift(slope, 1) for slope in slopes])
        from_up = jnp.concatenate([shift(slope, -1) for slope in slopes])

    def grad_w(slope_part):
        return lax.dot_general(both, slope_part, TN, preferred_element_type=F32).astype(BF)

    def shards(values):
        rows = values.shape[0] // peers
        split = values.reshape(2, peers // 2, rows, share)
        return split.transpose(1, 0, 2, 3).reshape(peers, rows, share)

    def scatter_sum(values):
        return jnp.sum(exchange(values).astype(F32), axis=0).astype(BF)

    with jax.named_scope("second_layer"):
        hidden = jnp.concatenate(hiddens)
        seed_hidden = hidden[:seeds]
        second_mean = (
            jnp.dot(counts_second, hidden, preferred_element_type=F32) / second_width
        ).astype(BF)
        grad_v = jnp.concatenate(
            [
                lax.dot_general(seed_hidden, cotangent, TN, preferred_element_type=F32),
                lax.dot_general(second_mean, cotangent, TN, preferred_element_type=F32),
            ]
        ).astype(BF)
        grad_v = jnp.concatenate([grad_v[:, c * share:(c + 1) * share] for c in range(quarters)])
        partial_out = jnp.dot(seed_hidden, v_self, preferred_element_type=F32) + jnp.dot(
            second_mean, v_near, preferred_element_type=F32
        )

        def out_part(d):
            return lax.dynamic_slice_in_dim(partial_out, (z + d) % quarters * share, share, 1)

        outs = [shift(out_part(d).astype(BF), d) for d in range(1, quarters)]
    with jax.named_scope("gradients"):
        early = scatter_sum(
            jnp.concatenate([shards(grad_v), shards(grad_w(jnp.concatenate(slopes)))], axis=1)
        )
        near_two = grad_w(jnp.concatenate([from_up, from_down], axis=1))
        late = scatter_sum(
            jnp.concatenate(
                [shards(near_two[:, :share]), shards(near_two[:, share:]), shards(grad_w(from_far))], axis=1
            )
        )
        sums, *outs = lax.optimization_barrier((jnp.concatenate([early, late]), *outs))
        seed_out = out_part(0)
        for part in outs:
            seed_out = seed_out + part.astype(F32)
        seed_out = seed_out.astype(BF)
        chips = peers // 2
        mine = lax.all_to_all(
            jnp.broadcast_to(sums, (chips, *sums.shape)),
            "wide",
            split_axis=0,
            concat_axis=0,
            axis_index_groups=[list(range(c, peers, 2)) for c in range(2)],
            tiled=True,
        )
        other = lax.ppermute(mine, "wide", [(i, i ^ 1) for i in range(peers)])
        grads = pl.pallas_call(
            finish_kernel,
            in_specs=[pl.BlockSpec(memory_space=pltpu.SMEM)] + [pl.BlockSpec(memory_space=pltpu.VMEM)] * 2,
            out_specs=[pl.BlockSpec(memory_space=pltpu.VMEM)] * 4,
            out_shape=[jax.ShapeDtypeStruct((feats, hidden_units), F32)] * 2
            + [jax.ShapeDtypeStruct((share, hidden_units), F32)] * 2,
            compiler_params=pltpu.CompilerParams(vmem_limit_bytes=16 << 20),
            name="finish",
        )(jnp.stack([z, core]).astype(jnp.int32), mine, other)
    return (seed_out, *grads)


def solution(mesh):
    placed = (
        P("wide", "blk"),
        P("wide", None),
        P("wide"),
        P("wide", None),
        P("wide", None),
        P("blk", None),
        P("blk", None),
        P("blk"),
        P("blk", None),
        P("blk", None),
        P("wide", None),
    )
    return jax.shard_map(
        body,
        mesh=mesh,
        in_specs=placed,
        out_specs=(
            P("wide", "blk"),
            P("blk", None),
            P("blk", None),
            P("blk", None),
            P("blk", None),
        ),
        check_vma=False,
    )
```

time: 226 us -> 206 us (0.912)
  blocking collectives: 41.6 us -> 30.8 us
  local copies, waits for them, and re-layouts: 10.1 us -> 4.56 us
  other arithmetic: 9.02 us -> 3.61 us
  matrix products: 11.2 us -> 8.16 us
  Pallas kernels: 54 us -> 56.7 us
    all_gather x1 -> x0, blocking collectives: 26 us -> none  [body(): sums = lax.all_gather(jnp.concatenate([early, late]), 'wide', axis=0)]
    all_to_all x1 -> x2, blocking collectives: 15.6 us -> 30.8 us  [the longest x1 16 us: exchange(): lax.all_to_all(value, 'wide', split_axis=0, concat_axis=0, tiled=True)]
    pallas_call x1, Pallas kernels: 23.7 us -> 19.4 us  [first_layer(): pl.pallas_call(functools.partial(layer_kernel, list_width), grid_spec=plt...]
    pallas_call x1 -> x3, Pallas kernels: 1.47 us -> 5.35 us  [the longest x1 2.9 us: request_table(): pl.pallas_call(request_kernel, out_shape=(jax.ShapeDtypeStruct((peers, 1,...]
    add x3 -> x1, other arithmetic: 3.22 us -> 0.11 us  [body(): d_hidden = d_hidden + jnp.pad(d_self, ((0, targets - seeds), (0, 0)))]
    pallas_call x1, Pallas kernels: 11.8 us -> 14.5 us  [gather_rows(): pl.pallas_call(gather_kernel, grid_spec=pltpu.PrefetchScalarGridSpec(num_...]
    unnamed x32 -> x34, local copies, waits for them, and re-layouts: 6.24 us -> 3.64 us
    ppermute x0 -> x1, starting transfers between devices: none -> 2.58 us  [body(): other = lax.ppermute(mine, 'wide', [(i, i ^ 1) for i in range(peers)])]
  transfers between devices with their start and end apart: 18 -> 19, of which waited for: 7 -> 9; matrix products, arithmetic and copies ran while one was open for 9% -> 6% of each run, Pallas kernels for 7% -> 9%
where the time goes in v2:
time: 206 us
  Pallas kernels  56.7 us (28%)
  waiting for transfers between devices  52.6 us (26%)
  starting transfers between devices  48 us (23%)
  blocking collectives  30.8 us (15%)
  matrix products  8.16 us (4%)
  local copies, waits for them, and re-layouts  4.56 us (2%)
  other arithmetic  3.61 us (2%)
    all_to_all x3, waiting for transfers between devices, exchange(): lax.all_to_all(value, 'wide', split_axis=0, concat_axis=0, tiled=True)  35.8 us
    all_to_all x3, starting transfers between devices, exchange(): lax.all_to_all(value, 'wide', split_axis=0, concat_axis=0, tiled=True)  26.6 us
    pallas_call x1, Pallas kernels, first_layer(): pl.pallas_call(functools.partial(layer_kernel, list_width), grid_spec=plt...  19.4 us
    ppermute x15, starting transfers between devices, shift(): lax.ppermute(value, 'blk', [(i, (i + by) % quarters) for i in range(quart...  18.9 us
    ppermute x15, waiting for transfers between devices, shift(): lax.ppermute(value, 'blk', [(i, (i + by) % quarters) for i in range(quart...  16.8 us
    all_to_all x1, blocking collectives, exchange(): lax.all_to_all(value, 'wide', split_axis=0, concat_axis=0, tiled=True)  16 us
    pallas_call x2, Pallas kernels, neighbour_counts(): pl.pallas_call(count_kernel, grid=(targets // 16 // block_groups,), in_sp...  15.7 us
    all_to_all x1, blocking collectives, body(): lax.all_to_all(jnp.broadcast_to(sums, (chips, *sums.shape)), 'wide', spli...  14.8 us
  transfers between devices with their start and end apart: 19, of which 9 were waited for; matrix products, arithmetic and copies ran while one was open for 6% of the time, Pallas kernels for 9%

profile of v2, /device:TPU:1, one launch (start us, length us, event | category | flops | bytes accessed | tf_op | source)
XLA Modules:
  0.0 205.6 jit_solution(15650279237332420074)
XLA Ops:
  0.6 2.9 %request_table.1 = (s32[32,1,256]{2,1,0:T(1,128)}, s32[32,128]{1,0:T(8,128)}) custom-call(s32[32,128]{1,0:T(8,128)} %bitcast.58, s32[32,128]{1,0:T(8,128)} %bitcast.59), custom_call_target="tpu_custom_call" | custom-call | tf_op jit(solution)/shard_map/requests/request_table/pallas_call | solution.py:66
  3.6 16.0 %all_to_all.25 = s32[32,1,256]{2,1,0:T(1,128)} all-to-all(s32[32,1,256]{2,1,0:T(1,128)} %get-tuple-element.33), channel_id=1, replica_groups=mesh['blk'=4,'wide'=32] {'wide'}, dimensions={0} | all-to-all | bytes 65536 | tf_op jit(solution)/shard_map/requests/all_to_all | solution.py:382
  19.5 14.5 %gather_rows.1 = bf16[8192,256]{1,0:T(8,128)(2,1)} custom-call(s32[8192]{0:T(1024)} %bitcast.55, bf16[8192,256]{1,0:T(8,128)(2,1)} %table_ref.1), custom_call_target="tpu_custom_call" | custom-call | tf_op jit(solution)/shard_map/rows/gather_rows/pallas_call | solution.py:196
  34.0 5.0 %all-to-all-start.1 = ((bf16[32,256,256]{2,1,0:T(8,128)(2,1)}), bf16[32,256,256]{2,1,0:T(8,128)(2,1)}, u32[]{:S(2)}, u32[]{:S(2)}) async-start(bf16[32,256,256]{2,1,0:T(8,128)(2,1)} %bitcast.46), calls=%async_computation.1 | async-start | bytes 8388608 | tf_op jit(solution)/shard_map/rows/all_to_all | solution.py:382
  40.3 2.6 %neighbour_counts.3 = bf16[512,2048]{1,0:T(8,128)(2,1)S(1)} custom-call(s32[32,256]{1,0:T(8,128)S(1)} %reshape.75.idx_ref), custom_call_target="tpu_custom_call" | custom-call | flops 536870912 | bytes 2097152 | tf_op jit(solution)/shard_map/beside_rows/neighbour_counts/pallas_call | solution.py:112
  45.1 13.1 %neighbour_counts.2.counts_ref = bf16[2048,4096]{1,0:T(8,128)(2,1)} custom-call(s32[128,256]{1,0:T(8,128)S(1)} %reshape.74.idx_ref), custom_call_target="tpu_custom_call" | custom-call | flops 4294967296 | bytes 16777216 | tf_op jit(solution)/shard_map/beside_rows/neighbour_counts/pallas_call | solution.py:112
  58.3 31.1 %all-to-all-done.1 = bf16[32,256,256]{2,1,0:T(8,128)(2,1)} async-done(((bf16[32,256,256]{2,1,0:T(8,128)(2,1)}), bf16[32,256,256]{2,1,0:T(8,128)(2,1)}, u32[]{:S(2)}, u32[]{:S(2)}) %all-to-all-start.1) | async-done | bytes 4194336 | tf_op jit(solution)/shard_map/rows/all_to_all | solution.py:382
  89.4 19.4 %first_layer.1 = (bf16[1024,128]{1,0:T(8,128)(2,1)}, bf16[1024,128]{1,0:T(8,128)(2,1)}, bf16[1024,128]{1,0:T(8,128)(2,1)}, bf16[1024,128]{1,0:T(8,128)(2,1)}, bf...) custom-call(s32[4096]{0:T(1024)} %bitcast.60, ...), custom_call_target="tpu_custom_call" | custom-call | tf_op jit(solution)/shard_map/first_layer/first_layer/pallas_call | solution.py:274
  108.8 1.7 collective-permute-start
  110.5 2.2 %collective-permute-start.1 = (bf16[1024,128]{1,0:T(8,128)(2,1)}, bf16[1024,128]{1,0:T(8,128)(2,1)S(1)}, u32[]{:S(2)}, u32[]{:S(2)}) collective-permute-start(bf16[1024,128]{1,0:T(8,128)(2,1)} %get-tuple-element.38), channel_id=1, source_target_pairs={{0,96},{32,0},{64,32},{96,64},{1,97},{33,1},{65,33},{97,65},{2,98}... | collective-permute-start | bytes 786440 | tf_op jit(solution)/shard_map/pre_act_exchange/ppermute | solution.py:379
  112.7 1.2 collective-permute-start.2
  114.7 1.9 collective-permute-start.4
  116.6 1.3 collective-permute-start.5
  118.7 3.6 %collective-permute-done.2.far = bf16[1024,128]{1,0:T(8,128)(2,1)} collective-permute-done((bf16[1024,128]{1,0:T(8,128)(2,1)}, bf16[1024,128]{1,0:T(8,128)(2,1)}, u32[]{:S(2)}, u32[]{:S(2)}) %collective-permute-start.2) | collective-permute-done | bytes 262176 | tf_op jit(solution)/shard_map/pre_act_exchange/ppermute | solution.py:379
  123.3 2.1 %hidden_and_slope.2 = (bf16[1024,128]{1,0:T(8,128)(2,1)S(1)}, bf16[1024,128]{1,0:T(8,128)(2,1)}) custom-call(bf16[1024,128]{1,0:T(8,128)(2,1)S(1)} %copy-done.4, bf16[1024,128]{1,0:T(8,128)(2,1)S(1)} %collective-permute-done.up, bf16[1024,128]{1,0:T(8,128)(2,1)S(1)} %collective-permute-done.1.down, bf16[1024,128]{1,0:T(8,128)(2,1)} %collective-permute-done.2.far, ...), custom_call_target="tpu_custom_call" | custom-call | tf_op jit(solution)/shard_map/pre_act_exchange/hidden_and_slope/pallas_call | solution.py:315
  126.9 1.3 collective-permute-done.3.up
  128.2 1.7 collective-permute-done.4.down
  129.9 3.6 %collective-permute-done.5.far = bf16[1024,128]{1,0:T(8,128)(2,1)S(1)} collective-permute-done((bf16[1024,128]{1,0:T(8,128)(2,1)}, bf16[1024,128]{1,0:T(8,128)(2,1)S(1)}, u32[]{:S(2)}, u32[]{:S(2)}) %collective-permute-start.5) | collective-permute-done | bytes 262176 | tf_op jit(solution)/shard_map/pre_act_exchange/ppermute | solution.py:379
  138.3 1.7 convolution_convert_fusion.2
  140.8 13.3 %all-to-all-start.2 = ((bf16[32,48,128]{2,1,0:T(8,128)(2,1)}), bf16[32,48,128]{2,1,0:T(8,128)(2,1)S(1)}, u32[]{:S(2)}, u32[]{:S(2)}) async-start(bf16[32,48,128]{2,1,0:T(8,128)(2,1)} %pad_maximum_fusion), calls=%async_computation.2 | async-start | bytes 786432 | tf_op jit(solution)/shard_map/gradients/all_to_all | solution.py:382
  154.4 1.8 collective-permute-start.11
  156.3 2.4 %convolution_convert_fusion = bf16[512,256]{1,0:T(8,128)(2,1)S(1)} fusion(bf16[2048,512]{1,0:T(8,128)(2,1)} %get-tuple-element.48, bf16[1024,128]{1,0:T(8,128)(2,1)S(1)} %collective-permute-done.9, bf16[1024,128]{1,0:T(8,128)(2,1)} %collective-permute-done.8, bf16[1024,128]{1,0:T(8,128)(2,1)S(1)} %collective-permute-done.7, ...), kind=kOutput, calls=%fused_computation.1 | convolution fusion | flops 541196288 | bytes 3407872 | tf_op jit(solution)/shard_map/gradients/dot_general | solution.py:442
  158.8 4.7 %collective-permute-done.11 = bf16[1024,128]{1,0:T(8,128)(2,1)S(1)} collective-permute-done((bf16[1024,128]{1,0:T(8,128)(2,1)S(1)}, bf16[1024,128]{1,0:T(8,128)(2,1)S(1)}, u32[]{:S(2)}, u32[]{:S(2)}) %collective-permute-start.11) | collective-permute-done | bytes 262176 | tf_op jit(solution)/shard_map/slope_exchange/ppermute | solution.py:379
  165.1 8.3 %all-to-all-start.3 = ((bf16[32,48,128]{2,1,0:T(8,128)(2,1)}), bf16[32,48,128]{2,1,0:T(8,128)(2,1)S(1)}, u32[]{:S(2)}, u32[]{:S(2)}) async-start(bf16[32,48,128]{2,1,0:T(8,128)(2,1)} %pad_maximum_fusion.1), calls=%async_computation.3 | async-start | bytes 786432 | tf_op jit(solution)/shard_map/gradients/all_to_all | solution.py:382
  173.7 1.0 copy-done.8
  174.8 1.5 collective-permute-start.12
  176.3 2.1 %collective-permute-start.13 = (bf16[512,128]{1,0:T(8,128)(2,1)S(1)}, bf16[512,128]{1,0:T(8,128)(2,1)S(1)}, u32[]{:S(2)}, u32[]{:S(2)}) collective-permute-start(bf16[512,128]{1,0:T(8,128)(2,1)S(1)} %get-tuple-element.62), channel_id=1, source_target_pairs={{0,64},{32,96},{64,0},{96,32},{1,65},{33,97},{65,1},{97,33},{2,66}... | collective-permute-start | bytes 393224 | tf_op jit(solution)/shard_map/second_layer/ppermute | solution.py:379
  178.9 4.7 %all-to-all-done.3 = bf16[32,48,128]{2,1,0:T(8,128)(2,1)S(1)} async-done(((bf16[32,48,128]{2,1,0:T(8,128)(2,1)}), bf16[32,48,128]{2,1,0:T(8,128)(2,1)S(1)}, u32[]{:S(2)}, u32[]{:S(2)}) %all-to-all-start.3) | async-done | bytes 393248 | tf_op jit(solution)/shard_map/gradients/all_to_all | solution.py:382
  184.7 14.8 %all_to_all.26.mine_ref = bf16[16,96,128]{2,1,0:T(8,128)(2,1)S(1)} all-to-all(bf16[16,96,128]{2,1,0:T(8,128)(2,1)S(1)} %broadcast_in_dim.7), channel_id=1, replica_groups={{0,2,4,6,8,10,12,14,16,18,20,22,24,26,28,30},{1,3,5,7,9,11,13,15,17,19,..., dimensions={0} | all-to-all | bytes 786432 | tf_op jit(solution)/shard_map/gradients/all_to_all | solution.py:489
  199.5 2.6 %collective-permute-start.15 = (bf16[16,96,128]{2,1,0:T(8,128)(2,1)S(1)}, bf16[16,96,128]{2,1,0:T(8,128)(2,1)S(1)}, u32[]{:S(2)}, u32[]{:S(2)}) collective-permute-start(bf16[16,96,128]{2,1,0:T(8,128)(2,1)S(1)} %all_to_all.26.mine_ref), channel_id=1, source_target_pairs={{0,1},{1,0},{2,3},{3,2},{4,5},{5,4},{6,7},{7,6},{8,9},{9,8},{10,11... | collective-permute-start | bytes 1179656 | tf_op jit(solution)/shard_map/gradients/ppermute | solution.py:497
  202.1 1.7 add_convert_fusion
  203.8 1.8 finish.1
  (83 shorter events, 16.7 us)
Async XLA Ops:
  0.6 42.3 %copy-start = (bf16[512,512]{1,0:T(8,128)(2,1)S(1)}, bf16[512,512]{1,0:T(8,128)(2,1)}, u32[]{:S(2)}) copy-start(bf16[512,512]{1,0:T(8,128)(2,1)} %param.21) | copy-start | bytes 1572868
  34.0 5.0 %copy-start.13 = (s32[512,10]{0,1:T(8,128)S(1)}, s32[512,10]{0,1:T(8,128)}, u32[]{:S(2)}) copy-start(s32[512,10]{0,1:T(8,128)} %param.15) | copy-start | bytes 61444
  34.0 5.3 %copy-start.12 = (s32[2048,15]{0,1:T(8,128)S(1)}, s32[2048,15]{0,1:T(8,128)}, u32[]{:S(2)}) copy-start(s32[2048,15]{0,1:T(8,128)} %param.14) | copy-start | bytes 368644
  34.0 55.4 %all-to-all-start.1 = ((bf16[32,256,256]{2,1,0:T(8,128)(2,1)}), bf16[32,256,256]{2,1,0:T(8,128)(2,1)}, u32[]{:S(2)}, u32[]{:S(2)}) async-start(bf16[32,256,256]{2,1,0:T(8,128)(2,1)} %bitcast.46), calls=%async_computation.1 | async-start | bytes 8388608 | tf_op jit(solution)/shard_map/rows/all_to_all | solution.py:382
  39.8 3.1 %copy-start.9 = (bf16[128,512]{1,0:T(8,128)(2,1)S(1)}, bf16[128,512]{1,0:T(8,128)(2,1)}, u32[]{:S(2)}) copy-start(bf16[128,512]{1,0:T(8,128)(2,1)} %param.20) | copy-start | bytes 393220
  39.8 3.4 %copy-start.10 = (bf16[128,512]{1,0:T(8,128)(2,1)S(1)}, bf16[128,512]{1,0:T(8,128)(2,1)}, u32[]{:S(2)}) copy-start(bf16[128,512]{1,0:T(8,128)(2,1)} %param.19) | copy-start | bytes 393220
  89.4 33.0 %copy-start.7 = (bf16[128]{0:T(256)(128)(2,1)S(1)}, bf16[128]{0:T(256)(128)(2,1)}, u32[]{:S(2)}) copy-start(bf16[128]{0:T(256)(128)(2,1)} %param.18) | copy-start | bytes 772
  108.8 24.7 %copy-start.3 = (bf16[1024,128]{1,0:T(8,128)(2,1)S(1)}, bf16[1024,128]{1,0:T(8,128)(2,1)}, u32[]{:S(2)}) copy-start(bf16[1024,128]{1,0:T(8,128)(2,1)} %get-tuple-element.43.part0) | copy-start | bytes 786436
  108.8 7.8 %collective-permute-start = (bf16[1024,128]{1,0:T(8,128)(2,1)}, bf16[1024,128]{1,0:T(8,128)(2,1)S(1)}, u32[]{:S(2)}, u32[]{:S(2)}) collective-permute-start(bf16[1024,128]{1,0:T(8,128)(2,1)} %get-tuple-element.37), channel_id=1, source_target_pairs={{0,32},{32,64},{64,96},{96,0},{1,33},{33,65},{65,97},{97,1},{2,34}... | collective-permute-start | bytes 786440 | tf_op jit(solution)/shard_map/pre_act_exchange/ppermute | solution.py:379
  110.5 8.2 %collective-permute-start.1 = (bf16[1024,128]{1,0:T(8,128)(2,1)}, bf16[1024,128]{1,0:T(8,128)(2,1)S(1)}, u32[]{:S(2)}, u32[]{:S(2)}) collective-permute-start(bf16[1024,128]{1,0:T(8,128)(2,1)} %get-tuple-element.38), channel_id=1, source_target_pairs={{0,96},{32,0},{64,32},{96,64},{1,97},{33,1},{65,33},{97,65},{2,98}... | collective-permute-start | bytes 786440 | tf_op jit(solution)/shard_map/pre_act_exchange/ppermute | solution.py:379
  112.7 9.7 %collective-permute-start.2 = (bf16[1024,128]{1,0:T(8,128)(2,1)}, bf16[1024,128]{1,0:T(8,128)(2,1)}, u32[]{:S(2)}, u32[]{:S(2)}) collective-permute-start(bf16[1024,128]{1,0:T(8,128)(2,1)} %get-tuple-element.39), channel_id=1, source_target_pairs={{0,64},{32,96},{64,0},{96,32},{1,65},{33,97},{65,1},{97,33},{2,66}... | collective-permute-start | bytes 786440 | tf_op jit(solution)/shard_map/pre_act_exchange/ppermute | solution.py:379
  114.0 14.2 %collective-permute-start.3 = (bf16[1024,128]{1,0:T(8,128)(2,1)}, bf16[1024,128]{1,0:T(8,128)(2,1)S(1)}, u32[]{:S(2)}, u32[]{:S(2)}) collective-permute-start(bf16[1024,128]{1,0:T(8,128)(2,1)} %get-tuple-element.44), channel_id=1, source_target_pairs={{0,32},{32,64},{64,96},{96,0},{1,33},{33,65},{65,97},{97,1},{2,34}... | collective-permute-start | bytes 786440 | tf_op jit(solution)/shard_map/pre_act_exchange/ppermute | solution.py:379
  114.7 15.2 %collective-permute-start.4 = (bf16[1024,128]{1,0:T(8,128)(2,1)}, bf16[1024,128]{1,0:T(8,128)(2,1)S(1)}, u32[]{:S(2)}, u32[]{:S(2)}) collective-permute-start(bf16[1024,128]{1,0:T(8,128)(2,1)} %get-tuple-element.45), channel_id=1, source_target_pairs={{0,96},{32,0},{64,32},{96,64},{1,97},{33,1},{65,33},{97,65},{2,98}... | collective-permute-start | bytes 786440 | tf_op jit(solution)/shard_map/pre_act_exchange/ppermute | solution.py:379
  116.6 16.9 %collective-permute-start.5 = (bf16[1024,128]{1,0:T(8,128)(2,1)}, bf16[1024,128]{1,0:T(8,128)(2,1)S(1)}, u32[]{:S(2)}, u32[]{:S(2)}) collective-permute-start(bf16[1024,128]{1,0:T(8,128)(2,1)} %get-tuple-element.46), channel_id=1, source_target_pairs={{0,64},{32,96},{64,0},{96,32},{1,65},{33,97},{65,1},{97,33},{2,66}... | collective-permute-start | bytes 786440 | tf_op jit(solution)/shard_map/pre_act_exchange/ppermute | solution.py:379
  123.3 13.3 %copy-start.2 = (bf16[512,2048]{1,0:T(8,128)(2,1)S(1)}, bf16[512,2048]{1,0:T(8,128)(2,1)}, u32[]{:S(2)}) copy-start(bf16[512,2048]{1,0:T(8,128)(2,1)} %copy-done.1) | copy-start | bytes 6291460
  125.4 12.1 %copy-start.5 = (bf16[1024,128]{1,0:T(8,128)(2,1)}, bf16[1024,128]{1,0:T(8,128)(2,1)S(1)}, u32[]{:S(2)}) copy-start(bf16[1024,128]{1,0:T(8,128)(2,1)S(1)} %get-tuple-element.41) | copy-start | bytes 786436
  125.4 29.0 %collective-permute-start.6 = (bf16[1024,128]{1,0:T(8,128)(2,1)}, bf16[1024,128]{1,0:T(8,128)(2,1)}, u32[]{:S(2)}, u32[]{:S(2)}) collective-permute-start(bf16[1024,128]{1,0:T(8,128)(2,1)} %get-tuple-element.49), channel_id=1, source_target_pairs={{0,96},{32,0},{64,32},{96,64},{1,97},{33,1},{65,33},{97,65},{2,98}... | collective-permute-start | bytes 786440 | tf_op jit(solution)/shard_map/slope_exchange/ppermute | solution.py:379
  126.0 30.2 %collective-permute-start.8 = (bf16[1024,128]{1,0:T(8,128)(2,1)}, bf16[1024,128]{1,0:T(8,128)(2,1)}, u32[]{:S(2)}, u32[]{:S(2)}) collective-permute-start(bf16[1024,128]{1,0:T(8,128)(2,1)} %get-tuple-element.49), channel_id=1, source_target_pairs={{0,32},{32,64},{64,96},{96,0},{1,33},{33,65},{65,97},{97,1},{2,34}... | collective-permute-start | bytes 786440 | tf_op jit(solution)/shard_map/slope_exchange/ppermute | solution.py:379
  133.9 22.3 %collective-permute-start.7 = (bf16[1024,128]{1,0:T(8,128)(2,1)S(1)}, bf16[1024,128]{1,0:T(8,128)(2,1)S(1)}, u32[]{:S(2)}, u32[]{:S(2)}) collective-permute-start(bf16[1024,128]{1,0:T(8,128)(2,1)S(1)} %get-tuple-element.50), channel_id=1, source_target_pairs={{0,96},{32,0},{64,32},{96,64},{1,97},{33,1},{65,33},{97,65},{2,98}... | collective-permute-start | bytes 786440 | tf_op jit(solution)/shard_map/slope_exchange/ppermute | solution.py:379
  134.6 21.7 %collective-permute-start.9 = (bf16[1024,128]{1,0:T(8,128)(2,1)S(1)}, bf16[1024,128]{1,0:T(8,128)(2,1)S(1)}, u32[]{:S(2)}, u32[]{:S(2)}) collective-permute-start(bf16[1024,128]{1,0:T(8,128)(2,1)S(1)} %get-tuple-element.50), channel_id=1, source_target_pairs={{0,32},{32,64},{64,96},{96,0},{1,33},{33,65},{65,97},{97,1},{2,34}... | collective-permute-start | bytes 786440 | tf_op jit(solution)/shard_map/slope_exchange/ppermute | solution.py:379
  135.5 23.4 %collective-permute-start.10 = (bf16[1024,128]{1,0:T(8,128)(2,1)}, bf16[1024,128]{1,0:T(8,128)(2,1)S(1)}, u32[]{:S(2)}, u32[]{:S(2)}) collective-permute-start(bf16[1024,128]{1,0:T(8,128)(2,1)} %get-tuple-element.49), channel_id=1, source_target_pairs={{0,64},{32,96},{64,0},{96,32},{1,65},{33,97},{65,1},{97,33},{2,66}... | collective-permute-start | bytes 786440 | tf_op jit(solution)/shard_map/slope_exchange/ppermute | solution.py:379
  136.7 1.6 copy-start.14
  140.8 24.3 %all-to-all-start.2 = ((bf16[32,48,128]{2,1,0:T(8,128)(2,1)}), bf16[32,48,128]{2,1,0:T(8,128)(2,1)S(1)}, u32[]{:S(2)}, u32[]{:S(2)}) async-start(bf16[32,48,128]{2,1,0:T(8,128)(2,1)} %pad_maximum_fusion), calls=%async_computation.2 | async-start | bytes 786432 | tf_op jit(solution)/shard_map/gradients/all_to_all | solution.py:382
  154.4 9.2 %copy-start.15 = (bf16[2048,512]{1,0:T(8,128)(2,1)S(1)}, bf16[2048,512]{1,0:T(8,128)(2,1)}, u32[]{:S(2)}) copy-start(bf16[2048,512]{1,0:T(8,128)(2,1)} %get-tuple-element.48) | copy-start | bytes 6291460
  154.4 9.1 %collective-permute-start.11 = (bf16[1024,128]{1,0:T(8,128)(2,1)S(1)}, bf16[1024,128]{1,0:T(8,128)(2,1)S(1)}, u32[]{:S(2)}, u32[]{:S(2)}) collective-permute-start(bf16[1024,128]{1,0:T(8,128)(2,1)S(1)} %get-tuple-element.50), channel_id=1, source_target_pairs={{0,64},{32,96},{64,0},{96,32},{1,65},{33,97},{65,1},{97,33},{2,66}... | collective-permute-start | bytes 786440 | tf_op jit(solution)/shard_map/slope_exchange/ppermute | solution.py:379
  158.8 14.6 %copy-start.6 = (bf16[1024,128]{1,0:T(8,128)(2,1)S(1)}, bf16[1024,128]{1,0:T(8,128)(2,1)}, u32[]{:S(2)}) copy-start(bf16[1024,128]{1,0:T(8,128)(2,1)} %copy-done.5) | copy-start | bytes 786436
  158.8 14.6 %copy-start.11 = (bf16[128,512]{1,0:T(8,128)(2,1)S(1)}, bf16[128,512]{1,0:T(8,128)(2,1)}, u32[]{:S(2)}) copy-start(bf16[128,512]{1,0:T(8,128)(2,1)} %param.19) | copy-start | bytes 393220
  165.1 18.5 %all-to-all-start.3 = ((bf16[32,48,128]{2,1,0:T(8,128)(2,1)}), bf16[32,48,128]{2,1,0:T(8,128)(2,1)S(1)}, u32[]{:S(2)}, u32[]{:S(2)}) async-start(bf16[32,48,128]{2,1,0:T(8,128)(2,1)} %pad_maximum_fusion.1), calls=%async_computation.3 | async-start | bytes 786432 | tf_op jit(solution)/shard_map/gradients/all_to_all | solution.py:382
  174.8 8.9 %collective-permute-start.12 = (bf16[512,128]{1,0:T(8,128)(2,1)S(1)}, bf16[512,128]{1,0:T(8,128)(2,1)S(1)}, u32[]{:S(2)}, u32[]{:S(2)}) collective-permute-start(bf16[512,128]{1,0:T(8,128)(2,1)S(1)} %get-tuple-element.63), channel_id=1, source_target_pairs={{0,32},{32,64},{64,96},{96,0},{1,33},{33,65},{65,97},{97,1},{2,34}... | collective-permute-start | bytes 393224 | tf_op jit(solution)/shard_map/second_layer/ppermute | solution.py:379
  176.3 8.3 %collective-permute-start.13 = (bf16[512,128]{1,0:T(8,128)(2,1)S(1)}, bf16[512,128]{1,0:T(8,128)(2,1)S(1)}, u32[]{:S(2)}, u32[]{:S(2)}) collective-permute-start(bf16[512,128]{1,0:T(8,128)(2,1)S(1)} %get-tuple-element.62), channel_id=1, source_target_pairs={{0,64},{32,96},{64,0},{96,32},{1,65},{33,97},{65,1},{97,33},{2,66}... | collective-permute-start | bytes 393224 | tf_op jit(solution)/shard_map/second_layer/ppermute | solution.py:379
  178.4 6.2 %collective-permute-start.14 = (bf16[512,128]{1,0:T(8,128)(2,1)S(1)}, bf16[512,128]{1,0:T(8,128)(2,1)S(1)}, u32[]{:S(2)}, u32[]{:S(2)}) collective-permute-start(bf16[512,128]{1,0:T(8,128)(2,1)S(1)} %get-tuple-element.61), channel_id=1, source_target_pairs={{0,96},{32,0},{64,32},{96,64},{1,97},{33,1},{65,33},{97,65},{2,98}... | collective-permute-start | bytes 393224 | tf_op jit(solution)/shard_map/second_layer/ppermute | solution.py:379
  199.5 4.3 %collective-permute-start.15 = (bf16[16,96,128]{2,1,0:T(8,128)(2,1)S(1)}, bf16[16,96,128]{2,1,0:T(8,128)(2,1)S(1)}, u32[]{:S(2)}, u32[]{:S(2)}) collective-permute-start(bf16[16,96,128]{2,1,0:T(8,128)(2,1)S(1)} %all_to_all.26.mine_ref), channel_id=1, source_target_pairs={{0,1},{1,0},{2,3},{3,2},{4,5},{5,4},{6,7},{7,6},{8,9},{9,8},{10,11... | collective-permute-start | bytes 1179656 | tf_op jit(solution)/shard_map/gradients/ppermute | solution.py:497
  (3 other events, 3.3 us)

commit v3 on v2

--- a/solution.py
+++ b/solution.py
@@ -300,8 +300,8 @@
     )(idx, spot, arrived, counts, w_self, w_near)
 
 
-def slope_kernel(part0, up, down, far, bias_ref, d_ref, hidden_ref, slope_ref):
-    active = part0[...].astype(F32) + up[...].astype(F32) + down[...].astype(F32) + far[...].astype(F32)
+def slope_kernel(part0, up, down, bias_ref, d_ref, hidden_ref, slope_ref):
+    active = part0[...].astype(F32) + up[...].astype(F32) + down[...].astype(F32)
     active = active + bias_ref[...].astype(F32)
     below = 1.0 + jnp.exp(-active)
     sigmoid = 1.0 / below
@@ -309,13 +309,13 @@
     slope_ref[...] = (d_ref[...] * (sigmoid * (1.0 + active * (1.0 - sigmoid)))).astype(BF)
 
 
-def hidden_and_slope(part0, up, down, far, bias, d_hidden, first, block=512):
+def hidden_and_slope(part0, up, down, bias, d_hidden, first, block=512):
     rows, share = part0.shape
     place = pl.BlockSpec((block, share), lambda i: (i, 0))
     return pl.pallas_call(
         slope_kernel,
         grid=(rows // block,),
-        in_specs=[place] * 4
+        in_specs=[place] * 3
         + [
             pl.BlockSpec((1, share), lambda i: (0, 0)),
             pl.BlockSpec((block, share), lambda i: (i + first // block, 0)),
@@ -324,7 +324,33 @@
         out_shape=[jax.ShapeDtypeStruct((rows, share), BF)] * 2,
         compiler_params=pltpu.CompilerParams(vmem_limit_bytes=16 << 20),
         name="hidden_and_slope",
-    )(part0, up, down, far, bias, d_hidden)
+    )(part0, up, down, bias, d_hidden)
+
+
+def pack_kernel(*refs):
+    *value_refs, out_ref = refs
+    peers, _, share = out_ref.shape
+    chips = peers // 2
+    first = 0
+    for ref in value_refs:
+        rows = ref.shape[0] // peers
+        for c in range(ref.shape[1] // share):
+            for peer in range(peers):
+                shard = peer % 2 * chips + peer // 2
+                out_ref[peer, first:first + rows, :] = ref[shard * rows:(shard + 1) * rows, c * share:(c + 1) * share]
+            first += rows
+
+
+def pack_shards(values, peers, share):
+    rows = sum(v.size for v in values) // (peers * share)
+    return pl.pallas_call(
+        pack_kernel,
+        in_specs=[pl.BlockSpec(memory_space=pltpu.VMEM)] * len(values),
+        out_specs=pl.BlockSpec(memory_space=pltpu.VMEM),
+        out_shape=jax.ShapeDtypeStruct((peers, rows, share), BF),
+        compiler_params=pltpu.CompilerParams(vmem_limit_bytes=16 << 20),
+        name="pack_shards",
+    )(*values)
 
 
 def finish_kernel(spot_ref, mine_ref, other_ref, ws_ref, wn_ref, vs_ref, vn_ref):
@@ -422,29 +448,32 @@
             first_width,
             quarters,
         )
+    def added(left, right):
+        return (left.astype(F32) + right.astype(F32)).astype(BF)
+
     with jax.named_scope("pre_act_exchange"):
+        own, above, far, below = [parts[2 * d:2 * d + 2] for d in range(quarters)]
+        passing_up = shift(far[0], 1)
+        passing_down = shift(far[1], -1)
+        down_0 = shift(below[0], -1)
+        up_1 = shift(above[1], 1)
+        up_0 = shift(added(above[0], passing_up), 1)
+        down_1 = shift(added(below[1], passing_down), -1)
         hiddens, slopes = [], []
-        for half in range(2):
-            far = shift(parts[2 * 2 + half], 2)
-            up = shift(parts[2 * 1 + half], 1)
-            down = shift(parts[2 * 3 + half], -1)
+        for half, (up, down) in enumerate([(up_0, down_0), (up_1, down_1)]):
             hidden, slope = hidden_and_slope(
-                parts[half], up, down, far, bias_hidden.reshape(1, share), d_hidden, half * targets // 2
+                own[half], up, down, bias_hidden.reshape(1, share), d_hidden, half * targets // 2
             )
             hiddens.append(hidden)
             slopes.append(slope)
     with jax.named_scope("slope_exchange"):
-        from_far = jnp.concatenate([shift(slope, 2) for slope in slopes])
-        from_down = jnp.concatenate([shift(slope, 1) for slope in slopes])
-        from_up = jnp.concatenate([shift(slope, -1) for slope in slopes])
+        from_down = [shift(slope, 1) for slope in slopes]
+        from_up = [shift(slope, -1) for slope in slopes]
+        from_far = [shift(from_down[0], 1), shift(from_up[1], -1)]
+        from_down, from_up, from_far = [jnp.concatenate(v) for v in (from_down, from_up, from_far)]
 
     def grad_w(slope_part):
         return lax.dot_general(both, slope_part, TN, preferred_element_type=F32).astype(BF)
-
-    def shards(values):
-        rows = values.shape[0] // peers
-        split = values.reshape(2, peers // 2, rows, share)
-        return split.transpose(1, 0, 2, 3).reshape(peers, rows, share)
 
     def scatter_sum(values):
         return jnp.sum(exchange(values).astype(F32), axis=0).astype(BF)
@@ -471,20 +500,17 @@
 
         outs = [shift(out_part(d).astype(BF), d) for d in range(1, quarters)]
     with jax.named_scope("gradients"):
-        early = scatter_sum(
-            jnp.concatenate([shards(grad_v), shards(grad_w(jnp.concatenate(slopes)))], axis=1)
-        )
         near_two = grad_w(jnp.concatenate([from_up, from_down], axis=1))
-        late = scatter_sum(
-            jnp.concatenate(
-                [shards(near_two[:, :share]), shards(near_two[:, share:]), shards(grad_w(from_far))], axis=1
-            )
-        )
-        sums, *outs = lax.optimization_barrier((jnp.concatenate([early, late]), *outs))
+        packed = pack_shards(
+            [grad_v, grad_w(jnp.concatenate(slopes)), near_two, grad_w(from_far)], peers, share
+        )
+        sums = scatter_sum(packed)
+        sums, *outs = lax.optimization_barrier((sums, *outs))
         seed_out = out_part(0)
         for part in outs:
             seed_out = seed_out + part.astype(F32)
         seed_out = seed_out.astype(BF)
+        sums, seed_out = lax.optimization_barrier((sums, seed_out))
         chips = peers // 2
         mine = lax.all_to_all(
             jnp.broadcast_to(sums, (chips, *sums.shape)),

time: 206 us -> 195 us (0.947)
  starting transfers between devices: 48 us -> 39.2 us
  waiting for transfers between devices: 52.6 us -> 57.6 us
  blocking collectives: 30.8 us -> 28.1 us
  matrix products: 8.16 us -> 5.55 us
    all_to_all x3 -> x2, starting transfers between devices: 26.6 us -> 16.5 us  [exchange(): lax.all_to_all(value, 'wide', split_axis=0, concat_axis=0, tiled=True)]
    all_to_all x3 -> x2, waiting for transfers between devices: 35.8 us -> 39.9 us  [exchange(): lax.all_to_all(value, 'wide', split_axis=0, concat_axis=0, tiled=True)]
    convert_element_type x0 -> x2, other arithmetic: none -> 2.74 us  [added(): return (left.astype(F32) + right.astype(F32)).astype(BF)]
    dot_general x3, matrix products: 4.91 us -> 2.29 us  [grad_w(): lax.dot_general(both, slope_part, TN, preferred_element_type=F32).astype(BF)]
    all_to_all x1, blocking collectives: 14.8 us -> 12.2 us  [body(): lax.all_to_all(jnp.broadcast_to(sums, (chips, *sums.shape)), 'wide', spli...]
  transfers between devices with their start and end apart: 19 -> 18, of which waited for: 9 -> 7; matrix products, arithmetic and copies ran while one was open for 6% -> 5% of each run, Pallas kernels for 9% -> 8%
where the time goes in v3:
time: 195 us
  waiting for transfers between devices  57.6 us (30%)
  Pallas kernels  55.9 us (29%)
  starting transfers between devices  39.2 us (20%)
  blocking collectives  28.1 us (14%)
  matrix products  5.55 us (3%)
  other arithmetic  3.84 us (2%)
  local copies, waits for them, and re-layouts  3.53 us (2%)
    all_to_all x2, waiting for transfers between devices, exchange(): lax.all_to_all(value, 'wide', split_axis=0, concat_axis=0, tiled=True)  39.9 us
    ppermute x15, starting transfers between devices, shift(): lax.ppermute(value, 'blk', [(i, (i + by) % quarters) for i in range(quart...  20.3 us
    pallas_call x1, Pallas kernels, first_layer(): pl.pallas_call(functools.partial(layer_kernel, list_width), grid_spec=plt...  19.4 us
    all_to_all x2, starting transfers between devices, exchange(): lax.all_to_all(value, 'wide', split_axis=0, concat_axis=0, tiled=True)  16.5 us
    ppermute x15, waiting for transfers between devices, shift(): lax.ppermute(value, 'blk', [(i, (i + by) % quarters) for i in range(quart...  16.4 us
    all_to_all x1, blocking collectives, exchange(): lax.all_to_all(value, 'wide', split_axis=0, concat_axis=0, tiled=True)  15.9 us
    pallas_call x2, Pallas kernels, neighbour_counts(): pl.pallas_call(count_kernel, grid=(targets // 16 // block_groups,), in_sp...  15.7 us
    pallas_call x1, Pallas kernels, gather_rows(): pl.pallas_call(gather_kernel, grid_spec=pltpu.PrefetchScalarGridSpec(num_...  14.5 us
  transfers between devices with their start and end apart: 18, of which 7 were waited for; matrix products, arithmetic and copies ran while one was open for 5% of the time, Pallas kernels for 8%

profile of v3, /device:TPU:1, one launch (start us, length us, event | category | flops | bytes accessed | tf_op | source)
XLA Modules:
  0.0 194.8 jit_solution(13305322623050575544)
XLA Ops:
  0.6 2.9 %request_table.1 = (s32[32,1,256]{2,1,0:T(1,128)}, s32[32,128]{1,0:T(8,128)}) custom-call(s32[32,128]{1,0:T(8,128)} %bitcast.28, s32[32,128]{1,0:T(8,128)} %bitcast.29), custom_call_target="tpu_custom_call" | custom-call | tf_op jit(solution)/shard_map/requests/request_table/pallas_call | solution.py:66
  3.6 15.9 %all_to_all.20 = s32[32,1,256]{2,1,0:T(1,128)} all-to-all(s32[32,1,256]{2,1,0:T(1,128)} %get-tuple-element.35), channel_id=1, replica_groups=mesh['blk'=4,'wide'=32] {'wide'}, dimensions={0} | all-to-all | bytes 65536 | tf_op jit(solution)/shard_map/requests/all_to_all | solution.py:408
  19.4 14.5 %gather_rows.1 = bf16[8192,256]{1,0:T(8,128)(2,1)} custom-call(s32[8192]{0:T(1024)} %bitcast.27, bf16[8192,256]{1,0:T(8,128)(2,1)} %table_ref.1), custom_call_target="tpu_custom_call" | custom-call | tf_op jit(solution)/shard_map/rows/gather_rows/pallas_call | solution.py:196
  33.9 4.9 %all-to-all-start.1 = ((bf16[32,256,256]{2,1,0:T(8,128)(2,1)}), bf16[32,256,256]{2,1,0:T(8,128)(2,1)}, u32[]{:S(2)}, u32[]{:S(2)}) async-start(bf16[32,256,256]{2,1,0:T(8,128)(2,1)} %bitcast.26), calls=%async_computation.1 | async-start | bytes 8388608 | tf_op jit(solution)/shard_map/rows/all_to_all | solution.py:408
  40.1 2.6 %neighbour_counts.3 = bf16[512,2048]{1,0:T(8,128)(2,1)S(1)} custom-call(s32[32,256]{1,0:T(8,128)S(1)} %reshape.45.idx_ref), custom_call_target="tpu_custom_call" | custom-call | flops 536870912 | bytes 2097152 | tf_op jit(solution)/shard_map/beside_rows/neighbour_counts/pallas_call | solution.py:112
  44.9 13.1 %neighbour_counts.2.counts_ref = bf16[2048,4096]{1,0:T(8,128)(2,1)} custom-call(s32[128,256]{1,0:T(8,128)S(1)} %reshape.44.idx_ref), custom_call_target="tpu_custom_call" | custom-call | flops 4294967296 | bytes 16777216 | tf_op jit(solution)/shard_map/beside_rows/neighbour_counts/pallas_call | solution.py:112
  58.1 31.1 %all-to-all-done.1 = bf16[32,256,256]{2,1,0:T(8,128)(2,1)} async-done(((bf16[32,256,256]{2,1,0:T(8,128)(2,1)}), bf16[32,256,256]{2,1,0:T(8,128)(2,1)}, u32[]{:S(2)}, u32[]{:S(2)}) %all-to-all-start.1) | async-done | bytes 4194336 | tf_op jit(solution)/shard_map/rows/all_to_all | solution.py:408
  89.3 19.4 %first_layer.1 = (bf16[1024,128]{1,0:T(8,128)(2,1)}, bf16[1024,128]{1,0:T(8,128)(2,1)}, bf16[1024,128]{1,0:T(8,128)(2,1)}, bf16[1024,128]{1,0:T(8,128)(2,1)}, bf...) custom-call(s32[4096]{0:T(1024)} %bitcast.30, ...), custom_call_target="tpu_custom_call" | custom-call | tf_op jit(solution)/shard_map/first_layer/first_layer/pallas_call | solution.py:274
  108.7 1.7 collective-permute-start
  110.4 2.2 %collective-permute-start.4 = (bf16[1024,128]{1,0:T(8,128)(2,1)}, bf16[1024,128]{1,0:T(8,128)(2,1)S(1)}, u32[]{:S(2)}, u32[]{:S(2)}) collective-permute-start(bf16[1024,128]{1,0:T(8,128)(2,1)} %get-tuple-element.48), channel_id=1, source_target_pairs={{0,96},{32,0},{64,32},{96,64},{1,97},{33,1},{65,33},{97,65},{2,98}... | collective-permute-start | bytes 786440 | tf_op jit(solution)/shard_map/pre_act_exchange/ppermute | solution.py:405
  112.6 1.4 collective-permute-start.2
  114.0 2.4 %collective-permute-done = bf16[1024,128]{1,0:T(8,128)(2,1)S(1)} collective-permute-done((bf16[1024,128]{1,0:T(8,128)(2,1)}, bf16[1024,128]{1,0:T(8,128)(2,1)S(1)}, u32[]{:S(2)}, u32[]{:S(2)}) %collective-permute-start) | collective-permute-done | bytes 262176 | tf_op jit(solution)/shard_map/pre_act_exchange/ppermute | solution.py:405
  116.5 1.0 add_convert_fusion.1
  117.6 1.7 add_convert_fusion
  119.3 2.7 %collective-permute-start.5 = (bf16[1024,128]{1,0:T(8,128)(2,1)}, bf16[1024,128]{1,0:T(8,128)(2,1)S(1)}, u32[]{:S(2)}, u32[]{:S(2)}) collective-permute-start(bf16[1024,128]{1,0:T(8,128)(2,1)} %add_convert_fusion), channel_id=1, source_target_pairs={{0,96},{32,0},{64,32},{96,64},{1,97},{33,1},{65,33},{97,65},{2,98}... | collective-permute-start | bytes 786440 | tf_op jit(solution)/shard_map/pre_act_exchange/ppermute | solution.py:405
  122.0 7.0 %collective-permute-done.1.up = bf16[1024,128]{1,0:T(8,128)(2,1)S(1)} collective-permute-done((bf16[1024,128]{1,0:T(8,128)(2,1)S(1)}, bf16[1024,128]{1,0:T(8,128)(2,1)S(1)}, u32[]{:S(2)}, u32[]{:S(2)}) %collective-permute-start.1) | collective-permute-done | bytes 262176 | tf_op jit(solution)/shard_map/pre_act_exchange/ppermute | solution.py:405
  128.9 0.9 copy-done.4
  130.5 2.7 %collective-permute-start.6 = (bf16[1024,128]{1,0:T(8,128)(2,1)S(1)}, bf16[1024,128]{1,0:T(8,128)(2,1)S(1)}, u32[]{:S(2)}, u32[]{:S(2)}) collective-permute-start(bf16[1024,128]{1,0:T(8,128)(2,1)S(1)} %get-tuple-element.51), channel_id=1, source_target_pairs={{0,96},{32,0},{64,32},{96,64},{1,97},{33,1},{65,33},{97,65},{2,98}... | collective-permute-start | bytes 786440 | tf_op jit(solution)/shard_map/slope_exchange/ppermute | solution.py:405
  133.6 1.5 collective-permute-start.9
  135.3 0.8 fusion
  137.8 3.6 %collective-permute-done.7 = bf16[1024,128]{1,0:T(8,128)(2,1)S(1)} collective-permute-done((bf16[1024,128]{1,0:T(8,128)(2,1)S(1)}, bf16[1024,128]{1,0:T(8,128)(2,1)S(1)}, u32[]{:S(2)}, u32[]{:S(2)}) %collective-permute-start.7) | collective-permute-done | bytes 262176 | tf_op jit(solution)/shard_map/slope_exchange/ppermute | solution.py:405
  141.4 3.0 %collective-permute-start.11 = (bf16[1024,128]{1,0:T(8,128)(2,1)S(1)}, bf16[1024,128]{1,0:T(8,128)(2,1)S(1)}, u32[]{:S(2)}, u32[]{:S(2)}) collective-permute-start(bf16[1024,128]{1,0:T(8,128)(2,1)S(1)} %collective-permute-done.7), channel_id=1, source_target_pairs={{0,96},{32,0},{64,32},{96,64},{1,97},{33,1},{65,33},{97,65},{2,98}... | collective-permute-start | bytes 786440 | tf_op jit(solution)/shard_map/slope_exchange/ppermute | solution.py:405
  144.3 0.8 convolution_convert_fusion.refs_2_
  145.1 3.4 %collective-permute-done.10 = bf16[1024,128]{1,0:T(8,128)(2,1)S(1)} collective-permute-done((bf16[1024,128]{1,0:T(8,128)(2,1)S(1)}, bf16[1024,128]{1,0:T(8,128)(2,1)S(1)}, u32[]{:S(2)}, u32[]{:S(2)}) %collective-permute-start.10) | collective-permute-done | bytes 262176 | tf_op jit(solution)/shard_map/slope_exchange/ppermute | solution.py:405
  149.3 1.0 pack_shards.1
  150.3 11.6 %all-to-all-start.2 = ((bf16[32,96,128]{2,1,0:T(8,128)(2,1)}), bf16[32,96,128]{2,1,0:T(8,128)(2,1)S(1)}, u32[]{:S(2)}, u32[]{:S(2)}) async-start(bf16[32,96,128]{2,1,0:T(8,128)(2,1)} %pack_shards.1), calls=%async_computation.2 | async-start | bytes 1572864 | tf_op jit(solution)/shard_map/gradients/all_to_all | solution.py:408
  163.0 4.3 %collective-permute-start.13 = (bf16[512,128]{1,0:T(8,128)(2,1)S(1)}, bf16[512,128]{1,0:T(8,128)(2,1)S(1)}, u32[]{:S(2)}, u32[]{:S(2)}) collective-permute-start(bf16[512,128]{1,0:T(8,128)(2,1)S(1)} %get-tuple-element.66), channel_id=1, source_target_pairs={{0,64},{32,96},{64,0},{96,32},{1,65},{33,97},{65,1},{97,33},{2,66}... | collective-permute-start | bytes 393224 | tf_op jit(solution)/shard_map/second_layer/ppermute | solution.py:405
  167.3 8.8 %all-to-all-done.2 = bf16[32,96,128]{2,1,0:T(8,128)(2,1)S(1)} async-done(((bf16[32,96,128]{2,1,0:T(8,128)(2,1)}), bf16[32,96,128]{2,1,0:T(8,128)(2,1)S(1)}, u32[]{:S(2)}, u32[]{:S(2)}) %all-to-all-start.2) | async-done | bytes 786464 | tf_op jit(solution)/shard_map/gradients/all_to_all | solution.py:408
  177.0 12.2 %all_to_all.21.mine_ref = bf16[16,96,128]{2,1,0:T(8,128)(2,1)S(1)} all-to-all(bf16[16,96,128]{2,1,0:T(8,128)(2,1)S(1)} %broadcast_in_dim.7), channel_id=1, replica_groups={{0,2,4,6,8,10,12,14,16,18,20,22,24,26,28,30},{1,3,5,7,9,11,13,15,17,19,..., dimensions={0} | all-to-all | bytes 786432 | tf_op jit(solution)/shard_map/gradients/all_to_all | solution.py:515
  189.3 2.4 %collective-permute-start.15 = (bf16[16,96,128]{2,1,0:T(8,128)(2,1)S(1)}, bf16[16,96,128]{2,1,0:T(8,128)(2,1)S(1)}, u32[]{:S(2)}, u32[]{:S(2)}) collective-permute-start(bf16[16,96,128]{2,1,0:T(8,128)(2,1)S(1)} %all_to_all.21.mine_ref), channel_id=1, source_target_pairs={{0,1},{1,0},{2,3},{3,2},{4,5},{5,4},{6,7},{7,6},{8,9},{9,8},{10,11... | collective-permute-start | bytes 1179656 | tf_op jit(solution)/shard_map/gradients/ppermute | solution.py:523
  191.7 1.3 collective-permute-done.15.other_ref
  193.0 1.8 finish.1
  (66 shorter events, 9.3 us)
Async XLA Ops:
  0.6 42.1 %copy-start = (bf16[512,512]{1,0:T(8,128)(2,1)S(1)}, bf16[512,512]{1,0:T(8,128)(2,1)}, u32[]{:S(2)}) copy-start(bf16[512,512]{1,0:T(8,128)(2,1)} %param.21) | copy-start | bytes 1572868
  33.9 5.0 %copy-start.10 = (s32[512,10]{0,1:T(8,128)S(1)}, s32[512,10]{0,1:T(8,128)}, u32[]{:S(2)}) copy-start(s32[512,10]{0,1:T(8,128)} %param.15) | copy-start | bytes 61444
  33.9 5.3 %copy-start.9 = (s32[2048,15]{0,1:T(8,128)S(1)}, s32[2048,15]{0,1:T(8,128)}, u32[]{:S(2)}) copy-start(s32[2048,15]{0,1:T(8,128)} %param.14) | copy-start | bytes 368644
  33.9 55.3 %all-to-all-start.1 = ((bf16[32,256,256]{2,1,0:T(8,128)(2,1)}), bf16[32,256,256]{2,1,0:T(8,128)(2,1)}, u32[]{:S(2)}, u32[]{:S(2)}) async-start(bf16[32,256,256]{2,1,0:T(8,128)(2,1)} %bitcast.26), calls=%async_computation.1 | async-start | bytes 8388608 | tf_op jit(solution)/shard_map/rows/all_to_all | solution.py:408
  39.7 3.1 %copy-start.6 = (bf16[128,512]{1,0:T(8,128)(2,1)S(1)}, bf16[128,512]{1,0:T(8,128)(2,1)}, u32[]{:S(2)}) copy-start(bf16[128,512]{1,0:T(8,128)(2,1)} %param.20) | copy-start | bytes 393220
  39.7 3.4 %copy-start.7 = (bf16[128,512]{1,0:T(8,128)(2,1)S(1)}, bf16[128,512]{1,0:T(8,128)(2,1)}, u32[]{:S(2)}) copy-start(bf16[128,512]{1,0:T(8,128)(2,1)} %param.19) | copy-start | bytes 393220
  42.8 1.4 copy-start.1
  89.2 39.7 %copy-start.5 = (bf16[128]{0:T(256)(128)(2,1)S(1)}, bf16[128]{0:T(256)(128)(2,1)}, u32[]{:S(2)}) copy-start(bf16[128]{0:T(256)(128)(2,1)} %param.18) | copy-start | bytes 772
  108.7 24.5 %copy-start.3 = (bf16[1024,128]{1,0:T(8,128)(2,1)S(1)}, bf16[1024,128]{1,0:T(8,128)(2,1)}, u32[]{:S(2)}) copy-start(bf16[1024,128]{1,0:T(8,128)(2,1)} %get-tuple-element.45.part0) | copy-start | bytes 786436
  108.7 7.8 %collective-permute-start = (bf16[1024,128]{1,0:T(8,128)(2,1)}, bf16[1024,128]{1,0:T(8,128)(2,1)S(1)}, u32[]{:S(2)}, u32[]{:S(2)}) collective-permute-start(bf16[1024,128]{1,0:T(8,128)(2,1)} %get-tuple-element.40), channel_id=1, source_target_pairs={{0,32},{32,64},{64,96},{96,0},{1,33},{33,65},{65,97},{97,1},{2,34}... | collective-permute-start | bytes 786440 | tf_op jit(solution)/shard_map/pre_act_exchange/ppermute | solution.py:405
  110.4 7.2 %collective-permute-start.4 = (bf16[1024,128]{1,0:T(8,128)(2,1)}, bf16[1024,128]{1,0:T(8,128)(2,1)S(1)}, u32[]{:S(2)}, u32[]{:S(2)}) collective-permute-start(bf16[1024,128]{1,0:T(8,128)(2,1)} %get-tuple-element.48), channel_id=1, source_target_pairs={{0,96},{32,0},{64,32},{96,64},{1,97},{33,1},{65,33},{97,65},{2,98}... | collective-permute-start | bytes 786440 | tf_op jit(solution)/shard_map/pre_act_exchange/ppermute | solution.py:405
  112.6 9.4 %collective-permute-start.2 = (bf16[1024,128]{1,0:T(8,128)(2,1)}, bf16[1024,128]{1,0:T(8,128)(2,1)S(1)}, u32[]{:S(2)}, u32[]{:S(2)}) collective-permute-start(bf16[1024,128]{1,0:T(8,128)(2,1)} %get-tuple-element.41), channel_id=1, source_target_pairs={{0,96},{32,0},{64,32},{96,64},{1,97},{33,1},{65,33},{97,65},{2,98}... | collective-permute-start | bytes 786440 | tf_op jit(solution)/shard_map/pre_act_exchange/ppermute | solution.py:405
  114.0 19.2 %collective-permute-start.3 = (bf16[1024,128]{1,0:T(8,128)(2,1)}, bf16[1024,128]{1,0:T(8,128)(2,1)S(1)}, u32[]{:S(2)}, u32[]{:S(2)}) collective-permute-start(bf16[1024,128]{1,0:T(8,128)(2,1)} %get-tuple-element.46), channel_id=1, source_target_pairs={{0,32},{32,64},{64,96},{96,0},{1,33},{33,65},{65,97},{97,1},{2,34}... | collective-permute-start | bytes 786440 | tf_op jit(solution)/shard_map/pre_act_exchange/ppermute | solution.py:405
  117.5 11.4 %collective-permute-start.1 = (bf16[1024,128]{1,0:T(8,128)(2,1)S(1)}, bf16[1024,128]{1,0:T(8,128)(2,1)S(1)}, u32[]{:S(2)}, u32[]{:S(2)}) collective-permute-start(bf16[1024,128]{1,0:T(8,128)(2,1)S(1)} %add_convert_fusion.1), channel_id=1, source_target_pairs={{0,32},{32,64},{64,96},{96,0},{1,33},{33,65},{65,97},{97,1},{2,34}... | collective-permute-start | bytes 786440 | tf_op jit(solution)/shard_map/pre_act_exchange/ppermute | solution.py:405
  119.3 13.9 %collective-permute-start.5 = (bf16[1024,128]{1,0:T(8,128)(2,1)}, bf16[1024,128]{1,0:T(8,128)(2,1)S(1)}, u32[]{:S(2)}, u32[]{:S(2)}) collective-permute-start(bf16[1024,128]{1,0:T(8,128)(2,1)} %add_convert_fusion), channel_id=1, source_target_pairs={{0,96},{32,0},{64,32},{96,64},{1,97},{33,1},{65,33},{97,65},{2,98}... | collective-permute-start | bytes 786440 | tf_op jit(solution)/shard_map/pre_act_exchange/ppermute | solution.py:405
  128.9 1.0 copy-start.4
  129.9 5.5 %copy-start.2 = (bf16[512,2048]{1,0:T(8,128)(2,1)S(1)}, bf16[512,2048]{1,0:T(8,128)(2,1)}, u32[]{:S(2)}) copy-start(bf16[512,2048]{1,0:T(8,128)(2,1)} %copy-done.1) | copy-start | bytes 6291460
  130.2 7.5 %collective-permute-start.8 = (bf16[1024,128]{1,0:T(8,128)(2,1)S(1)}, bf16[1024,128]{1,0:T(8,128)(2,1)S(1)}, u32[]{:S(2)}, u32[]{:S(2)}) collective-permute-start(bf16[1024,128]{1,0:T(8,128)(2,1)S(1)} %get-tuple-element.51), channel_id=1, source_target_pairs={{0,32},{32,64},{64,96},{96,0},{1,33},{33,65},{65,97},{97,1},{2,34}... | collective-permute-start | bytes 786440 | tf_op jit(solution)/shard_map/slope_exchange/ppermute | solution.py:405
  130.5 13.9 %collective-permute-start.6 = (bf16[1024,128]{1,0:T(8,128)(2,1)S(1)}, bf16[1024,128]{1,0:T(8,128)(2,1)S(1)}, u32[]{:S(2)}, u32[]{:S(2)}) collective-permute-start(bf16[1024,128]{1,0:T(8,128)(2,1)S(1)} %get-tuple-element.51), channel_id=1, source_target_pairs={{0,96},{32,0},{64,32},{96,64},{1,97},{33,1},{65,33},{97,65},{2,98}... | collective-permute-start | bytes 786440 | tf_op jit(solution)/shard_map/slope_exchange/ppermute | solution.py:405
  133.5 7.8 %collective-permute-start.7 = (bf16[1024,128]{1,0:T(8,128)(2,1)S(1)}, bf16[1024,128]{1,0:T(8,128)(2,1)S(1)}, u32[]{:S(2)}, u32[]{:S(2)}) collective-permute-start(bf16[1024,128]{1,0:T(8,128)(2,1)S(1)} %get-tuple-element.52), channel_id=1, source_target_pairs={{0,96},{32,0},{64,32},{96,64},{1,97},{33,1},{65,33},{97,65},{2,98}... | collective-permute-start | bytes 786440 | tf_op jit(solution)/shard_map/slope_exchange/ppermute | solution.py:405
  133.6 10.7 %collective-permute-start.9 = (bf16[1024,128]{1,0:T(8,128)(2,1)S(1)}, bf16[1024,128]{1,0:T(8,128)(2,1)S(1)}, u32[]{:S(2)}, u32[]{:S(2)}) collective-permute-start(bf16[1024,128]{1,0:T(8,128)(2,1)S(1)} %get-tuple-element.52), channel_id=1, source_target_pairs={{0,32},{32,64},{64,96},{96,0},{1,33},{33,65},{65,97},{97,1},{2,34}... | collective-permute-start | bytes 786440 | tf_op jit(solution)/shard_map/slope_exchange/ppermute | solution.py:405
  135.3 1.6 copy-start.11
  137.7 10.8 %collective-permute-start.10 = (bf16[1024,128]{1,0:T(8,128)(2,1)S(1)}, bf16[1024,128]{1,0:T(8,128)(2,1)S(1)}, u32[]{:S(2)}, u32[]{:S(2)}) collective-permute-start(bf16[1024,128]{1,0:T(8,128)(2,1)S(1)} %collective-permute-done.8), channel_id=1, source_target_pairs={{0,32},{32,64},{64,96},{96,0},{1,33},{33,65},{65,97},{97,1},{2,34}... | collective-permute-start | bytes 786440 | tf_op jit(solution)/shard_map/slope_exchange/ppermute | solution.py:405
  141.4 7.1 %collective-permute-start.11 = (bf16[1024,128]{1,0:T(8,128)(2,1)S(1)}, bf16[1024,128]{1,0:T(8,128)(2,1)S(1)}, u32[]{:S(2)}, u32[]{:S(2)}) collective-permute-start(bf16[1024,128]{1,0:T(8,128)(2,1)S(1)} %collective-permute-done.7), channel_id=1, source_target_pairs={{0,96},{32,0},{64,32},{96,64},{1,97},{33,1},{65,33},{97,65},{2,98}... | collective-permute-start | bytes 786440 | tf_op jit(solution)/shard_map/slope_exchange/ppermute | solution.py:405
  149.3 12.9 %copy-start.8 = (bf16[128,512]{1,0:T(8,128)(2,1)S(1)}, bf16[128,512]{1,0:T(8,128)(2,1)}, u32[]{:S(2)}) copy-start(bf16[128,512]{1,0:T(8,128)(2,1)} %param.19) | copy-start | bytes 393220
  150.3 25.8 %all-to-all-start.2 = ((bf16[32,96,128]{2,1,0:T(8,128)(2,1)}), bf16[32,96,128]{2,1,0:T(8,128)(2,1)S(1)}, u32[]{:S(2)}, u32[]{:S(2)}) async-start(bf16[32,96,128]{2,1,0:T(8,128)(2,1)} %pack_shards.1), calls=%async_computation.2 | async-start | bytes 1572864 | tf_op jit(solution)/shard_map/gradients/all_to_all | solution.py:408
  162.6 13.6 %collective-permute-start.12 = (bf16[512,128]{1,0:T(8,128)(2,1)S(1)}, bf16[512,128]{1,0:T(8,128)(2,1)S(1)}, u32[]{:S(2)}, u32[]{:S(2)}) collective-permute-start(bf16[512,128]{1,0:T(8,128)(2,1)S(1)} %get-tuple-element.67), channel_id=1, source_target_pairs={{0,32},{32,64},{64,96},{96,0},{1,33},{33,65},{65,97},{97,1},{2,34}... | collective-permute-start | bytes 393224 | tf_op jit(solution)/shard_map/second_layer/ppermute | solution.py:405
  163.0 13.3 %collective-permute-start.13 = (bf16[512,128]{1,0:T(8,128)(2,1)S(1)}, bf16[512,128]{1,0:T(8,128)(2,1)S(1)}, u32[]{:S(2)}, u32[]{:S(2)}) collective-permute-start(bf16[512,128]{1,0:T(8,128)(2,1)S(1)} %get-tuple-element.66), channel_id=1, source_target_pairs={{0,64},{32,96},{64,0},{96,32},{1,65},{33,97},{65,1},{97,33},{2,66}... | collective-permute-start | bytes 393224 | tf_op jit(solution)/shard_map/second_layer/ppermute | solution.py:405
  167.3 9.0 %collective-permute-start.14 = (bf16[512,128]{1,0:T(8,128)(2,1)S(1)}, bf16[512,128]{1,0:T(8,128)(2,1)S(1)}, u32[]{:S(2)}, u32[]{:S(2)}) collective-permute-start(bf16[512,128]{1,0:T(8,128)(2,1)S(1)} %get-tuple-element.65), channel_id=1, source_target_pairs={{0,96},{32,0},{64,32},{96,64},{1,97},{33,1},{65,33},{97,65},{2,98}... | collective-permute-start | bytes 393224 | tf_op jit(solution)/shard_map/second_layer/ppermute | solution.py:405
  189.3 3.7 %collective-permute-start.15 = (bf16[16,96,128]{2,1,0:T(8,128)(2,1)S(1)}, bf16[16,96,128]{2,1,0:T(8,128)(2,1)S(1)}, u32[]{:S(2)}, u32[]{:S(2)}) collective-permute-start(bf16[16,96,128]{2,1,0:T(8,128)(2,1)S(1)} %all_to_all.21.mine_ref), channel_id=1, source_target_pairs={{0,1},{1,0},{2,3},{3,2},{4,5},{5,4},{6,7},{7,6},{8,9},{9,8},{10,11... | collective-permute-start | bytes 1179656 | tf_op jit(solution)/shard_map/gradients/ppermute | solution.py:523

commit v4 on v3

--- a/solution.py
+++ b/solution.py
@@ -148,7 +148,7 @@
         out_ref[pl.ds(begin, 16), half:] = jnp.concatenate(highs, axis=0).astype(BF)
         return carry
 
-    lax.fori_loop(0, count // 16, some, 0, unroll=4)
+    lax.fori_loop(0, count // 16, some, 0, unroll=8)
 
 
 def piece_copies(source_ref, held, sems):
@@ -293,9 +293,10 @@
                 pltpu.SemaphoreType.DMA((steps,)),
             ],
         ),
-        out_shape=[jax.ShapeDtypeStruct((targets // 2, share), BF)] * (2 * quarters)
+        out_shape=[jax.ShapeDtypeStruct((targets // 2, share), BF)] * 2
+        + [pltpu.VMEM((targets // 2, share), BF)] * (2 * quarters - 2)
         + [jax.ShapeDtypeStruct((targets, 2 * width), BF)],
-        compiler_params=pltpu.CompilerParams(vmem_limit_bytes=62 << 20),
+        compiler_params=pltpu.CompilerParams(vmem_limit_bytes=60 << 20),
         name="first_layer",
     )(idx, spot, arrived, counts, w_self, w_near)
 
@@ -327,30 +328,31 @@
     )(part0, up, down, bias, d_hidden)
 
 
-def pack_kernel(*refs):
-    *value_refs, out_ref = refs
-    peers, _, share = out_ref.shape
-    chips = peers // 2
+def pack_kernel(core_ref, *refs):
+    *value_refs, keep_ref, give_ref = refs
+    chips, _, share = keep_ref.shape
     first = 0
     for ref in value_refs:
-        rows = ref.shape[0] // peers
+        rows = ref.shape[0] // (2 * chips)
         for c in range(ref.shape[1] // share):
-            for peer in range(peers):
-                shard = peer % 2 * chips + peer // 2
-                out_ref[peer, first:first + rows, :] = ref[shard * rows:(shard + 1) * rows, c * share:(c + 1) * share]
+            cols = slice(c * share, (c + 1) * share)
+            for out_ref, core in ((keep_ref, core_ref[0]), (give_ref, 1 - core_ref[0])):
+                block = ref[chunk(core, chips * rows), cols]
+                out_ref[:, first:first + rows, :] = block.reshape(chips, rows, share)
             first += rows
 
 
-def pack_shards(values, peers, share):
-    rows = sum(v.size for v in values) // (peers * share)
+def pack_shards(core, values, chips, share):
+    rows = sum(v.size for v in values) // (2 * chips * share)
     return pl.pallas_call(
         pack_kernel,
-        in_specs=[pl.BlockSpec(memory_space=pltpu.VMEM)] * len(values),
-        out_specs=pl.BlockSpec(memory_space=pltpu.VMEM),
-        out_shape=jax.ShapeDtypeStruct((peers, rows, share), BF),
+        in_specs=[pl.BlockSpec(memory_space=pltpu.SMEM)]
+        + [pl.BlockSpec(memory_space=pltpu.VMEM)] * len(values),
+        out_specs=[pl.BlockSpec(memory_space=pltpu.VMEM)] * 2,
+        out_shape=[jax.ShapeDtypeStruct((chips, rows, share), BF)] * 2,
         compiler_params=pltpu.CompilerParams(vmem_limit_bytes=16 << 20),
         name="pack_shards",
-    )(*values)
+    )(core, *values)
 
 
 def finish_kernel(spot_ref, mine_ref, other_ref, ws_ref, wn_ref, vs_ref, vn_ref):
@@ -475,8 +477,18 @@
     def grad_w(slope_part):
         return lax.dot_general(both, slope_part, TN, preferred_element_type=F32).astype(BF)
 
-    def scatter_sum(values):
-        return jnp.sum(exchange(values).astype(F32), axis=0).astype(BF)
+    def swap(value):
+        return lax.ppermute(value, "wide", [(i, i ^ 1) for i in range(peers)])
+
+    def between_chips(value):
+        return lax.all_to_all(
+            value,
+            "wide",
+            split_axis=0,
+            concat_axis=0,
+            axis_index_groups=[list(range(c, peers, 2)) for c in range(2)],
+            tiled=True,
+        )
 
     with jax.named_scope("second_layer"):
         hidden = jnp.concatenate(hiddens)
@@ -501,26 +513,19 @@
         outs = [shift(out_part(d).astype(BF), d) for d in range(1, quarters)]
     with jax.named_scope("gradients"):
         near_two = grad_w(jnp.concatenate([from_up, from_down], axis=1))
-        packed = pack_shards(
-            [grad_v, grad_w(jnp.concatenate(slopes)), near_two, grad_w(from_far)], peers, share
-        )
-        sums = scatter_sum(packed)
-        sums, *outs = lax.optimization_barrier((sums, *outs))
+        chips = peers // 2
+        keep, give = pack_shards(
+            core.reshape(1), [grad_v, grad_w(jnp.concatenate(slopes)), near_two, grad_w(from_far)], chips, share
+        )
+        sums = between_chips(added(keep, swap(give)))
+        sums = jnp.sum(sums.astype(F32), axis=0).astype(BF)
+        mine = between_chips(jnp.broadcast_to(sums, (chips, *sums.shape)))
+        mine, *outs = lax.optimization_barrier((mine, *outs))
+        other = swap(mine)
         seed_out = out_part(0)
         for part in outs:
             seed_out = seed_out + part.astype(F32)
         seed_out = seed_out.astype(BF)
-        sums, seed_out = lax.optimization_barrier((sums, seed_out))
-        chips = peers // 2
-        mine = lax.all_to_all(
-            jnp.broadcast_to(sums, (chips, *sums.shape)),
-            "wide",
-            split_axis=0,
-            concat_axis=0,
-            axis_index_groups=[list(range(c, peers, 2)) for c in range(2)],
-            tiled=True,
-        )
-        other = lax.ppermute(mine, "wide", [(i, i ^ 1) for i in range(peers)])
         grads = pl.pallas_call(
             finish_kernel,
             in_specs=[pl.BlockSpec(memory_space=pltpu.SMEM)] + [pl.BlockSpec(memory_space=pltpu.VMEM)] * 2,

time: 195 us -> 193 us (0.990)
  blocking collectives: 28.1 us -> 16 us
  waiting for transfers between devices: 57.6 us -> 65.8 us
  starting transfers between devices: 39.2 us -> 42 us
    all_to_all x1 -> x0, blocking collectives: 12.2 us -> none  [body(): lax.all_to_all(jnp.broadcast_to(sums, (chips, *sums.shape)), 'wide', spli...]
    all_to_all x2 -> x1, starting transfers between devices: 16.5 us -> 4.99 us  [exchange(): lax.all_to_all(value, 'wide', split_axis=0, concat_axis=0, tiled=True)]
    all_to_all x0 -> x2, starting transfers between devices: none -> 10.7 us  [between_chips(): lax.all_to_all(value, 'wide', split_axis=0, concat_axis=0, axis_index_gro...]
    all_to_all x0 -> x2, waiting for transfers between devices: none -> 9.16 us  [between_chips(): lax.all_to_all(value, 'wide', split_axis=0, concat_axis=0, axis_index_gro...]
    all_to_all x2 -> x1, waiting for transfers between devices: 39.9 us -> 31.1 us  [exchange(): lax.all_to_all(value, 'wide', split_axis=0, concat_axis=0, tiled=True)]
    ppermute x15, waiting for transfers between devices: 16.4 us -> 23.6 us  [shift(): lax.ppermute(value, 'blk', [(i, (i + by) % quarters) for i in range(quart...]
    ppermute x1 -> x2, starting transfers between devices: 2.39 us -> 6.21 us  [swap(): return lax.ppermute(value, 'wide', [(i, i ^ 1) for i in range(peers)])]
  transfers between devices with their start and end apart: 18 -> 20, of which waited for: 7 -> 12; matrix products, arithmetic and copies ran while one was open for 5% -> 4% of each run, Pallas kernels for 8% -> 9%
where the time goes in v4:
time: 193 us; the launch traced here: 192 us
  waiting for transfers between devices  65.8 us (34%)
  Pallas kernels  54.8 us (28%)
  starting transfers between devices  42 us (22%)
  blocking collectives  16 us (8%)
  matrix products  5.53 us (3%)
  local copies, waits for them, and re-layouts  4.26 us (2%)
  other arithmetic  2.72 us (1%)
    all_to_all x1, waiting for transfers between devices, exchange(): lax.all_to_all(value, 'wide', split_axis=0, concat_axis=0, tiled=True)  31.1 us
    ppermute x15, waiting for transfers between devices, shift(): lax.ppermute(value, 'blk', [(i, (i + by) % quarters) for i in range(quart...  23.6 us
    ppermute x15, starting transfers between devices, shift(): lax.ppermute(value, 'blk', [(i, (i + by) % quarters) for i in range(quart...  20.2 us
    pallas_call x1, Pallas kernels, first_layer(): pl.pallas_call(functools.partial(layer_kernel, list_width), grid_spec=plt...  18.9 us
    all_to_all x1, blocking collectives, exchange(): lax.all_to_all(value, 'wide', split_axis=0, concat_axis=0, tiled=True)  16 us
    pallas_call x2, Pallas kernels, neighbour_counts(): pl.pallas_call(count_kernel, grid=(targets // 16 // block_groups,), in_sp...  15.7 us
    pallas_call x1, Pallas kernels, gather_rows(): pl.pallas_call(gather_kernel, grid_spec=pltpu.PrefetchScalarGridSpec(num_...  14.7 us
    all_to_all x2, starting transfers between devices, between_chips(): lax.all_to_all(value, 'wide', split_axis=0, concat_axis=0, axis_index_gro...  10.7 us
  transfers between devices with their start and end apart: 20, of which 12 were waited for; matrix products, arithmetic and copies ran while one was open for 4% of the time, Pallas kernels for 9%

profile of v4, /device:TPU:1, one launch (start us, length us, event | category | flops | bytes accessed | tf_op | source)
XLA Modules:
  0.0 192.1 jit_solution(14002627097090245008)
XLA Ops:
  0.6 2.9 %request_table.1 = (s32[32,1,256]{2,1,0:T(1,128)}, s32[32,128]{1,0:T(8,128)}) custom-call(s32[32,128]{1,0:T(8,128)} %bitcast.28, s32[32,128]{1,0:T(8,128)} %bitcast.29), custom_call_target="tpu_custom_call" | custom-call | tf_op jit(solution)/shard_map/requests/request_table/pallas_call | solution.py:66
  3.6 16.0 %all_to_all.20 = s32[32,1,256]{2,1,0:T(1,128)} all-to-all(s32[32,1,256]{2,1,0:T(1,128)} %get-tuple-element.35), channel_id=1, replica_groups=mesh['blk'=4,'wide'=32] {'wide'}, dimensions={0} | all-to-all | bytes 65536 | tf_op jit(solution)/shard_map/requests/all_to_all | solution.py:410
  19.5 14.7 %gather_rows.1 = bf16[8192,256]{1,0:T(8,128)(2,1)} custom-call(s32[8192]{0:T(1024)} %bitcast.27, bf16[8192,256]{1,0:T(8,128)(2,1)} %table_ref.1), custom_call_target="tpu_custom_call" | custom-call | tf_op jit(solution)/shard_map/rows/gather_rows/pallas_call | solution.py:196
  34.3 5.0 %all-to-all-start.1 = ((bf16[32,256,256]{2,1,0:T(8,128)(2,1)}), bf16[32,256,256]{2,1,0:T(8,128)(2,1)}, u32[]{:S(2)}, u32[]{:S(2)}) async-start(bf16[32,256,256]{2,1,0:T(8,128)(2,1)} %bitcast.26), calls=%async_computation.1 | async-start | bytes 8388608 | tf_op jit(solution)/shard_map/rows/all_to_all | solution.py:410
  40.5 2.6 %neighbour_counts.3 = bf16[512,2048]{1,0:T(8,128)(2,1)S(1)} custom-call(s32[32,256]{1,0:T(8,128)S(1)} %reshape.48.idx_ref), custom_call_target="tpu_custom_call" | custom-call | flops 536870912 | bytes 2097152 | tf_op jit(solution)/shard_map/beside_rows/neighbour_counts/pallas_call | solution.py:112
  45.3 13.1 %neighbour_counts.2.counts_ref = bf16[2048,4096]{1,0:T(8,128)(2,1)} custom-call(s32[128,256]{1,0:T(8,128)S(1)} %reshape.47.idx_ref), custom_call_target="tpu_custom_call" | custom-call | flops 4294967296 | bytes 16777216 | tf_op jit(solution)/shard_map/beside_rows/neighbour_counts/pallas_call | solution.py:112
  58.5 31.1 %all-to-all-done.1 = bf16[32,256,256]{2,1,0:T(8,128)(2,1)} async-done(((bf16[32,256,256]{2,1,0:T(8,128)(2,1)}), bf16[32,256,256]{2,1,0:T(8,128)(2,1)}, u32[]{:S(2)}, u32[]{:S(2)}) %all-to-all-start.1) | async-done | bytes 4194336 | tf_op jit(solution)/shard_map/rows/all_to_all | solution.py:410
  89.6 18.9 %first_layer.1 = (bf16[1024,128]{1,0:T(8,128)(2,1)}, bf16[1024,128]{1,0:T(8,128)(2,1)}, bf16[1024,128]{1,0:T(8,128)(2,1)S(1)}, bf16[1024,128]{1,0:T(8,128)(2,1)}...) custom-call(s32[4096]{0:T(1024)} %bitcast.30, ...), custom_call_target="tpu_custom_call" | custom-call | tf_op jit(solution)/shard_map/first_layer/first_layer/pallas_call | solution.py:274
  108.6 1.7 collective-permute-start
  110.3 2.2 %collective-permute-start.4 = (bf16[1024,128]{1,0:T(8,128)(2,1)}, bf16[1024,128]{1,0:T(8,128)(2,1)S(1)}, u32[]{:S(2)}, u32[]{:S(2)}) collective-permute-start(bf16[1024,128]{1,0:T(8,128)(2,1)} %get-tuple-element.48), channel_id=1, source_target_pairs={{0,96},{32,0},{64,32},{96,64},{1,97},{33,1},{65,33},{97,65},{2,98}... | collective-permute-start | bytes 786440 | tf_op jit(solution)/shard_map/pre_act_exchange/ppermute | solution.py:407
  112.5 1.4 collective-permute-start.2
  114.0 2.2 %collective-permute-done = bf16[1024,128]{1,0:T(8,128)(2,1)S(1)} collective-permute-done((bf16[1024,128]{1,0:T(8,128)(2,1)S(1)}, bf16[1024,128]{1,0:T(8,128)(2,1)S(1)}, u32[]{:S(2)}, u32[]{:S(2)}) %collective-permute-start) | collective-permute-done | bytes 262176 | tf_op jit(solution)/shard_map/pre_act_exchange/ppermute | solution.py:407
  117.1 2.8 %collective-permute-start.5 = (bf16[1024,128]{1,0:T(8,128)(2,1)}, bf16[1024,128]{1,0:T(8,128)(2,1)S(1)}, u32[]{:S(2)}, u32[]{:S(2)}) collective-permute-start(bf16[1024,128]{1,0:T(8,128)(2,1)} %add_convert_fusion.1), channel_id=1, source_target_pairs={{0,96},{32,0},{64,32},{96,64},{1,97},{33,1},{65,33},{97,65},{2,98}... | collective-permute-start | bytes 786440 | tf_op jit(solution)/shard_map/pre_act_exchange/ppermute | solution.py:407
  120.5 8.2 %collective-permute-done.1.up = bf16[1024,128]{1,0:T(8,128)(2,1)S(1)} collective-permute-done((bf16[1024,128]{1,0:T(8,128)(2,1)S(1)}, bf16[1024,128]{1,0:T(8,128)(2,1)S(1)}, u32[]{:S(2)}, u32[]{:S(2)}) %collective-permute-start.1) | collective-permute-done | bytes 262176 | tf_op jit(solution)/shard_map/pre_act_exchange/ppermute | solution.py:407
  128.7 0.9 copy-done.4
  130.1 2.7 %collective-permute-start.6 = (bf16[1024,128]{1,0:T(8,128)(2,1)S(1)}, bf16[1024,128]{1,0:T(8,128)(2,1)S(1)}, u32[]{:S(2)}, u32[]{:S(2)}) collective-permute-start(bf16[1024,128]{1,0:T(8,128)(2,1)S(1)} %get-tuple-element.51), channel_id=1, source_target_pairs={{0,96},{32,0},{64,32},{96,64},{1,97},{33,1},{65,33},{97,65},{2,98}... | collective-permute-start | bytes 786440 | tf_op jit(solution)/shard_map/slope_exchange/ppermute | solution.py:407
  133.2 1.5 collective-permute-start.9
  134.9 0.8 fusion
  137.4 3.7 %collective-permute-done.7 = bf16[1024,128]{1,0:T(8,128)(2,1)S(1)} collective-permute-done((bf16[1024,128]{1,0:T(8,128)(2,1)S(1)}, bf16[1024,128]{1,0:T(8,128)(2,1)S(1)}, u32[]{:S(2)}, u32[]{:S(2)}) %collective-permute-start.7) | collective-permute-done | bytes 262176 | tf_op jit(solution)/shard_map/slope_exchange/ppermute | solution.py:407
  141.1 2.9 %collective-permute-start.11 = (bf16[1024,128]{1,0:T(8,128)(2,1)S(1)}, bf16[1024,128]{1,0:T(8,128)(2,1)S(1)}, u32[]{:S(2)}, u32[]{:S(2)}) collective-permute-start(bf16[1024,128]{1,0:T(8,128)(2,1)S(1)} %collective-permute-done.7), channel_id=1, source_target_pairs={{0,96},{32,0},{64,32},{96,64},{1,97},{33,1},{65,33},{97,65},{2,98}... | collective-permute-start | bytes 786440 | tf_op jit(solution)/shard_map/slope_exchange/ppermute | solution.py:407
  144.7 3.4 %collective-permute-done.10 = bf16[1024,128]{1,0:T(8,128)(2,1)S(1)} collective-permute-done((bf16[1024,128]{1,0:T(8,128)(2,1)S(1)}, bf16[1024,128]{1,0:T(8,128)(2,1)S(1)}, u32[]{:S(2)}, u32[]{:S(2)}) %collective-permute-start.10) | collective-permute-done | bytes 262176 | tf_op jit(solution)/shard_map/slope_exchange/ppermute | solution.py:407
  149.0 4.4 %collective-permute-start.12 = (bf16[16,96,128]{2,1,0:T(8,128)(2,1)S(1)}, bf16[16,96,128]{2,1,0:T(8,128)(2,1)S(1)}, u32[]{:S(2)}, u32[]{:S(2)}) collective-permute-start(bf16[16,96,128]{2,1,0:T(8,128)(2,1)S(1)} %get-tuple-element.54), channel_id=1, source_target_pairs={{0,1},{1,0},{2,3},{3,2},{4,5},{5,4},{6,7},{7,6},{8,9},{9,8},{10,11... | collective-permute-start | bytes 1179656 | tf_op jit(solution)/shard_map/gradients/ppermute | solution.py:481
  153.4 1.3 collective-permute-done.12
  154.7 0.8 add_convert_fusion
  155.6 7.1 %all-to-all-start.2 = ((bf16[16,96,128]{2,1,0:T(8,128)(2,1)}), bf16[16,96,128]{2,1,0:T(8,128)(2,1)S(1)}, u32[]{:S(2)}, u32[]{:S(2)}) async-start(bf16[16,96,128]{2,1,0:T(8,128)(2,1)} %add_convert_fusion), calls=%async_computation.2 | async-start | bytes 786432 | tf_op jit(solution)/shard_map/gradients/all_to_all | solution.py:484
  163.1 9.2 %all-to-all-done.2 = bf16[16,96,128]{2,1,0:T(8,128)(2,1)S(1)} async-done(((bf16[16,96,128]{2,1,0:T(8,128)(2,1)}), bf16[16,96,128]{2,1,0:T(8,128)(2,1)S(1)}, u32[]{:S(2)}, u32[]{:S(2)}) %all-to-all-start.2) | async-done | bytes 393248 | tf_op jit(solution)/shard_map/gradients/all_to_all | solution.py:484
  173.1 3.6 %all-to-all-start.3 = ((bf16[16,96,128]{2,1,0:T(8,128)(2,1)}), bf16[16,96,128]{2,1,0:T(8,128)(2,1)S(1)}, u32[]{:S(2)}, u32[]{:S(2)}) async-start(bf16[16,96,128]{2,1,0:T(8,128)(2,1)} %broadcast_in_dim.7), calls=%async_computation.3 | async-start | bytes 786432 | tf_op jit(solution)/shard_map/gradients/all_to_all | solution.py:484
  177.2 4.5 %collective-permute-start.14 = (bf16[512,128]{1,0:T(8,128)(2,1)S(1)}, bf16[512,128]{1,0:T(8,128)(2,1)S(1)}, u32[]{:S(2)}, u32[]{:S(2)}) collective-permute-start(bf16[512,128]{1,0:T(8,128)(2,1)S(1)} %get-tuple-element.66), channel_id=1, source_target_pairs={{0,64},{32,96},{64,0},{96,32},{1,65},{33,97},{65,1},{97,33},{2,66}... | collective-permute-start | bytes 393224 | tf_op jit(solution)/shard_map/second_layer/ppermute | solution.py:407
  181.7 1.5 collective-permute-done.13
  183.2 3.3 %collective-permute-done.14 = bf16[512,128]{1,0:T(8,128)(2,1)S(1)} collective-permute-done((bf16[512,128]{1,0:T(8,128)(2,1)S(1)}, bf16[512,128]{1,0:T(8,128)(2,1)S(1)}, u32[]{:S(2)}, u32[]{:S(2)}) %collective-permute-start.14) | collective-permute-done | bytes 131104 | tf_op jit(solution)/shard_map/second_layer/ppermute | solution.py:407
  187.2 1.8 collective-permute-start.16
  190.4 1.8 finish.1
  (68 shorter events, 13.1 us)
Async XLA Ops:
  0.6 42.5 %copy-start = (bf16[512,512]{1,0:T(8,128)(2,1)S(1)}, bf16[512,512]{1,0:T(8,128)(2,1)}, u32[]{:S(2)}) copy-start(bf16[512,512]{1,0:T(8,128)(2,1)} %param.21) | copy-start | bytes 1572868
  34.2 5.0 %copy-start.9 = (s32[512,10]{0,1:T(8,128)S(1)}, s32[512,10]{0,1:T(8,128)}, u32[]{:S(2)}) copy-start(s32[512,10]{0,1:T(8,128)} %param.15) | copy-start | bytes 61444
  34.3 5.3 %copy-start.8 = (s32[2048,15]{0,1:T(8,128)S(1)}, s32[2048,15]{0,1:T(8,128)}, u32[]{:S(2)}) copy-start(s32[2048,15]{0,1:T(8,128)} %param.14) | copy-start | bytes 368644
  34.3 55.4 %all-to-all-start.1 = ((bf16[32,256,256]{2,1,0:T(8,128)(2,1)}), bf16[32,256,256]{2,1,0:T(8,128)(2,1)}, u32[]{:S(2)}, u32[]{:S(2)}) async-start(bf16[32,256,256]{2,1,0:T(8,128)(2,1)} %bitcast.26), calls=%async_computation.1 | async-start | bytes 8388608 | tf_op jit(solution)/shard_map/rows/all_to_all | solution.py:410
  40.1 3.1 %copy-start.6 = (bf16[128,512]{1,0:T(8,128)(2,1)S(1)}, bf16[128,512]{1,0:T(8,128)(2,1)}, u32[]{:S(2)}) copy-start(bf16[128,512]{1,0:T(8,128)(2,1)} %param.20) | copy-start | bytes 393220
  40.1 3.4 %copy-start.7 = (bf16[128,512]{1,0:T(8,128)(2,1)S(1)}, bf16[128,512]{1,0:T(8,128)(2,1)}, u32[]{:S(2)}) copy-start(bf16[128,512]{1,0:T(8,128)(2,1)} %param.19) | copy-start | bytes 393220
  43.2 1.4 copy-start.1
  89.6 39.0 %copy-start.5 = (bf16[128]{0:T(256)(128)(2,1)S(1)}, bf16[128]{0:T(256)(128)(2,1)}, u32[]{:S(2)}) copy-start(bf16[128]{0:T(256)(128)(2,1)} %param.18) | copy-start | bytes 772
  108.6 24.2 %copy-start.3 = (bf16[1024,128]{1,0:T(8,128)(2,1)S(1)}, bf16[1024,128]{1,0:T(8,128)(2,1)}, u32[]{:S(2)}) copy-start(bf16[1024,128]{1,0:T(8,128)(2,1)} %get-tuple-element.45.part0) | copy-start | bytes 786436
  108.6 7.6 %collective-permute-start = (bf16[1024,128]{1,0:T(8,128)(2,1)S(1)}, bf16[1024,128]{1,0:T(8,128)(2,1)S(1)}, u32[]{:S(2)}, u32[]{:S(2)}) collective-permute-start(bf16[1024,128]{1,0:T(8,128)(2,1)S(1)} %get-tuple-element.40), channel_id=1, source_target_pairs={{0,32},{32,64},{64,96},{96,0},{1,33},{33,65},{65,97},{97,1},{2,34}... | collective-permute-start | bytes 786440 | tf_op jit(solution)/shard_map/pre_act_exchange/ppermute | solution.py:407
  110.3 6.0 %collective-permute-start.4 = (bf16[1024,128]{1,0:T(8,128)(2,1)}, bf16[1024,128]{1,0:T(8,128)(2,1)S(1)}, u32[]{:S(2)}, u32[]{:S(2)}) collective-permute-start(bf16[1024,128]{1,0:T(8,128)(2,1)} %get-tuple-element.48), channel_id=1, source_target_pairs={{0,96},{32,0},{64,32},{96,64},{1,97},{33,1},{65,33},{97,65},{2,98}... | collective-permute-start | bytes 786440 | tf_op jit(solution)/shard_map/pre_act_exchange/ppermute | solution.py:407
  112.5 8.0 %collective-permute-start.2 = (bf16[1024,128]{1,0:T(8,128)(2,1)}, bf16[1024,128]{1,0:T(8,128)(2,1)S(1)}, u32[]{:S(2)}, u32[]{:S(2)}) collective-permute-start(bf16[1024,128]{1,0:T(8,128)(2,1)} %get-tuple-element.41), channel_id=1, source_target_pairs={{0,96},{32,0},{64,32},{96,64},{1,97},{33,1},{65,33},{97,65},{2,98}... | collective-permute-start | bytes 786440 | tf_op jit(solution)/shard_map/pre_act_exchange/ppermute | solution.py:407
  113.9 18.8 %collective-permute-start.3 = (bf16[1024,128]{1,0:T(8,128)(2,1)}, bf16[1024,128]{1,0:T(8,128)(2,1)S(1)}, u32[]{:S(2)}, u32[]{:S(2)}) collective-permute-start(bf16[1024,128]{1,0:T(8,128)(2,1)} %get-tuple-element.46), channel_id=1, source_target_pairs={{0,32},{32,64},{64,96},{96,0},{1,33},{33,65},{65,97},{97,1},{2,34}... | collective-permute-start | bytes 786440 | tf_op jit(solution)/shard_map/pre_act_exchange/ppermute | solution.py:407
  116.3 12.4 %collective-permute-start.1 = (bf16[1024,128]{1,0:T(8,128)(2,1)S(1)}, bf16[1024,128]{1,0:T(8,128)(2,1)S(1)}, u32[]{:S(2)}, u32[]{:S(2)}) collective-permute-start(bf16[1024,128]{1,0:T(8,128)(2,1)S(1)} %add_convert_fusion.2), channel_id=1, source_target_pairs={{0,32},{32,64},{64,96},{96,0},{1,33},{33,65},{65,97},{97,1},{2,34}... | collective-permute-start | bytes 786440 | tf_op jit(solution)/shard_map/pre_act_exchange/ppermute | solution.py:407
  117.1 15.6 %collective-permute-start.5 = (bf16[1024,128]{1,0:T(8,128)(2,1)}, bf16[1024,128]{1,0:T(8,128)(2,1)S(1)}, u32[]{:S(2)}, u32[]{:S(2)}) collective-permute-start(bf16[1024,128]{1,0:T(8,128)(2,1)} %add_convert_fusion.1), channel_id=1, source_target_pairs={{0,96},{32,0},{64,32},{96,64},{1,97},{33,1},{65,33},{97,65},{2,98}... | collective-permute-start | bytes 786440 | tf_op jit(solution)/shard_map/pre_act_exchange/ppermute | solution.py:407
  128.7 1.0 copy-start.4
  129.6 5.3 %copy-start.2 = (bf16[512,2048]{1,0:T(8,128)(2,1)S(1)}, bf16[512,2048]{1,0:T(8,128)(2,1)}, u32[]{:S(2)}) copy-start(bf16[512,2048]{1,0:T(8,128)(2,1)} %copy-done.1) | copy-start | bytes 6291460
  130.0 7.3 %collective-permute-start.8 = (bf16[1024,128]{1,0:T(8,128)(2,1)S(1)}, bf16[1024,128]{1,0:T(8,128)(2,1)S(1)}, u32[]{:S(2)}, u32[]{:S(2)}) collective-permute-start(bf16[1024,128]{1,0:T(8,128)(2,1)S(1)} %get-tuple-element.51), channel_id=1, source_target_pairs={{0,32},{32,64},{64,96},{96,0},{1,33},{33,65},{65,97},{97,1},{2,34}... | collective-permute-start | bytes 786440 | tf_op jit(solution)/shard_map/slope_exchange/ppermute | solution.py:407
  130.1 13.9 %collective-permute-start.6 = (bf16[1024,128]{1,0:T(8,128)(2,1)S(1)}, bf16[1024,128]{1,0:T(8,128)(2,1)S(1)}, u32[]{:S(2)}, u32[]{:S(2)}) collective-permute-start(bf16[1024,128]{1,0:T(8,128)(2,1)S(1)} %get-tuple-element.51), channel_id=1, source_target_pairs={{0,96},{32,0},{64,32},{96,64},{1,97},{33,1},{65,33},{97,65},{2,98}... | collective-permute-start | bytes 786440 | tf_op jit(solution)/shard_map/slope_exchange/ppermute | solution.py:407
  133.1 8.0 %collective-permute-start.7 = (bf16[1024,128]{1,0:T(8,128)(2,1)S(1)}, bf16[1024,128]{1,0:T(8,128)(2,1)S(1)}, u32[]{:S(2)}, u32[]{:S(2)}) collective-permute-start(bf16[1024,128]{1,0:T(8,128)(2,1)S(1)} %get-tuple-element.52), channel_id=1, source_target_pairs={{0,96},{32,0},{64,32},{96,64},{1,97},{33,1},{65,33},{97,65},{2,98}... | collective-permute-start | bytes 786440 | tf_op jit(solution)/shard_map/slope_exchange/ppermute | solution.py:407
  133.2 10.8 %collective-permute-start.9 = (bf16[1024,128]{1,0:T(8,128)(2,1)S(1)}, bf16[1024,128]{1,0:T(8,128)(2,1)S(1)}, u32[]{:S(2)}, u32[]{:S(2)}) collective-permute-start(bf16[1024,128]{1,0:T(8,128)(2,1)S(1)} %get-tuple-element.52), channel_id=1, source_target_pairs={{0,32},{32,64},{64,96},{96,0},{1,33},{33,65},{65,97},{97,1},{2,34}... | collective-permute-start | bytes 786440 | tf_op jit(solution)/shard_map/slope_exchange/ppermute | solution.py:407
  134.9 1.6 copy-start.10
  137.3 10.8 %collective-permute-start.10 = (bf16[1024,128]{1,0:T(8,128)(2,1)S(1)}, bf16[1024,128]{1,0:T(8,128)(2,1)S(1)}, u32[]{:S(2)}, u32[]{:S(2)}) collective-permute-start(bf16[1024,128]{1,0:T(8,128)(2,1)S(1)} %collective-permute-done.8), channel_id=1, source_target_pairs={{0,32},{32,64},{64,96},{96,0},{1,33},{33,65},{65,97},{97,1},{2,34}... | collective-permute-start | bytes 786440 | tf_op jit(solution)/shard_map/slope_exchange/ppermute | solution.py:407
  141.1 7.1 %collective-permute-start.11 = (bf16[1024,128]{1,0:T(8,128)(2,1)S(1)}, bf16[1024,128]{1,0:T(8,128)(2,1)S(1)}, u32[]{:S(2)}, u32[]{:S(2)}) collective-permute-start(bf16[1024,128]{1,0:T(8,128)(2,1)S(1)} %collective-permute-done.7), channel_id=1, source_target_pairs={{0,96},{32,0},{64,32},{96,64},{1,97},{33,1},{65,33},{97,65},{2,98}... | collective-permute-start | bytes 786440 | tf_op jit(solution)/shard_map/slope_exchange/ppermute | solution.py:407
  149.0 5.7 %collective-permute-start.12 = (bf16[16,96,128]{2,1,0:T(8,128)(2,1)S(1)}, bf16[16,96,128]{2,1,0:T(8,128)(2,1)S(1)}, u32[]{:S(2)}, u32[]{:S(2)}) collective-permute-start(bf16[16,96,128]{2,1,0:T(8,128)(2,1)S(1)} %get-tuple-element.54), channel_id=1, source_target_pairs={{0,1},{1,0},{2,3},{3,2},{4,5},{5,4},{6,7},{7,6},{8,9},{9,8},{10,11... | collective-permute-start | bytes 1179656 | tf_op jit(solution)/shard_map/gradients/ppermute | solution.py:481
  155.6 16.6 %all-to-all-start.2 = ((bf16[16,96,128]{2,1,0:T(8,128)(2,1)}), bf16[16,96,128]{2,1,0:T(8,128)(2,1)S(1)}, u32[]{:S(2)}, u32[]{:S(2)}) async-start(bf16[16,96,128]{2,1,0:T(8,128)(2,1)} %add_convert_fusion), calls=%async_computation.2 | async-start | bytes 786432 | tf_op jit(solution)/shard_map/gradients/all_to_all | solution.py:484
  173.1 14.1 %all-to-all-start.3 = ((bf16[16,96,128]{2,1,0:T(8,128)(2,1)}), bf16[16,96,128]{2,1,0:T(8,128)(2,1)S(1)}, u32[]{:S(2)}, u32[]{:S(2)}) async-start(bf16[16,96,128]{2,1,0:T(8,128)(2,1)} %broadcast_in_dim.7), calls=%async_computation.3 | async-start | bytes 786432 | tf_op jit(solution)/shard_map/gradients/all_to_all | solution.py:484
  177.1 6.1 %collective-permute-start.13 = (bf16[512,128]{1,0:T(8,128)(2,1)S(1)}, bf16[512,128]{1,0:T(8,128)(2,1)S(1)}, u32[]{:S(2)}, u32[]{:S(2)}) collective-permute-start(bf16[512,128]{1,0:T(8,128)(2,1)S(1)} %get-tuple-element.67), channel_id=1, source_target_pairs={{0,32},{32,64},{64,96},{96,0},{1,33},{33,65},{65,97},{97,1},{2,34}... | collective-permute-start | bytes 393224 | tf_op jit(solution)/shard_map/second_layer/ppermute | solution.py:407
  177.2 9.3 %collective-permute-start.14 = (bf16[512,128]{1,0:T(8,128)(2,1)S(1)}, bf16[512,128]{1,0:T(8,128)(2,1)S(1)}, u32[]{:S(2)}, u32[]{:S(2)}) collective-permute-start(bf16[512,128]{1,0:T(8,128)(2,1)S(1)} %get-tuple-element.66), channel_id=1, source_target_pairs={{0,64},{32,96},{64,0},{96,32},{1,65},{33,97},{65,1},{97,33},{2,66}... | collective-permute-start | bytes 393224 | tf_op jit(solution)/shard_map/second_layer/ppermute | solution.py:407
  181.7 5.5 %collective-permute-start.15 = (bf16[512,128]{1,0:T(8,128)(2,1)S(1)}, bf16[512,128]{1,0:T(8,128)(2,1)S(1)}, u32[]{:S(2)}, u32[]{:S(2)}) collective-permute-start(bf16[512,128]{1,0:T(8,128)(2,1)S(1)} %get-tuple-element.65), channel_id=1, source_target_pairs={{0,96},{32,0},{64,32},{96,64},{1,97},{33,1},{65,33},{97,65},{2,98}... | collective-permute-start | bytes 393224 | tf_op jit(solution)/shard_map/second_layer/ppermute | solution.py:407
  187.2 3.2 %collective-permute-start.16 = (bf16[16,96,128]{2,1,0:T(8,128)(2,1)S(1)}, bf16[16,96,128]{2,1,0:T(8,128)(2,1)S(1)}, u32[]{:S(2)}, u32[]{:S(2)}) collective-permute-start(bf16[16,96,128]{2,1,0:T(8,128)(2,1)S(1)} %all-to-all-done.3.mine_ref), channel_id=1, source_target_pairs={{0,1},{1,0},{2,3},{3,2},{4,5},{5,4},{6,7},{7,6},{8,9},{9,8},{10,11... | collective-permute-start | bytes 1179656 | tf_op jit(solution)/shard_map/gradients/ppermute | solution.py:481

commit v5 on v4

--- a/solution.py
+++ b/solution.py
@@ -162,10 +162,12 @@
 
 
 def widen(held, low, high, copies):
-    rows = held.shape[0] // len(copies)
+    pieces = max(1, len(copies))
+    rows = held.shape[0] // pieces
     half = low.shape[1]
-    for p, copy in enumerate(copies):
-        copy.wait()
+    for p in range(pieces):
+        if copies:
+            copies[p].wait()
 
         def some(i, carry):
             part = pl.ds(pl.multiple_of(p * rows + i * 128, 128), 128)
@@ -176,16 +178,18 @@
         lax.fori_loop(0, rows // 128, some, 0, unroll=2)
 
 
-def gather_kernel(idx_ref, table_ref, out_ref, held, low, high, sems):
+def gather_kernel(idx_hbm, table_ref, out_ref, idx_ref, held, low, high, sems, idx_sem):
     step = pl.program_id(0)
     rows = out_ref.shape[0]
 
     @pl.when(step == 0)
     def _():
         copies = piece_copies(table_ref, held, sems)
-        for copy in copies:
+        idx_copy = pltpu.make_async_copy(idx_hbm, idx_ref, idx_sem)
+        for copy in [idx_copy] + copies:
             copy.start()
         widen(held, low, high, copies)
+        idx_copy.wait()
 
     pick_rows(idx_ref, step * rows, rows, low, high, out_ref)
 
@@ -195,18 +199,17 @@
     own_rows, width = table.shape
     return pl.pallas_call(
         gather_kernel,
-        grid_spec=pltpu.PrefetchScalarGridSpec(
-            num_scalar_prefetch=1,
-            grid=(total // rows,),
-            in_specs=[pl.BlockSpec(memory_space=pltpu.HBM)],
-            out_specs=pl.BlockSpec((rows, width), lambda i, s: (i, 0)),
-            scratch_shapes=[
-                pltpu.VMEM((own_rows, width), BF),
-                pltpu.VMEM((own_rows, width // 2), F32),
-                pltpu.VMEM((own_rows, width // 2), F32),
-                pltpu.SemaphoreType.DMA((8,)),
-            ],
-        ),
+        grid=(total // rows,),
+        in_specs=[pl.BlockSpec(memory_space=pltpu.HBM)] * 2,
+        out_specs=pl.BlockSpec((rows, width), lambda i: (i, 0)),
+        scratch_shapes=[
+            pltpu.SMEM((total,), jnp.int32),
+            pltpu.VMEM((own_rows, width), BF),
+            pltpu.VMEM((own_rows, width // 2), F32),
+            pltpu.VMEM((own_rows, width // 2), F32),
+            pltpu.SemaphoreType.DMA((8,)),
+            pltpu.SemaphoreType.DMA,
+        ],
         out_shape=pltpu.HBM((total, width), BF),
         compiler_params=pltpu.CompilerParams(vmem_limit_bytes=62 << 20),
         name="gather_rows",
@@ -215,10 +218,10 @@
 
 def layer_kernel(list_width, idx_ref, spot_ref, arrived_ref, counts_ref, ws_ref, wn_ref,
                  *refs):
-    part_refs, (both_ref, held, low, high, frontier, counts, sems, count_sems) = refs[:-8], refs[-8:]
+    part_refs, (both_ref, low, high, frontier, counts, count_sems) = refs[:-6], refs[-6:]
     step = pl.program_id(0)
     block = both_ref.shape[0]
-    width = held.shape[1]
+    width = arrived_ref.shape[1]
 
     def count_copy(b):
         return pltpu.make_async_copy(
@@ -229,12 +232,9 @@
 
     @pl.when(step == 0)
     def _():
-        copies = piece_copies(arrived_ref, held, sems)
-        for copy in copies:
-            copy.start()
         for b in range(counts.shape[0] // block):
             count_copy(b).start()
-        widen(held, low, high, copies)
+        widen(arrived_ref, low, high, [])
         pick_rows(idx_ref, 0, frontier.shape[0], low, high, frontier)
 
     count_copy(step).wait()
@@ -277,55 +277,66 @@
             num_scalar_prefetch=2,
             grid=(steps,),
             in_specs=[
-                pl.BlockSpec(memory_space=pltpu.HBM),
+                pl.BlockSpec(memory_space=pltpu.VMEM),
                 pl.BlockSpec(memory_space=pltpu.HBM),
                 full(w_self.shape),
                 full(w_near.shape),
             ],
             out_specs=halves * quarters + [pl.BlockSpec((block, 2 * width), lambda i, *s: (i, 0))],
             scratch_shapes=[
-                pltpu.VMEM((slots, width), BF),
                 pltpu.VMEM((slots, width // 2), F32),
                 pltpu.VMEM((slots, width // 2), F32),
                 pltpu.VMEM((positions, width), BF),
                 pltpu.VMEM((targets, positions), BF),
-                pltpu.SemaphoreType.DMA((8,)),
                 pltpu.SemaphoreType.DMA((steps,)),
             ],
         ),
         out_shape=[jax.ShapeDtypeStruct((targets // 2, share), BF)] * 2
         + [pltpu.VMEM((targets // 2, share), BF)] * (2 * quarters - 2)
         + [jax.ShapeDtypeStruct((targets, 2 * width), BF)],
-        compiler_params=pltpu.CompilerParams(vmem_limit_bytes=60 << 20),
+        compiler_params=pltpu.CompilerParams(vmem_limit_bytes=54 << 20),
         name="first_layer",
     )(idx, spot, arrived, counts, w_self, w_near)
 
 
-def slope_kernel(part0, up, down, bias_ref, d_ref, hidden_ref, slope_ref):
-    active = part0[...].astype(F32) + up[...].astype(F32) + down[...].astype(F32)
-    active = active + bias_ref[...].astype(F32)
+def add_kernel(left, right, out_ref):
+    out_ref[...] = (left[...].astype(F32) + right[...].astype(F32)).astype(BF)
+
+
+def added(left, right):
+    return pl.pallas_call(
+        add_kernel,
+        in_specs=[pl.BlockSpec(memory_space=pltpu.VMEM)] * 2,
+        out_specs=pl.BlockSpec(memory_space=pltpu.VMEM),
+        out_shape=jax.ShapeDtypeStruct(left.shape, BF),
+        compiler_params=pltpu.CompilerParams(vmem_limit_bytes=16 << 20),
+        name="added",
+    )(left, right)
+
+
+def slope_kernel(base, up, down, d_ref, hidden_ref, slope_ref):
+    active = base[...] + up[...].astype(F32) + down[...].astype(F32)
     below = 1.0 + jnp.exp(-active)
     sigmoid = 1.0 / below
     hidden_ref[...] = (active / below).astype(BF)
     slope_ref[...] = (d_ref[...] * (sigmoid * (1.0 + active * (1.0 - sigmoid)))).astype(BF)
 
 
-def hidden_and_slope(part0, up, down, bias, d_hidden, first, block=512):
-    rows, share = part0.shape
+def hidden_and_slope(base, up, down, d_hidden, first, block=512):
+    rows, share = base.shape
     place = pl.BlockSpec((block, share), lambda i: (i, 0))
     return pl.pallas_call(
         slope_kernel,
         grid=(rows // block,),
         in_specs=[place] * 3
         + [
-            pl.BlockSpec((1, share), lambda i: (0, 0)),
             pl.BlockSpec((block, share), lambda i: (i + first // block, 0)),
         ],
         out_specs=[place, place],
         out_shape=[jax.ShapeDtypeStruct((rows, share), BF)] * 2,
         compiler_params=pltpu.CompilerParams(vmem_limit_bytes=16 << 20),
         name="hidden_and_slope",
-    )(part0, up, down, bias, d_hidden)
+    )(base, up, down, d_hidden)
 
 
 def pack_kernel(core_ref, *refs):
@@ -377,6 +388,41 @@
             cols = slice((2 * half + e) * share, (2 * half + e + 1) * share)
             vs_ref[:, cols] = block[2 * e * share:(2 * e + 1) * share]
             vn_ref[:, cols] = block[(2 * e + 1) * share:(2 * e + 2) * share]
+
+
+def join_kernel(keep, got, keep_far, got_far, out_ref):
+    rows = keep.shape[1]
+    out_ref[:, :rows, :] = (keep[...].astype(F32) + got[...].astype(F32)).astype(BF)
+    out_ref[:, rows:, :] = (keep_far[...].astype(F32) + got_far[...].astype(F32)).astype(BF)
+
+
+def joined(keep, got, keep_far, got_far):
+    chips, rows, share = keep.shape
+    return pl.pallas_call(
+        join_kernel,
+        in_specs=[pl.BlockSpec(memory_space=pltpu.VMEM)] * 4,
+        out_specs=pl.BlockSpec(memory_space=pltpu.VMEM),
+        out_shape=jax.ShapeDtypeStruct((chips, rows + keep_far.shape[1], share), BF),
+        compiler_params=pltpu.CompilerParams(vmem_limit_bytes=16 << 20),
+        name="joined",
+    )(keep, got, keep_far, got_far)
+
+
+def spread_kernel(got_ref, out_ref):
+    total = jnp.sum(got_ref[...].astype(F32), axis=0).astype(BF)
+    for chip in range(out_ref.shape[0]):
+        out_ref[chip] = total
+
+
+def sum_and_spread(got):
+    return pl.pallas_call(
+        spread_kernel,
+        in_specs=[pl.BlockSpec(memory_space=pltpu.VMEM)],
+        out_specs=pl.BlockSpec(memory_space=pltpu.VMEM),
+        out_shape=jax.ShapeDtypeStruct(got.shape, BF),
+        compiler_params=pltpu.CompilerParams(vmem_limit_bytes=16 << 20),
+        name="sum_and_spread",
+    )(got)
 
 
 def body(
@@ -450,9 +496,6 @@
             first_width,
             quarters,
         )
-    def added(left, right):
-        return (left.astype(F32) + right.astype(F32)).astype(BF)
-
     with jax.named_scope("pre_act_exchange"):
         own, above, far, below = [parts[2 * d:2 * d + 2] for d in range(quarters)]
         passing_up = shift(far[0], 1)
@@ -463,9 +506,8 @@
         down_1 = shift(added(below[1], passing_down), -1)
         hiddens, slopes = [], []
         for half, (up, down) in enumerate([(up_0, down_0), (up_1, down_1)]):
-            hidden, slope = hidden_and_slope(
-                own[half], up, down, bias_hidden.reshape(1, share), d_hidden, half * targets // 2
-            )
+            base = own[half].astype(F32) + bias_hidden.astype(F32)
+            hidden, slope = hidden_and_slope(base, up, down, d_hidden, half * targets // 2)
             hiddens.append(hidden)
             slopes.append(slope)
     with jax.named_scope("slope_exchange"):
@@ -514,12 +556,13 @@
     with jax.named_scope("gradients"):
         near_two = grad_w(jnp.concatenate([from_up, from_down], axis=1))
         chips = peers // 2
+        near_two, outs[0] = lax.optimization_barrier((near_two, outs[0]))
         keep, give = pack_shards(
-            core.reshape(1), [grad_v, grad_w(jnp.concatenate(slopes)), near_two, grad_w(from_far)], chips, share
-        )
-        sums = between_chips(added(keep, swap(give)))
-        sums = jnp.sum(sums.astype(F32), axis=0).astype(BF)
-        mine = between_chips(jnp.broadcast_to(sums, (chips, *sums.shape)))
+            core.reshape(1), [grad_v, grad_w(jnp.concatenate(slopes)), near_two], chips, share
+        )
+        keep_far, give_far = pack_shards(core.reshape(1), [grad_w(from_far)], chips, share)
+        sums = between_chips(joined(keep, swap(give), keep_far, swap(give_far)))
+        mine = between_chips(sum_and_spread(sums))
         mine, *outs = lax.optimization_barrier((mine, *outs))
         other = swap(mine)
         seed_out = out_part(0)

time: 193 us -> 188 us (0.974)
  blocking collectives: 16 us -> 31.1 us
  waiting for transfers between devices: 65.8 us -> 52 us
  starting transfers between devices: 42 us -> 38.8 us
    all_to_all x0 -> x1, blocking collectives: none -> 15.2 us  [between_chips(): lax.all_to_all(value, 'wide', split_axis=0, concat_axis=0, axis_index_gro...]
    all_to_all x2 -> x1, waiting for transfers between devices: 9.16 us -> 0.21 us  [between_chips(): lax.all_to_all(value, 'wide', split_axis=0, concat_axis=0, axis_index_gro...]
    all_to_all x2 -> x1, starting transfers between devices: 10.7 us -> 3.55 us  [between_chips(): lax.all_to_all(value, 'wide', split_axis=0, concat_axis=0, axis_index_gro...]
    ppermute x2 -> x3, starting transfers between devices: 6.21 us -> 11.7 us  [swap(): return lax.ppermute(value, 'wide', [(i, i ^ 1) for i in range(peers)])]
    ppermute x15, waiting for transfers between devices: 23.6 us -> 19.2 us  [shift(): lax.ppermute(value, 'blk', [(i, (i + by) % quarters) for i in range(quart...]
    pallas_call x1 -> x5, Pallas kernels: 14.7 us -> 14.6 us  [the longest x1 13.5 us: gather_rows(): pl.pallas_call(gather_kernel, grid=(total // rows,), in_specs=[pl.BlockSp...]
  transfers between devices with their start and end apart: 20 -> 20, of which waited for: 12 -> 10; matrix products, arithmetic and copies ran while one was open for 4% -> 5% of each run, Pallas kernels for 9% -> 9%
where the time goes in v5:
time: 188 us
  Pallas kernels  54.1 us (29%)
  waiting for transfers between devices  52 us (28%)
  starting transfers between devices  38.8 us (21%)
  blocking collectives  31.1 us (17%)
  matrix products  5.52 us (3%)
  local copies, waits for them, and re-layouts  3.1 us (2%)
  other arithmetic  2.07 us (1%)
    all_to_all x1, waiting for transfers between devices, exchange(): lax.all_to_all(value, 'wide', split_axis=0, concat_axis=0, tiled=True)  31.1 us
    ppermute x15, waiting for transfers between devices, shift(): lax.ppermute(value, 'blk', [(i, (i + by) % quarters) for i in range(quart...  19.2 us
    ppermute x15, starting transfers between devices, shift(): lax.ppermute(value, 'blk', [(i, (i + by) % quarters) for i in range(quart...  18.6 us
    pallas_call x1, Pallas kernels, first_layer(): pl.pallas_call(functools.partial(layer_kernel, list_width), grid_spec=plt...  18.4 us
    all_to_all x1, blocking collectives, exchange(): lax.all_to_all(value, 'wide', split_axis=0, concat_axis=0, tiled=True)  16 us
    pallas_call x2, Pallas kernels, neighbour_counts(): pl.pallas_call(count_kernel, grid=(targets // 16 // block_groups,), in_sp...  15.7 us
    all_to_all x1, blocking collectives, between_chips(): lax.all_to_all(value, 'wide', split_axis=0, concat_axis=0, axis_index_gro...  15.2 us
    pallas_call x1, Pallas kernels, gather_rows(): pl.pallas_call(gather_kernel, grid=(total // rows,), in_specs=[pl.BlockSp...  13.5 us
  transfers between devices with their start and end apart: 20, of which 10 were waited for; matrix products, arithmetic and copies ran while one was open for 5% of the time, Pallas kernels for 9%

profile of v5, /device:TPU:1, one launch (start us, length us, event | category | flops | bytes accessed | tf_op | source)
XLA Modules:
  0.0 187.8 jit_solution(5660978335820171343)
XLA Ops:
  0.6 2.9 %request_table.1 = (s32[32,1,256]{2,1,0:T(1,128)}, s32[32,128]{1,0:T(8,128)}) custom-call(s32[32,128]{1,0:T(8,128)} %bitcast.25, s32[32,128]{1,0:T(8,128)} %bitcast.26), custom_call_target="tpu_custom_call" | custom-call | tf_op jit(solution)/shard_map/requests/request_table/pallas_call | solution.py:66
  3.6 16.0 %all_to_all.20 = s32[32,1,256]{2,1,0:T(1,128)} all-to-all(s32[32,1,256]{2,1,0:T(1,128)} %get-tuple-element.39), channel_id=1, replica_groups=mesh['blk'=4,'wide'=32] {'wide'}, dimensions={0} | all-to-all | bytes 65536 | tf_op jit(solution)/shard_map/requests/all_to_all | solution.py:456
  19.5 13.5 %gather_rows.1 = bf16[8192,256]{1,0:T(8,128)(2,1)} custom-call(s32[8192]{0:T(1024)} %bitcast.24, bf16[8192,256]{1,0:T(8,128)(2,1)} %table_ref.1), custom_call_target="tpu_custom_call" | custom-call | tf_op jit(solution)/shard_map/rows/gather_rows/pallas_call | solution.py:200
  33.1 5.0 %all-to-all-start.1 = ((bf16[32,256,256]{2,1,0:T(8,128)(2,1)}), bf16[32,256,256]{2,1,0:T(8,128)(2,1)}, u32[]{:S(2)}, u32[]{:S(2)}) async-start(bf16[32,256,256]{2,1,0:T(8,128)(2,1)} %bitcast.23), calls=%async_computation.1 | async-start | bytes 8388608 | tf_op jit(solution)/shard_map/rows/all_to_all | solution.py:456
  39.3 2.6 %neighbour_counts.3 = bf16[512,2048]{1,0:T(8,128)(2,1)S(1)} custom-call(s32[32,256]{1,0:T(8,128)S(1)} %reshape.46.idx_ref), custom_call_target="tpu_custom_call" | custom-call | flops 536870912 | bytes 2097152 | tf_op jit(solution)/shard_map/beside_rows/neighbour_counts/pallas_call | solution.py:112
  44.1 13.1 %neighbour_counts.2.counts_ref = bf16[2048,4096]{1,0:T(8,128)(2,1)} custom-call(s32[128,256]{1,0:T(8,128)S(1)} %reshape.45.idx_ref), custom_call_target="tpu_custom_call" | custom-call | flops 4294967296 | bytes 16777216 | tf_op jit(solution)/shard_map/beside_rows/neighbour_counts/pallas_call | solution.py:112
  57.3 31.1 %all-to-all-done.1 = bf16[32,256,256]{2,1,0:T(8,128)(2,1)} async-done(((bf16[32,256,256]{2,1,0:T(8,128)(2,1)}), bf16[32,256,256]{2,1,0:T(8,128)(2,1)}, u32[]{:S(2)}, u32[]{:S(2)}) %all-to-all-start.1) | async-done | bytes 4194336 | tf_op jit(solution)/shard_map/rows/all_to_all | solution.py:456
  88.4 18.4 %first_layer.1 = (bf16[1024,128]{1,0:T(8,128)(2,1)}, bf16[1024,128]{1,0:T(8,128)(2,1)}, bf16[1024,128]{1,0:T(8,128)(2,1)S(1)}, bf16[1024,128]{1,0:T(8,128)(2,1)S...) custom-call(s32[4096]{0:T(1024)} %bitcast.27, ...), custom_call_target="tpu_custom_call" | custom-call | tf_op jit(solution)/shard_map/first_layer/first_layer/pallas_call | solution.py:274
  106.9 1.7 collective-permute-start
  108.6 2.2 %collective-permute-start.4 = (bf16[1024,128]{1,0:T(8,128)(2,1)}, bf16[1024,128]{1,0:T(8,128)(2,1)S(1)}, u32[]{:S(2)}, u32[]{:S(2)}) collective-permute-start(bf16[1024,128]{1,0:T(8,128)(2,1)} %get-tuple-element.52), channel_id=1, source_target_pairs={{0,96},{32,0},{64,32},{96,64},{1,97},{33,1},{65,33},{97,65},{2,98}... | collective-permute-start | bytes 786440 | tf_op jit(solution)/shard_map/pre_act_exchange/ppermute | solution.py:453
  110.8 1.4 collective-permute-start.2
  112.2 2.4 %collective-permute-done.right = bf16[1024,128]{1,0:T(8,128)(2,1)S(1)} collective-permute-done((bf16[1024,128]{1,0:T(8,128)(2,1)}, bf16[1024,128]{1,0:T(8,128)(2,1)S(1)}, u32[]{:S(2)}, u32[]{:S(2)}) %collective-permute-start) | collective-permute-done | bytes 262176 | tf_op jit(solution)/shard_map/pre_act_exchange/ppermute | solution.py:453
  114.9 2.7 %collective-permute-start.5 = (bf16[1024,128]{1,0:T(8,128)(2,1)S(1)}, bf16[1024,128]{1,0:T(8,128)(2,1)S(1)}, u32[]{:S(2)}, u32[]{:S(2)}) collective-permute-start(bf16[1024,128]{1,0:T(8,128)(2,1)S(1)} %added.3), channel_id=1, source_target_pairs={{0,96},{32,0},{64,32},{96,64},{1,97},{33,1},{65,33},{97,65},{2,98}... | collective-permute-start | bytes 786440 | tf_op jit(solution)/shard_map/pre_act_exchange/ppermute | solution.py:453
  117.6 1.1 convert_add_fusion.1
  118.7 8.6 %collective-permute-done.1.up = bf16[1024,128]{1,0:T(8,128)(2,1)S(1)} collective-permute-done((bf16[1024,128]{1,0:T(8,128)(2,1)S(1)}, bf16[1024,128]{1,0:T(8,128)(2,1)S(1)}, u32[]{:S(2)}, u32[]{:S(2)}) %collective-permute-start.1) | collective-permute-done | bytes 262176 | tf_op jit(solution)/shard_map/pre_act_exchange/ppermute | solution.py:453
  127.9 2.7 %collective-permute-start.6 = (bf16[1024,128]{1,0:T(8,128)(2,1)S(1)}, bf16[1024,128]{1,0:T(8,128)(2,1)S(1)}, u32[]{:S(2)}, u32[]{:S(2)}) collective-permute-start(bf16[1024,128]{1,0:T(8,128)(2,1)S(1)} %get-tuple-element.55), channel_id=1, source_target_pairs={{0,96},{32,0},{64,32},{96,64},{1,97},{33,1},{65,33},{97,65},{2,98}... | collective-permute-start | bytes 786440 | tf_op jit(solution)/shard_map/slope_exchange/ppermute | solution.py:453
  131.0 1.4 collective-permute-start.9
  132.4 0.8 fusion
  134.7 1.0 copy-done.7
  136.5 2.4 %collective-permute-done.7 = bf16[1024,128]{1,0:T(8,128)(2,1)S(1)} collective-permute-done((bf16[1024,128]{1,0:T(8,128)(2,1)S(1)}, bf16[1024,128]{1,0:T(8,128)(2,1)S(1)}, u32[]{:S(2)}, u32[]{:S(2)}) %collective-permute-start.7) | collective-permute-done | bytes 262176 | tf_op jit(solution)/shard_map/slope_exchange/ppermute | solution.py:453
  138.9 3.0 %collective-permute-start.13 = (bf16[1024,128]{1,0:T(8,128)(2,1)S(1)}, bf16[1024,128]{1,0:T(8,128)(2,1)S(1)}, u32[]{:S(2)}, u32[]{:S(2)}) collective-permute-start(bf16[1024,128]{1,0:T(8,128)(2,1)S(1)} %collective-permute-done.7), channel_id=1, source_target_pairs={{0,96},{32,0},{64,32},{96,64},{1,97},{33,1},{65,33},{97,65},{2,98}... | collective-permute-start | bytes 786440 | tf_op jit(solution)/shard_map/slope_exchange/ppermute | solution.py:453
  143.2 6.4 %collective-permute-start.11 = (bf16[16,80,128]{2,1,0:T(8,128)(2,1)S(1)}, bf16[16,80,128]{2,1,0:T(8,128)(2,1)S(1)}, u32[]{:S(2)}, u32[]{:S(2)}) collective-permute-start(bf16[16,80,128]{2,1,0:T(8,128)(2,1)S(1)} %get-tuple-element.59), channel_id=1, source_target_pairs={{0,1},{1,0},{2,3},{3,2},{4,5},{5,4},{6,7},{7,6},{8,9},{9,8},{10,11... | collective-permute-start | bytes 983048 | tf_op jit(solution)/shard_map/gradients/ppermute | solution.py:523
  150.3 2.7 %collective-permute-start.14 = (bf16[16,16,128]{2,1,0:T(8,128)(2,1)S(1)}, bf16[16,16,128]{2,1,0:T(8,128)(2,1)S(1)}, u32[]{:S(2)}, u32[]{:S(2)}) collective-permute-start(bf16[16,16,128]{2,1,0:T(8,128)(2,1)S(1)} %get-tuple-element.61), channel_id=1, source_target_pairs={{0,1},{1,0},{2,3},{3,2},{4,5},{5,4},{6,7},{7,6},{8,9},{9,8},{10,11... | collective-permute-start | bytes 196616 | tf_op jit(solution)/shard_map/gradients/ppermute | solution.py:523
  153.1 0.9 collective-permute-done.14.got_far
  154.1 15.2 %all_to_all.21.got_ref = bf16[16,96,128]{2,1,0:T(8,128)(2,1)S(1)} all-to-all(bf16[16,96,128]{2,1,0:T(8,128)(2,1)S(1)} %joined.1), channel_id=1, replica_groups={{0,2,4,6,8,10,12,14,16,18,20,22,24,26,28,30},{1,3,5,7,9,11,13,15,17,19,..., dimensions={0} | all-to-all | bytes 786432 | tf_op jit(solution)/shard_map/gradients/all_to_all | solution.py:526
  170.1 3.6 %all-to-all-start.3 = ((bf16[16,96,128]{2,1,0:T(8,128)(2,1)}), bf16[16,96,128]{2,1,0:T(8,128)(2,1)S(1)}, u32[]{:S(2)}, u32[]{:S(2)}) async-start(bf16[16,96,128]{2,1,0:T(8,128)(2,1)} %sum_and_spread.1), calls=%async_computation.3 | async-start | bytes 786432 | tf_op jit(solution)/shard_map/gradients/all_to_all | solution.py:526
  173.6 1.2 collective-permute-start.15
  174.8 1.6 collective-permute-start.16
  176.4 2.6 %collective-permute-done.15 = bf16[512,128]{1,0:T(8,128)(2,1)S(1)} collective-permute-done((bf16[512,128]{1,0:T(8,128)(2,1)S(1)}, bf16[512,128]{1,0:T(8,128)(2,1)S(1)}, u32[]{:S(2)}, u32[]{:S(2)}) %collective-permute-start.15) | collective-permute-done | bytes 131104 | tf_op jit(solution)/shard_map/second_layer/ppermute | solution.py:453
  179.0 2.8 %collective-permute-done.16 = bf16[512,128]{1,0:T(8,128)(2,1)S(1)} collective-permute-done((bf16[512,128]{1,0:T(8,128)(2,1)S(1)}, bf16[512,128]{1,0:T(8,128)(2,1)S(1)}, u32[]{:S(2)}, u32[]{:S(2)}) %collective-permute-start.16) | collective-permute-done | bytes 131104 | tf_op jit(solution)/shard_map/second_layer/ppermute | solution.py:453
  182.0 2.6 %collective-permute-start.17 = (bf16[16,96,128]{2,1,0:T(8,128)(2,1)S(1)}, bf16[16,96,128]{2,1,0:T(8,128)(2,1)S(1)}, u32[]{:S(2)}, u32[]{:S(2)}) collective-permute-start(bf16[16,96,128]{2,1,0:T(8,128)(2,1)S(1)} %all-to-all-done.3.mine_ref), channel_id=1, source_target_pairs={{0,1},{1,0},{2,3},{3,2},{4,5},{5,4},{6,7},{7,6},{8,9},{9,8},{10,11... | collective-permute-start | bytes 1179656 | tf_op jit(solution)/shard_map/gradients/ppermute | solution.py:523
  186.0 1.8 finish.1
  (67 shorter events, 11.3 us)
Async XLA Ops:
  0.6 41.3 %copy-start = (bf16[512,512]{1,0:T(8,128)(2,1)S(1)}, bf16[512,512]{1,0:T(8,128)(2,1)}, u32[]{:S(2)}) copy-start(bf16[512,512]{1,0:T(8,128)(2,1)} %param.21) | copy-start | bytes 1572868
  33.1 5.0 %copy-start.6 = (s32[512,10]{0,1:T(8,128)S(1)}, s32[512,10]{0,1:T(8,128)}, u32[]{:S(2)}) copy-start(s32[512,10]{0,1:T(8,128)} %param.15) | copy-start | bytes 61444
  33.1 5.3 %copy-start.5 = (s32[2048,15]{0,1:T(8,128)S(1)}, s32[2048,15]{0,1:T(8,128)}, u32[]{:S(2)}) copy-start(s32[2048,15]{0,1:T(8,128)} %param.14) | copy-start | bytes 368644
  33.1 55.4 %all-to-all-start.1 = ((bf16[32,256,256]{2,1,0:T(8,128)(2,1)}), bf16[32,256,256]{2,1,0:T(8,128)(2,1)}, u32[]{:S(2)}, u32[]{:S(2)}) async-start(bf16[32,256,256]{2,1,0:T(8,128)(2,1)} %bitcast.23), calls=%async_computation.1 | async-start | bytes 8388608 | tf_op jit(solution)/shard_map/rows/all_to_all | solution.py:456
  38.9 3.1 %copy-start.3 = (bf16[128,512]{1,0:T(8,128)(2,1)S(1)}, bf16[128,512]{1,0:T(8,128)(2,1)}, u32[]{:S(2)}) copy-start(bf16[128,512]{1,0:T(8,128)(2,1)} %param.20) | copy-start | bytes 393220
  38.9 3.4 %copy-start.4 = (bf16[128,512]{1,0:T(8,128)(2,1)S(1)}, bf16[128,512]{1,0:T(8,128)(2,1)}, u32[]{:S(2)}) copy-start(bf16[128,512]{1,0:T(8,128)(2,1)} %param.19) | copy-start | bytes 393220
  42.0 1.4 copy-start.1
  88.4 22.3 %copy-start.8 = (bf16[128]{0:T(256)(128)(2,1)S(1)}, bf16[128]{0:T(256)(128)(2,1)}, u32[]{:S(2)}) copy-start(bf16[128]{0:T(256)(128)(2,1)} %param.18) | copy-start | bytes 772
  106.9 7.8 %collective-permute-start = (bf16[1024,128]{1,0:T(8,128)(2,1)}, bf16[1024,128]{1,0:T(8,128)(2,1)S(1)}, u32[]{:S(2)}, u32[]{:S(2)}) collective-permute-start(bf16[1024,128]{1,0:T(8,128)(2,1)} %get-tuple-element.44), channel_id=1, source_target_pairs={{0,32},{32,64},{64,96},{96,0},{1,33},{33,65},{65,97},{97,1},{2,34}... | collective-permute-start | bytes 786440 | tf_op jit(solution)/shard_map/pre_act_exchange/ppermute | solution.py:453
  108.6 6.2 %collective-permute-start.4 = (bf16[1024,128]{1,0:T(8,128)(2,1)}, bf16[1024,128]{1,0:T(8,128)(2,1)S(1)}, u32[]{:S(2)}, u32[]{:S(2)}) collective-permute-start(bf16[1024,128]{1,0:T(8,128)(2,1)} %get-tuple-element.52), channel_id=1, source_target_pairs={{0,96},{32,0},{64,32},{96,64},{1,97},{33,1},{65,33},{97,65},{2,98}... | collective-permute-start | bytes 786440 | tf_op jit(solution)/shard_map/pre_act_exchange/ppermute | solution.py:453
  110.8 8.0 %collective-permute-start.2 = (bf16[1024,128]{1,0:T(8,128)(2,1)S(1)}, bf16[1024,128]{1,0:T(8,128)(2,1)S(1)}, u32[]{:S(2)}, u32[]{:S(2)}) collective-permute-start(bf16[1024,128]{1,0:T(8,128)(2,1)S(1)} %get-tuple-element.45), channel_id=1, source_target_pairs={{0,96},{32,0},{64,32},{96,64},{1,97},{33,1},{65,33},{97,65},{2,98}... | collective-permute-start | bytes 786440 | tf_op jit(solution)/shard_map/pre_act_exchange/ppermute | solution.py:453
  112.2 18.4 %collective-permute-start.3 = (bf16[1024,128]{1,0:T(8,128)(2,1)S(1)}, bf16[1024,128]{1,0:T(8,128)(2,1)S(1)}, u32[]{:S(2)}, u32[]{:S(2)}) collective-permute-start(bf16[1024,128]{1,0:T(8,128)(2,1)S(1)} %get-tuple-element.50), channel_id=1, source_target_pairs={{0,32},{32,64},{64,96},{96,0},{1,33},{33,65},{65,97},{97,1},{2,34}... | collective-permute-start | bytes 786440 | tf_op jit(solution)/shard_map/pre_act_exchange/ppermute | solution.py:453
  114.7 12.6 %collective-permute-start.1 = (bf16[1024,128]{1,0:T(8,128)(2,1)S(1)}, bf16[1024,128]{1,0:T(8,128)(2,1)S(1)}, u32[]{:S(2)}, u32[]{:S(2)}) collective-permute-start(bf16[1024,128]{1,0:T(8,128)(2,1)S(1)} %added.2), channel_id=1, source_target_pairs={{0,32},{32,64},{64,96},{96,0},{1,33},{33,65},{65,97},{97,1},{2,34}... | collective-permute-start | bytes 786440 | tf_op jit(solution)/shard_map/pre_act_exchange/ppermute | solution.py:453
  114.9 15.7 %collective-permute-start.5 = (bf16[1024,128]{1,0:T(8,128)(2,1)S(1)}, bf16[1024,128]{1,0:T(8,128)(2,1)S(1)}, u32[]{:S(2)}, u32[]{:S(2)}) collective-permute-start(bf16[1024,128]{1,0:T(8,128)(2,1)S(1)} %added.3), channel_id=1, source_target_pairs={{0,96},{32,0},{64,32},{96,64},{1,97},{33,1},{65,33},{97,65},{2,98}... | collective-permute-start | bytes 786440 | tf_op jit(solution)/shard_map/pre_act_exchange/ppermute | solution.py:453
  127.3 5.1 %copy-start.2 = (bf16[512,2048]{1,0:T(8,128)(2,1)S(1)}, bf16[512,2048]{1,0:T(8,128)(2,1)}, u32[]{:S(2)}) copy-start(bf16[512,2048]{1,0:T(8,128)(2,1)} %copy-done.1) | copy-start | bytes 6291460
  127.6 8.8 %collective-permute-start.8 = (bf16[1024,128]{1,0:T(8,128)(2,1)S(1)}, bf16[1024,128]{1,0:T(8,128)(2,1)S(1)}, u32[]{:S(2)}, u32[]{:S(2)}) collective-permute-start(bf16[1024,128]{1,0:T(8,128)(2,1)S(1)} %get-tuple-element.55), channel_id=1, source_target_pairs={{0,32},{32,64},{64,96},{96,0},{1,33},{33,65},{65,97},{97,1},{2,34}... | collective-permute-start | bytes 786440 | tf_op jit(solution)/shard_map/slope_exchange/ppermute | solution.py:453
  127.9 14.1 %collective-permute-start.6 = (bf16[1024,128]{1,0:T(8,128)(2,1)S(1)}, bf16[1024,128]{1,0:T(8,128)(2,1)S(1)}, u32[]{:S(2)}, u32[]{:S(2)}) collective-permute-start(bf16[1024,128]{1,0:T(8,128)(2,1)S(1)} %get-tuple-element.55), channel_id=1, source_target_pairs={{0,96},{32,0},{64,32},{96,64},{1,97},{33,1},{65,33},{97,65},{2,98}... | collective-permute-start | bytes 786440 | tf_op jit(solution)/shard_map/slope_exchange/ppermute | solution.py:453
  130.9 8.0 %collective-permute-start.7 = (bf16[1024,128]{1,0:T(8,128)(2,1)S(1)}, bf16[1024,128]{1,0:T(8,128)(2,1)S(1)}, u32[]{:S(2)}, u32[]{:S(2)}) collective-permute-start(bf16[1024,128]{1,0:T(8,128)(2,1)S(1)} %get-tuple-element.56), channel_id=1, source_target_pairs={{0,96},{32,0},{64,32},{96,64},{1,97},{33,1},{65,33},{97,65},{2,98}... | collective-permute-start | bytes 786440 | tf_op jit(solution)/shard_map/slope_exchange/ppermute | solution.py:453
  131.0 11.0 %collective-permute-start.9 = (bf16[1024,128]{1,0:T(8,128)(2,1)S(1)}, bf16[1024,128]{1,0:T(8,128)(2,1)S(1)}, u32[]{:S(2)}, u32[]{:S(2)}) collective-permute-start(bf16[1024,128]{1,0:T(8,128)(2,1)S(1)} %get-tuple-element.56), channel_id=1, source_target_pairs={{0,32},{32,64},{64,96},{96,0},{1,33},{33,65},{65,97},{97,1},{2,34}... | collective-permute-start | bytes 786440 | tf_op jit(solution)/shard_map/slope_exchange/ppermute | solution.py:453
  134.1 1.6 copy-start.7
  134.5 8.6 %collective-permute-start.10 = (bf16[512,128]{1,0:T(8,128)(2,1)S(1)}, bf16[512,128]{1,0:T(8,128)(2,1)S(1)}, u32[]{:S(2)}, u32[]{:S(2)}) collective-permute-start(bf16[512,128]{1,0:T(8,128)(2,1)S(1)} %get-tuple-element.75), channel_id=1, source_target_pairs={{0,32},{32,64},{64,96},{96,0},{1,33},{33,65},{65,97},{97,1},{2,34}... | collective-permute-start | bytes 393224 | tf_op jit(solution)/shard_map/second_layer/ppermute | solution.py:453
  136.4 13.1 %collective-permute-start.12 = (bf16[1024,128]{1,0:T(8,128)(2,1)S(1)}, bf16[1024,128]{1,0:T(8,128)(2,1)S(1)}, u32[]{:S(2)}, u32[]{:S(2)}) collective-permute-start(bf16[1024,128]{1,0:T(8,128)(2,1)S(1)} %collective-permute-done.8), channel_id=1, source_target_pairs={{0,32},{32,64},{64,96},{96,0},{1,33},{33,65},{65,97},{97,1},{2,34}... | collective-permute-start | bytes 786440 | tf_op jit(solution)/shard_map/slope_exchange/ppermute | solution.py:453
  138.9 10.6 %collective-permute-start.13 = (bf16[1024,128]{1,0:T(8,128)(2,1)S(1)}, bf16[1024,128]{1,0:T(8,128)(2,1)S(1)}, u32[]{:S(2)}, u32[]{:S(2)}) collective-permute-start(bf16[1024,128]{1,0:T(8,128)(2,1)S(1)} %collective-permute-done.7), channel_id=1, source_target_pairs={{0,96},{32,0},{64,32},{96,64},{1,97},{33,1},{65,33},{97,65},{2,98}... | collective-permute-start | bytes 786440 | tf_op jit(solution)/shard_map/slope_exchange/ppermute | solution.py:453
  143.2 10.8 %collective-permute-start.11 = (bf16[16,80,128]{2,1,0:T(8,128)(2,1)S(1)}, bf16[16,80,128]{2,1,0:T(8,128)(2,1)S(1)}, u32[]{:S(2)}, u32[]{:S(2)}) collective-permute-start(bf16[16,80,128]{2,1,0:T(8,128)(2,1)S(1)} %get-tuple-element.59), channel_id=1, source_target_pairs={{0,1},{1,0},{2,3},{3,2},{4,5},{5,4},{6,7},{7,6},{8,9},{9,8},{10,11... | collective-permute-start | bytes 983048 | tf_op jit(solution)/shard_map/gradients/ppermute | solution.py:523
  150.3 3.6 %collective-permute-start.14 = (bf16[16,16,128]{2,1,0:T(8,128)(2,1)S(1)}, bf16[16,16,128]{2,1,0:T(8,128)(2,1)S(1)}, u32[]{:S(2)}, u32[]{:S(2)}) collective-permute-start(bf16[16,16,128]{2,1,0:T(8,128)(2,1)S(1)} %get-tuple-element.61), channel_id=1, source_target_pairs={{0,1},{1,0},{2,3},{3,2},{4,5},{5,4},{6,7},{7,6},{8,9},{9,8},{10,11... | collective-permute-start | bytes 196616 | tf_op jit(solution)/shard_map/gradients/ppermute | solution.py:523
  170.1 12.0 %all-to-all-start.3 = ((bf16[16,96,128]{2,1,0:T(8,128)(2,1)}), bf16[16,96,128]{2,1,0:T(8,128)(2,1)S(1)}, u32[]{:S(2)}, u32[]{:S(2)}) async-start(bf16[16,96,128]{2,1,0:T(8,128)(2,1)} %sum_and_spread.1), calls=%async_computation.3 | async-start | bytes 786432 | tf_op jit(solution)/shard_map/gradients/all_to_all | solution.py:526
  173.6 5.4 %collective-permute-start.15 = (bf16[512,128]{1,0:T(8,128)(2,1)S(1)}, bf16[512,128]{1,0:T(8,128)(2,1)S(1)}, u32[]{:S(2)}, u32[]{:S(2)}) collective-permute-start(bf16[512,128]{1,0:T(8,128)(2,1)S(1)} %get-tuple-element.74), channel_id=1, source_target_pairs={{0,64},{32,96},{64,0},{96,32},{1,65},{33,97},{65,1},{97,33},{2,66}... | collective-permute-start | bytes 393224 | tf_op jit(solution)/shard_map/second_layer/ppermute | solution.py:453
  174.8 7.0 %collective-permute-start.16 = (bf16[512,128]{1,0:T(8,128)(2,1)S(1)}, bf16[512,128]{1,0:T(8,128)(2,1)S(1)}, u32[]{:S(2)}, u32[]{:S(2)}) collective-permute-start(bf16[512,128]{1,0:T(8,128)(2,1)S(1)} %get-tuple-element.73), channel_id=1, source_target_pairs={{0,96},{32,0},{64,32},{96,64},{1,97},{33,1},{65,33},{97,65},{2,98}... | collective-permute-start | bytes 393224 | tf_op jit(solution)/shard_map/second_layer/ppermute | solution.py:453
  182.0 4.0 %collective-permute-start.17 = (bf16[16,96,128]{2,1,0:T(8,128)(2,1)S(1)}, bf16[16,96,128]{2,1,0:T(8,128)(2,1)S(1)}, u32[]{:S(2)}, u32[]{:S(2)}) collective-permute-start(bf16[16,96,128]{2,1,0:T(8,128)(2,1)S(1)} %all-to-all-done.3.mine_ref), channel_id=1, source_target_pairs={{0,1},{1,0},{2,3},{3,2},{4,5},{5,4},{6,7},{7,6},{8,9},{9,8},{10,11... | collective-permute-start | bytes 1179656 | tf_op jit(solution)/shard_map/gradients/ppermute | solution.py:523

commit v6 on v5

--- a/solution.py
+++ b/solution.py
@@ -148,7 +148,7 @@
         out_ref[pl.ds(begin, 16), half:] = jnp.concatenate(highs, axis=0).astype(BF)
         return carry
 
-    lax.fori_loop(0, count // 16, some, 0, unroll=8)
+    lax.fori_loop(0, count // 16, some, 0, unroll=16)
 
 
 def piece_copies(source_ref, held, sems):

time: 188 us -> 187 us (level)
  no operation moved by 1% of the time
where the time goes in v6:
time: 187 us
  Pallas kernels  53.2 us (28%)
  waiting for transfers between devices  51.8 us (28%)
  starting transfers between devices  38.8 us (21%)
  blocking collectives  31.2 us (17%)
  matrix products  5.54 us (3%)
  local copies, waits for them, and re-layouts  3.09 us (2%)
  other arithmetic  2.07 us (1%)
    all_to_all x1, waiting for transfers between devices, exchange(): lax.all_to_all(value, 'wide', split_axis=0, concat_axis=0, tiled=True)  31.1 us
    ppermute x15, waiting for transfers between devices, shift(): lax.ppermute(value, 'blk', [(i, (i + by) % quarters) for i in range(quart...  19 us
    ppermute x15, starting transfers between devices, shift(): lax.ppermute(value, 'blk', [(i, (i + by) % quarters) for i in range(quart...  18.6 us
    pallas_call x1, Pallas kernels, first_layer(): pl.pallas_call(functools.partial(layer_kernel, list_width), grid_spec=plt...  18.3 us
    all_to_all x1, blocking collectives, exchange(): lax.all_to_all(value, 'wide', split_axis=0, concat_axis=0, tiled=True)  16 us
    pallas_call x2, Pallas kernels, neighbour_counts(): pl.pallas_call(count_kernel, grid=(targets // 16 // block_groups,), in_sp...  15.7 us
    all_to_all x1, blocking collectives, between_chips(): lax.all_to_all(value, 'wide', split_axis=0, concat_axis=0, axis_index_gro...  15.2 us
    pallas_call x1, Pallas kernels, gather_rows(): pl.pallas_call(gather_kernel, grid=(total // rows,), in_specs=[pl.BlockSp...  12.7 us
  transfers between devices with their start and end apart: 20, of which 10 were waited for; matrix products, arithmetic and copies ran while one was open for 5% of the time, Pallas kernels for 9%

profile of v6, /device:TPU:1, one launch (start us, length us, event | category | flops | bytes accessed | tf_op | source)
XLA Modules:
  0.0 186.7 jit_solution(806122633914851218)
XLA Ops:
  0.6 2.9 %request_table.1 = (s32[32,1,256]{2,1,0:T(1,128)}, s32[32,128]{1,0:T(8,128)}) custom-call(s32[32,128]{1,0:T(8,128)} %bitcast.25, s32[32,128]{1,0:T(8,128)} %bitcast.26), custom_call_target="tpu_custom_call" | custom-call | tf_op jit(solution)/shard_map/requests/request_table/pallas_call | solution.py:66
  3.6 16.0 %all_to_all.20 = s32[32,1,256]{2,1,0:T(1,128)} all-to-all(s32[32,1,256]{2,1,0:T(1,128)} %get-tuple-element.39), channel_id=1, replica_groups=mesh['blk'=4,'wide'=32] {'wide'}, dimensions={0} | all-to-all | bytes 65536 | tf_op jit(solution)/shard_map/requests/all_to_all | solution.py:456
  19.5 12.7 %gather_rows.1 = bf16[8192,256]{1,0:T(8,128)(2,1)} custom-call(s32[8192]{0:T(1024)} %bitcast.24, bf16[8192,256]{1,0:T(8,128)(2,1)} %table_ref.1), custom_call_target="tpu_custom_call" | custom-call | tf_op jit(solution)/shard_map/rows/gather_rows/pallas_call | solution.py:200
  32.3 5.0 %all-to-all-start.1 = ((bf16[32,256,256]{2,1,0:T(8,128)(2,1)}), bf16[32,256,256]{2,1,0:T(8,128)(2,1)}, u32[]{:S(2)}, u32[]{:S(2)}) async-start(bf16[32,256,256]{2,1,0:T(8,128)(2,1)} %bitcast.23), calls=%async_computation.1 | async-start | bytes 8388608 | tf_op jit(solution)/shard_map/rows/all_to_all | solution.py:456
  38.5 2.6 %neighbour_counts.3 = bf16[512,2048]{1,0:T(8,128)(2,1)S(1)} custom-call(s32[32,256]{1,0:T(8,128)S(1)} %reshape.46.idx_ref), custom_call_target="tpu_custom_call" | custom-call | flops 536870912 | bytes 2097152 | tf_op jit(solution)/shard_map/beside_rows/neighbour_counts/pallas_call | solution.py:112
  43.3 13.1 %neighbour_counts.2.counts_ref = bf16[2048,4096]{1,0:T(8,128)(2,1)} custom-call(s32[128,256]{1,0:T(8,128)S(1)} %reshape.45.idx_ref), custom_call_target="tpu_custom_call" | custom-call | flops 4294967296 | bytes 16777216 | tf_op jit(solution)/shard_map/beside_rows/neighbour_counts/pallas_call | solution.py:112
  56.5 31.1 %all-to-all-done.1 = bf16[32,256,256]{2,1,0:T(8,128)(2,1)} async-done(((bf16[32,256,256]{2,1,0:T(8,128)(2,1)}), bf16[32,256,256]{2,1,0:T(8,128)(2,1)}, u32[]{:S(2)}, u32[]{:S(2)}) %all-to-all-start.1) | async-done | bytes 4194336 | tf_op jit(solution)/shard_map/rows/all_to_all | solution.py:456
  87.7 18.3 %first_layer.1 = (bf16[1024,128]{1,0:T(8,128)(2,1)}, bf16[1024,128]{1,0:T(8,128)(2,1)}, bf16[1024,128]{1,0:T(8,128)(2,1)S(1)}, bf16[1024,128]{1,0:T(8,128)(2,1)S...) custom-call(s32[4096]{0:T(1024)} %bitcast.27, ...), custom_call_target="tpu_custom_call" | custom-call | tf_op jit(solution)/shard_map/first_layer/first_layer/pallas_call | solution.py:274
  106.0 1.7 collective-permute-start
  107.7 2.2 %collective-permute-start.4 = (bf16[1024,128]{1,0:T(8,128)(2,1)}, bf16[1024,128]{1,0:T(8,128)(2,1)S(1)}, u32[]{:S(2)}, u32[]{:S(2)}) collective-permute-start(bf16[1024,128]{1,0:T(8,128)(2,1)} %get-tuple-element.52), channel_id=1, source_target_pairs={{0,96},{32,0},{64,32},{96,64},{1,97},{33,1},{65,33},{97,65},{2,98}... | collective-permute-start | bytes 786440 | tf_op jit(solution)/shard_map/pre_act_exchange/ppermute | solution.py:453
  109.9 1.4 collective-permute-start.2
  111.4 2.4 %collective-permute-done.right = bf16[1024,128]{1,0:T(8,128)(2,1)S(1)} collective-permute-done((bf16[1024,128]{1,0:T(8,128)(2,1)}, bf16[1024,128]{1,0:T(8,128)(2,1)S(1)}, u32[]{:S(2)}, u32[]{:S(2)}) %collective-permute-start) | collective-permute-done | bytes 262176 | tf_op jit(solution)/shard_map/pre_act_exchange/ppermute | solution.py:453
  114.0 2.9 %collective-permute-start.5 = (bf16[1024,128]{1,0:T(8,128)(2,1)S(1)}, bf16[1024,128]{1,0:T(8,128)(2,1)S(1)}, u32[]{:S(2)}, u32[]{:S(2)}) collective-permute-start(bf16[1024,128]{1,0:T(8,128)(2,1)S(1)} %added.3), channel_id=1, source_target_pairs={{0,96},{32,0},{64,32},{96,64},{1,97},{33,1},{65,33},{97,65},{2,98}... | collective-permute-start | bytes 786440 | tf_op jit(solution)/shard_map/pre_act_exchange/ppermute | solution.py:453
  116.9 1.1 convert_add_fusion.1
  118.0 8.4 %collective-permute-done.1.up = bf16[1024,128]{1,0:T(8,128)(2,1)S(1)} collective-permute-done((bf16[1024,128]{1,0:T(8,128)(2,1)S(1)}, bf16[1024,128]{1,0:T(8,128)(2,1)S(1)}, u32[]{:S(2)}, u32[]{:S(2)}) %collective-permute-start.1) | collective-permute-done | bytes 262176 | tf_op jit(solution)/shard_map/pre_act_exchange/ppermute | solution.py:453
  126.8 2.7 %collective-permute-start.6 = (bf16[1024,128]{1,0:T(8,128)(2,1)S(1)}, bf16[1024,128]{1,0:T(8,128)(2,1)S(1)}, u32[]{:S(2)}, u32[]{:S(2)}) collective-permute-start(bf16[1024,128]{1,0:T(8,128)(2,1)S(1)} %get-tuple-element.55), channel_id=1, source_target_pairs={{0,96},{32,0},{64,32},{96,64},{1,97},{33,1},{65,33},{97,65},{2,98}... | collective-permute-start | bytes 786440 | tf_op jit(solution)/shard_map/slope_exchange/ppermute | solution.py:453
  129.9 1.4 collective-permute-start.9
  131.3 0.8 fusion
  133.6 1.0 copy-done.7
  135.4 2.4 %collective-permute-done.7 = bf16[1024,128]{1,0:T(8,128)(2,1)S(1)} collective-permute-done((bf16[1024,128]{1,0:T(8,128)(2,1)S(1)}, bf16[1024,128]{1,0:T(8,128)(2,1)S(1)}, u32[]{:S(2)}, u32[]{:S(2)}) %collective-permute-start.7) | collective-permute-done | bytes 262176 | tf_op jit(solution)/shard_map/slope_exchange/ppermute | solution.py:453
  137.8 3.0 %collective-permute-start.13 = (bf16[1024,128]{1,0:T(8,128)(2,1)S(1)}, bf16[1024,128]{1,0:T(8,128)(2,1)S(1)}, u32[]{:S(2)}, u32[]{:S(2)}) collective-permute-start(bf16[1024,128]{1,0:T(8,128)(2,1)S(1)} %collective-permute-done.7), channel_id=1, source_target_pairs={{0,96},{32,0},{64,32},{96,64},{1,97},{33,1},{65,33},{97,65},{2,98}... | collective-permute-start | bytes 786440 | tf_op jit(solution)/shard_map/slope_exchange/ppermute | solution.py:453
  142.1 6.4 %collective-permute-start.11 = (bf16[16,80,128]{2,1,0:T(8,128)(2,1)S(1)}, bf16[16,80,128]{2,1,0:T(8,128)(2,1)S(1)}, u32[]{:S(2)}, u32[]{:S(2)}) collective-permute-start(bf16[16,80,128]{2,1,0:T(8,128)(2,1)S(1)} %get-tuple-element.59), channel_id=1, source_target_pairs={{0,1},{1,0},{2,3},{3,2},{4,5},{5,4},{6,7},{7,6},{8,9},{9,8},{10,11... | collective-permute-start | bytes 983048 | tf_op jit(solution)/shard_map/gradients/ppermute | solution.py:523
  149.3 2.7 %collective-permute-start.14 = (bf16[16,16,128]{2,1,0:T(8,128)(2,1)S(1)}, bf16[16,16,128]{2,1,0:T(8,128)(2,1)S(1)}, u32[]{:S(2)}, u32[]{:S(2)}) collective-permute-start(bf16[16,16,128]{2,1,0:T(8,128)(2,1)S(1)} %get-tuple-element.61), channel_id=1, source_target_pairs={{0,1},{1,0},{2,3},{3,2},{4,5},{5,4},{6,7},{7,6},{8,9},{9,8},{10,11... | collective-permute-start | bytes 196616 | tf_op jit(solution)/shard_map/gradients/ppermute | solution.py:523
  152.0 0.9 collective-permute-done.14.got_far
  153.0 15.2 %all_to_all.21.got_ref = bf16[16,96,128]{2,1,0:T(8,128)(2,1)S(1)} all-to-all(bf16[16,96,128]{2,1,0:T(8,128)(2,1)S(1)} %joined.1), channel_id=1, replica_groups={{0,2,4,6,8,10,12,14,16,18,20,22,24,26,28,30},{1,3,5,7,9,11,13,15,17,19,..., dimensions={0} | all-to-all | bytes 786432 | tf_op jit(solution)/shard_map/gradients/all_to_all | solution.py:526
  169.0 3.6 %all-to-all-start.3 = ((bf16[16,96,128]{2,1,0:T(8,128)(2,1)}), bf16[16,96,128]{2,1,0:T(8,128)(2,1)S(1)}, u32[]{:S(2)}, u32[]{:S(2)}) async-start(bf16[16,96,128]{2,1,0:T(8,128)(2,1)} %sum_and_spread.1), calls=%async_computation.3 | async-start | bytes 786432 | tf_op jit(solution)/shard_map/gradients/all_to_all | solution.py:526
  172.6 1.2 collective-permute-start.15
  173.7 1.6 collective-permute-start.16
  175.3 2.6 %collective-permute-done.15 = bf16[512,128]{1,0:T(8,128)(2,1)S(1)} collective-permute-done((bf16[512,128]{1,0:T(8,128)(2,1)S(1)}, bf16[512,128]{1,0:T(8,128)(2,1)S(1)}, u32[]{:S(2)}, u32[]{:S(2)}) %collective-permute-start.15) | collective-permute-done | bytes 131104 | tf_op jit(solution)/shard_map/second_layer/ppermute | solution.py:453
  178.0 2.8 %collective-permute-done.16 = bf16[512,128]{1,0:T(8,128)(2,1)S(1)} collective-permute-done((bf16[512,128]{1,0:T(8,128)(2,1)S(1)}, bf16[512,128]{1,0:T(8,128)(2,1)S(1)}, u32[]{:S(2)}, u32[]{:S(2)}) %collective-permute-start.16) | collective-permute-done | bytes 131104 | tf_op jit(solution)/shard_map/second_layer/ppermute | solution.py:453
  181.0 2.6 %collective-permute-start.17 = (bf16[16,96,128]{2,1,0:T(8,128)(2,1)S(1)}, bf16[16,96,128]{2,1,0:T(8,128)(2,1)S(1)}, u32[]{:S(2)}, u32[]{:S(2)}) collective-permute-start(bf16[16,96,128]{2,1,0:T(8,128)(2,1)S(1)} %all-to-all-done.3.mine_ref), channel_id=1, source_target_pairs={{0,1},{1,0},{2,3},{3,2},{4,5},{5,4},{6,7},{7,6},{8,9},{9,8},{10,11... | collective-permute-start | bytes 1179656 | tf_op jit(solution)/shard_map/gradients/ppermute | solution.py:523
  184.9 1.8 finish.1
  (67 shorter events, 11.2 us)
Async XLA Ops:
  0.6 40.5 %copy-start = (bf16[512,512]{1,0:T(8,128)(2,1)S(1)}, bf16[512,512]{1,0:T(8,128)(2,1)}, u32[]{:S(2)}) copy-start(bf16[512,512]{1,0:T(8,128)(2,1)} %param.21) | copy-start | bytes 1572868
  32.3 5.0 %copy-start.6 = (s32[512,10]{0,1:T(8,128)S(1)}, s32[512,10]{0,1:T(8,128)}, u32[]{:S(2)}) copy-start(s32[512,10]{0,1:T(8,128)} %param.15) | copy-start | bytes 61444
  32.3 5.3 %copy-start.5 = (s32[2048,15]{0,1:T(8,128)S(1)}, s32[2048,15]{0,1:T(8,128)}, u32[]{:S(2)}) copy-start(s32[2048,15]{0,1:T(8,128)} %param.14) | copy-start | bytes 368644
  32.3 55.4 %all-to-all-start.1 = ((bf16[32,256,256]{2,1,0:T(8,128)(2,1)}), bf16[32,256,256]{2,1,0:T(8,128)(2,1)}, u32[]{:S(2)}, u32[]{:S(2)}) async-start(bf16[32,256,256]{2,1,0:T(8,128)(2,1)} %bitcast.23), calls=%async_computation.1 | async-start | bytes 8388608 | tf_op jit(solution)/shard_map/rows/all_to_all | solution.py:456
  38.1 3.1 %copy-start.3 = (bf16[128,512]{1,0:T(8,128)(2,1)S(1)}, bf16[128,512]{1,0:T(8,128)(2,1)}, u32[]{:S(2)}) copy-start(bf16[128,512]{1,0:T(8,128)(2,1)} %param.20) | copy-start | bytes 393220
  38.1 3.4 %copy-start.4 = (bf16[128,512]{1,0:T(8,128)(2,1)S(1)}, bf16[128,512]{1,0:T(8,128)(2,1)}, u32[]{:S(2)}) copy-start(bf16[128,512]{1,0:T(8,128)(2,1)} %param.19) | copy-start | bytes 393220
  41.2 1.4 copy-start.1
  87.7 22.2 %copy-start.8 = (bf16[128]{0:T(256)(128)(2,1)S(1)}, bf16[128]{0:T(256)(128)(2,1)}, u32[]{:S(2)}) copy-start(bf16[128]{0:T(256)(128)(2,1)} %param.18) | copy-start | bytes 772
  106.0 7.8 %collective-permute-start = (bf16[1024,128]{1,0:T(8,128)(2,1)}, bf16[1024,128]{1,0:T(8,128)(2,1)S(1)}, u32[]{:S(2)}, u32[]{:S(2)}) collective-permute-start(bf16[1024,128]{1,0:T(8,128)(2,1)} %get-tuple-element.44), channel_id=1, source_target_pairs={{0,32},{32,64},{64,96},{96,0},{1,33},{33,65},{65,97},{97,1},{2,34}... | collective-permute-start | bytes 786440 | tf_op jit(solution)/shard_map/pre_act_exchange/ppermute | solution.py:453
  107.7 6.2 %collective-permute-start.4 = (bf16[1024,128]{1,0:T(8,128)(2,1)}, bf16[1024,128]{1,0:T(8,128)(2,1)S(1)}, u32[]{:S(2)}, u32[]{:S(2)}) collective-permute-start(bf16[1024,128]{1,0:T(8,128)(2,1)} %get-tuple-element.52), channel_id=1, source_target_pairs={{0,96},{32,0},{64,32},{96,64},{1,97},{33,1},{65,33},{97,65},{2,98}... | collective-permute-start | bytes 786440 | tf_op jit(solution)/shard_map/pre_act_exchange/ppermute | solution.py:453
  109.9 8.1 %collective-permute-start.2 = (bf16[1024,128]{1,0:T(8,128)(2,1)S(1)}, bf16[1024,128]{1,0:T(8,128)(2,1)S(1)}, u32[]{:S(2)}, u32[]{:S(2)}) collective-permute-start(bf16[1024,128]{1,0:T(8,128)(2,1)S(1)} %get-tuple-element.45), channel_id=1, source_target_pairs={{0,96},{32,0},{64,32},{96,64},{1,97},{33,1},{65,33},{97,65},{2,98}... | collective-permute-start | bytes 786440 | tf_op jit(solution)/shard_map/pre_act_exchange/ppermute | solution.py:453
  111.3 18.2 %collective-permute-start.3 = (bf16[1024,128]{1,0:T(8,128)(2,1)S(1)}, bf16[1024,128]{1,0:T(8,128)(2,1)S(1)}, u32[]{:S(2)}, u32[]{:S(2)}) collective-permute-start(bf16[1024,128]{1,0:T(8,128)(2,1)S(1)} %get-tuple-element.50), channel_id=1, source_target_pairs={{0,32},{32,64},{64,96},{96,0},{1,33},{33,65},{65,97},{97,1},{2,34}... | collective-permute-start | bytes 786440 | tf_op jit(solution)/shard_map/pre_act_exchange/ppermute | solution.py:453
  113.8 12.6 %collective-permute-start.1 = (bf16[1024,128]{1,0:T(8,128)(2,1)S(1)}, bf16[1024,128]{1,0:T(8,128)(2,1)S(1)}, u32[]{:S(2)}, u32[]{:S(2)}) collective-permute-start(bf16[1024,128]{1,0:T(8,128)(2,1)S(1)} %added.2), channel_id=1, source_target_pairs={{0,32},{32,64},{64,96},{96,0},{1,33},{33,65},{65,97},{97,1},{2,34}... | collective-permute-start | bytes 786440 | tf_op jit(solution)/shard_map/pre_act_exchange/ppermute | solution.py:453
  114.0 15.5 %collective-permute-start.5 = (bf16[1024,128]{1,0:T(8,128)(2,1)S(1)}, bf16[1024,128]{1,0:T(8,128)(2,1)S(1)}, u32[]{:S(2)}, u32[]{:S(2)}) collective-permute-start(bf16[1024,128]{1,0:T(8,128)(2,1)S(1)} %added.3), channel_id=1, source_target_pairs={{0,96},{32,0},{64,32},{96,64},{1,97},{33,1},{65,33},{97,65},{2,98}... | collective-permute-start | bytes 786440 | tf_op jit(solution)/shard_map/pre_act_exchange/ppermute | solution.py:453
  126.4 4.9 %copy-start.2 = (bf16[512,2048]{1,0:T(8,128)(2,1)S(1)}, bf16[512,2048]{1,0:T(8,128)(2,1)}, u32[]{:S(2)}) copy-start(bf16[512,2048]{1,0:T(8,128)(2,1)} %copy-done.1) | copy-start | bytes 6291460
  126.7 8.6 %collective-permute-start.8 = (bf16[1024,128]{1,0:T(8,128)(2,1)S(1)}, bf16[1024,128]{1,0:T(8,128)(2,1)S(1)}, u32[]{:S(2)}, u32[]{:S(2)}) collective-permute-start(bf16[1024,128]{1,0:T(8,128)(2,1)S(1)} %get-tuple-element.55), channel_id=1, source_target_pairs={{0,32},{32,64},{64,96},{96,0},{1,33},{33,65},{65,97},{97,1},{2,34}... | collective-permute-start | bytes 786440 | tf_op jit(solution)/shard_map/slope_exchange/ppermute | solution.py:453
  126.8 14.1 %collective-permute-start.6 = (bf16[1024,128]{1,0:T(8,128)(2,1)S(1)}, bf16[1024,128]{1,0:T(8,128)(2,1)S(1)}, u32[]{:S(2)}, u32[]{:S(2)}) collective-permute-start(bf16[1024,128]{1,0:T(8,128)(2,1)S(1)} %get-tuple-element.55), channel_id=1, source_target_pairs={{0,96},{32,0},{64,32},{96,64},{1,97},{33,1},{65,33},{97,65},{2,98}... | collective-permute-start | bytes 786440 | tf_op jit(solution)/shard_map/slope_exchange/ppermute | solution.py:453
  129.8 8.0 %collective-permute-start.7 = (bf16[1024,128]{1,0:T(8,128)(2,1)S(1)}, bf16[1024,128]{1,0:T(8,128)(2,1)S(1)}, u32[]{:S(2)}, u32[]{:S(2)}) collective-permute-start(bf16[1024,128]{1,0:T(8,128)(2,1)S(1)} %get-tuple-element.56), channel_id=1, source_target_pairs={{0,96},{32,0},{64,32},{96,64},{1,97},{33,1},{65,33},{97,65},{2,98}... | collective-permute-start | bytes 786440 | tf_op jit(solution)/shard_map/slope_exchange/ppermute | solution.py:453
  129.9 11.0 %collective-permute-start.9 = (bf16[1024,128]{1,0:T(8,128)(2,1)S(1)}, bf16[1024,128]{1,0:T(8,128)(2,1)S(1)}, u32[]{:S(2)}, u32[]{:S(2)}) collective-permute-start(bf16[1024,128]{1,0:T(8,128)(2,1)S(1)} %get-tuple-element.56), channel_id=1, source_target_pairs={{0,32},{32,64},{64,96},{96,0},{1,33},{33,65},{65,97},{97,1},{2,34}... | collective-permute-start | bytes 786440 | tf_op jit(solution)/shard_map/slope_exchange/ppermute | solution.py:453
  133.0 1.6 copy-start.7
  133.4 8.6 %collective-permute-start.10 = (bf16[512,128]{1,0:T(8,128)(2,1)S(1)}, bf16[512,128]{1,0:T(8,128)(2,1)S(1)}, u32[]{:S(2)}, u32[]{:S(2)}) collective-permute-start(bf16[512,128]{1,0:T(8,128)(2,1)S(1)} %get-tuple-element.75), channel_id=1, source_target_pairs={{0,32},{32,64},{64,96},{96,0},{1,33},{33,65},{65,97},{97,1},{2,34}... | collective-permute-start | bytes 393224 | tf_op jit(solution)/shard_map/second_layer/ppermute | solution.py:453
  135.4 13.1 %collective-permute-start.12 = (bf16[1024,128]{1,0:T(8,128)(2,1)S(1)}, bf16[1024,128]{1,0:T(8,128)(2,1)S(1)}, u32[]{:S(2)}, u32[]{:S(2)}) collective-permute-start(bf16[1024,128]{1,0:T(8,128)(2,1)S(1)} %collective-permute-done.8), channel_id=1, source_target_pairs={{0,32},{32,64},{64,96},{96,0},{1,33},{33,65},{65,97},{97,1},{2,34}... | collective-permute-start | bytes 786440 | tf_op jit(solution)/shard_map/slope_exchange/ppermute | solution.py:453
  137.8 10.6 %collective-permute-start.13 = (bf16[1024,128]{1,0:T(8,128)(2,1)S(1)}, bf16[1024,128]{1,0:T(8,128)(2,1)S(1)}, u32[]{:S(2)}, u32[]{:S(2)}) collective-permute-start(bf16[1024,128]{1,0:T(8,128)(2,1)S(1)} %collective-permute-done.7), channel_id=1, source_target_pairs={{0,96},{32,0},{64,32},{96,64},{1,97},{33,1},{65,33},{97,65},{2,98}... | collective-permute-start | bytes 786440 | tf_op jit(solution)/shard_map/slope_exchange/ppermute | solution.py:453
  142.1 10.8 %collective-permute-start.11 = (bf16[16,80,128]{2,1,0:T(8,128)(2,1)S(1)}, bf16[16,80,128]{2,1,0:T(8,128)(2,1)S(1)}, u32[]{:S(2)}, u32[]{:S(2)}) collective-permute-start(bf16[16,80,128]{2,1,0:T(8,128)(2,1)S(1)} %get-tuple-element.59), channel_id=1, source_target_pairs={{0,1},{1,0},{2,3},{3,2},{4,5},{5,4},{6,7},{7,6},{8,9},{9,8},{10,11... | collective-permute-start | bytes 983048 | tf_op jit(solution)/shard_map/gradients/ppermute | solution.py:523
  149.3 3.6 %collective-permute-start.14 = (bf16[16,16,128]{2,1,0:T(8,128)(2,1)S(1)}, bf16[16,16,128]{2,1,0:T(8,128)(2,1)S(1)}, u32[]{:S(2)}, u32[]{:S(2)}) collective-permute-start(bf16[16,16,128]{2,1,0:T(8,128)(2,1)S(1)} %get-tuple-element.61), channel_id=1, source_target_pairs={{0,1},{1,0},{2,3},{3,2},{4,5},{5,4},{6,7},{7,6},{8,9},{9,8},{10,11... | collective-permute-start | bytes 196616 | tf_op jit(solution)/shard_map/gradients/ppermute | solution.py:523
  169.0 12.0 %all-to-all-start.3 = ((bf16[16,96,128]{2,1,0:T(8,128)(2,1)}), bf16[16,96,128]{2,1,0:T(8,128)(2,1)S(1)}, u32[]{:S(2)}, u32[]{:S(2)}) async-start(bf16[16,96,128]{2,1,0:T(8,128)(2,1)} %sum_and_spread.1), calls=%async_computation.3 | async-start | bytes 786432 | tf_op jit(solution)/shard_map/gradients/all_to_all | solution.py:526
  172.6 5.4 %collective-permute-start.15 = (bf16[512,128]{1,0:T(8,128)(2,1)S(1)}, bf16[512,128]{1,0:T(8,128)(2,1)S(1)}, u32[]{:S(2)}, u32[]{:S(2)}) collective-permute-start(bf16[512,128]{1,0:T(8,128)(2,1)S(1)} %get-tuple-element.74), channel_id=1, source_target_pairs={{0,64},{32,96},{64,0},{96,32},{1,65},{33,97},{65,1},{97,33},{2,66}... | collective-permute-start | bytes 393224 | tf_op jit(solution)/shard_map/second_layer/ppermute | solution.py:453
  173.7 7.0 %collective-permute-start.16 = (bf16[512,128]{1,0:T(8,128)(2,1)S(1)}, bf16[512,128]{1,0:T(8,128)(2,1)S(1)}, u32[]{:S(2)}, u32[]{:S(2)}) collective-permute-start(bf16[512,128]{1,0:T(8,128)(2,1)S(1)} %get-tuple-element.73), channel_id=1, source_target_pairs={{0,96},{32,0},{64,32},{96,64},{1,97},{33,1},{65,33},{97,65},{2,98}... | collective-permute-start | bytes 393224 | tf_op jit(solution)/shard_map/second_layer/ppermute | solution.py:453
  181.0 4.0 %collective-permute-start.17 = (bf16[16,96,128]{2,1,0:T(8,128)(2,1)S(1)}, bf16[16,96,128]{2,1,0:T(8,128)(2,1)S(1)}, u32[]{:S(2)}, u32[]{:S(2)}) collective-permute-start(bf16[16,96,128]{2,1,0:T(8,128)(2,1)S(1)} %all-to-all-done.3.mine_ref), channel_id=1, source_target_pairs={{0,1},{1,0},{2,3},{3,2},{4,5},{5,4},{6,7},{7,6},{8,9},{9,8},{10,11... | collective-permute-start | bytes 1179656 | tf_op jit(solution)/shard_map/gradients/ppermute | solution.py:523

commit v7 on v6

--- a/solution.py
+++ b/solution.py
@@ -507,6 +507,8 @@
         hiddens, slopes = [], []
         for half, (up, down) in enumerate([(up_0, down_0), (up_1, down_1)]):
             base = own[half].astype(F32) + bias_hidden.astype(F32)
+            if half:
+                base, _ = lax.optimization_barrier((base, slopes[0]))
             hidden, slope = hidden_and_slope(base, up, down, d_hidden, half * targets // 2)
             hiddens.append(hidden)
             slopes.append(slope)

time: 187 us -> 187 us (level)
    all_to_all x1, waiting for transfers between devices: 0.22 us -> 2.35 us  [between_chips(): lax.all_to_all(value, 'wide', split_axis=0, concat_axis=0, axis_index_gro...]
where the time goes in v7:
time: 187 us
  waiting for transfers between devices  53.4 us (29%)
  Pallas kernels  53.2 us (28%)
  starting transfers between devices  37.1 us (20%)
  blocking collectives  31.2 us (17%)
  matrix products  5.52 us (3%)
  local copies, waits for them, and re-layouts  3.1 us (2%)
  other arithmetic  2.07 us (1%)
    all_to_all x1, waiting for transfers between devices, exchange(): lax.all_to_all(value, 'wide', split_axis=0, concat_axis=0, tiled=True)  31.1 us
    ppermute x15, waiting for transfers between devices, shift(): lax.ppermute(value, 'blk', [(i, (i + by) % quarters) for i in range(quart...  18.5 us
    pallas_call x1, Pallas kernels, first_layer(): pl.pallas_call(functools.partial(layer_kernel, list_width), grid_spec=plt...  18.3 us
    ppermute x15, starting transfers between devices, shift(): lax.ppermute(value, 'blk', [(i, (i + by) % quarters) for i in range(quart...  16.9 us
    all_to_all x1, blocking collectives, exchange(): lax.all_to_all(value, 'wide', split_axis=0, concat_axis=0, tiled=True)  16 us
    pallas_call x2, Pallas kernels, neighbour_counts(): pl.pallas_call(count_kernel, grid=(targets // 16 // block_groups,), in_sp...  15.7 us
    all_to_all x1, blocking collectives, between_chips(): lax.all_to_all(value, 'wide', split_axis=0, concat_axis=0, axis_index_gro...  15.3 us
    pallas_call x1, Pallas kernels, gather_rows(): pl.pallas_call(gather_kernel, grid=(total // rows,), in_specs=[pl.BlockSp...  12.7 us
  transfers between devices with their start and end apart: 20, of which 10 were waited for; matrix products, arithmetic and copies ran while one was open for 5% of the time, Pallas kernels for 9%

profile of v7, /device:TPU:1, one launch (start us, length us, event | category | flops | bytes accessed | tf_op | source)
XLA Modules:
  0.0 186.7 jit_solution(16614028882364011760)
XLA Ops:
  0.6 2.9 %request_table.1 = (s32[32,1,256]{2,1,0:T(1,128)}, s32[32,128]{1,0:T(8,128)}) custom-call(s32[32,128]{1,0:T(8,128)} %bitcast.25, s32[32,128]{1,0:T(8,128)} %bitcast.26), custom_call_target="tpu_custom_call" | custom-call | tf_op jit(solution)/shard_map/requests/request_table/pallas_call | solution.py:66
  3.6 16.0 %all_to_all.20 = s32[32,1,256]{2,1,0:T(1,128)} all-to-all(s32[32,1,256]{2,1,0:T(1,128)} %get-tuple-element.40), channel_id=1, replica_groups=mesh['blk'=4,'wide'=32] {'wide'}, dimensions={0} | all-to-all | bytes 65536 | tf_op jit(solution)/shard_map/requests/all_to_all | solution.py:456
  19.5 12.7 %gather_rows.1 = bf16[8192,256]{1,0:T(8,128)(2,1)} custom-call(s32[8192]{0:T(1024)} %bitcast.24, bf16[8192,256]{1,0:T(8,128)(2,1)} %table_ref.1), custom_call_target="tpu_custom_call" | custom-call | tf_op jit(solution)/shard_map/rows/gather_rows/pallas_call | solution.py:200
  32.3 5.0 %all-to-all-start.1 = ((bf16[32,256,256]{2,1,0:T(8,128)(2,1)}), bf16[32,256,256]{2,1,0:T(8,128)(2,1)}, u32[]{:S(2)}, u32[]{:S(2)}) async-start(bf16[32,256,256]{2,1,0:T(8,128)(2,1)} %bitcast.23), calls=%async_computation.1 | async-start | bytes 8388608 | tf_op jit(solution)/shard_map/rows/all_to_all | solution.py:456
  38.5 2.6 %neighbour_counts.3 = bf16[512,2048]{1,0:T(8,128)(2,1)S(1)} custom-call(s32[32,256]{1,0:T(8,128)S(1)} %reshape.46.idx_ref), custom_call_target="tpu_custom_call" | custom-call | flops 536870912 | bytes 2097152 | tf_op jit(solution)/shard_map/beside_rows/neighbour_counts/pallas_call | solution.py:112
  43.3 13.1 %neighbour_counts.2.counts_ref = bf16[2048,4096]{1,0:T(8,128)(2,1)} custom-call(s32[128,256]{1,0:T(8,128)S(1)} %reshape.45.idx_ref), custom_call_target="tpu_custom_call" | custom-call | flops 4294967296 | bytes 16777216 | tf_op jit(solution)/shard_map/beside_rows/neighbour_counts/pallas_call | solution.py:112
  56.5 31.1 %all-to-all-done.1 = bf16[32,256,256]{2,1,0:T(8,128)(2,1)} async-done(((bf16[32,256,256]{2,1,0:T(8,128)(2,1)}), bf16[32,256,256]{2,1,0:T(8,128)(2,1)}, u32[]{:S(2)}, u32[]{:S(2)}) %all-to-all-start.1) | async-done | bytes 4194336 | tf_op jit(solution)/shard_map/rows/all_to_all | solution.py:456
  87.7 18.3 %first_layer.1 = (bf16[1024,128]{1,0:T(8,128)(2,1)}, bf16[1024,128]{1,0:T(8,128)(2,1)}, bf16[1024,128]{1,0:T(8,128)(2,1)S(1)}, bf16[1024,128]{1,0:T(8,128)(2,1)S...) custom-call(s32[4096]{0:T(1024)} %bitcast.27, ...), custom_call_target="tpu_custom_call" | custom-call | tf_op jit(solution)/shard_map/first_layer/first_layer/pallas_call | solution.py:274
  106.0 1.7 collective-permute-start
  107.7 2.2 %collective-permute-start.4 = (bf16[1024,128]{1,0:T(8,128)(2,1)}, bf16[1024,128]{1,0:T(8,128)(2,1)S(1)}, u32[]{:S(2)}, u32[]{:S(2)}) collective-permute-start(bf16[1024,128]{1,0:T(8,128)(2,1)} %get-tuple-element.55), channel_id=1, source_target_pairs={{0,96},{32,0},{64,32},{96,64},{1,97},{33,1},{65,33},{97,65},{2,98}... | collective-permute-start | bytes 786440 | tf_op jit(solution)/shard_map/pre_act_exchange/ppermute | solution.py:453
  109.9 1.4 collective-permute-start.2
  111.4 2.4 %collective-permute-done.right = bf16[1024,128]{1,0:T(8,128)(2,1)S(1)} collective-permute-done((bf16[1024,128]{1,0:T(8,128)(2,1)}, bf16[1024,128]{1,0:T(8,128)(2,1)S(1)}, u32[]{:S(2)}, u32[]{:S(2)}) %collective-permute-start) | collective-permute-done | bytes 262176 | tf_op jit(solution)/shard_map/pre_act_exchange/ppermute | solution.py:453
  114.0 2.9 %collective-permute-start.5 = (bf16[1024,128]{1,0:T(8,128)(2,1)S(1)}, bf16[1024,128]{1,0:T(8,128)(2,1)S(1)}, u32[]{:S(2)}, u32[]{:S(2)}) collective-permute-start(bf16[1024,128]{1,0:T(8,128)(2,1)S(1)} %added.3), channel_id=1, source_target_pairs={{0,96},{32,0},{64,32},{96,64},{1,97},{33,1},{65,33},{97,65},{2,98}... | collective-permute-start | bytes 786440 | tf_op jit(solution)/shard_map/pre_act_exchange/ppermute | solution.py:453
  116.9 1.1 convert_add_fusion.1
  118.0 8.4 %collective-permute-done.1.up = bf16[1024,128]{1,0:T(8,128)(2,1)S(1)} collective-permute-done((bf16[1024,128]{1,0:T(8,128)(2,1)S(1)}, bf16[1024,128]{1,0:T(8,128)(2,1)S(1)}, u32[]{:S(2)}, u32[]{:S(2)}) %collective-permute-start.1) | collective-permute-done | bytes 262176 | tf_op jit(solution)/shard_map/pre_act_exchange/ppermute | solution.py:453
  127.2 2.7 %collective-permute-start.7 = (bf16[1024,128]{1,0:T(8,128)(2,1)S(1)}, bf16[1024,128]{1,0:T(8,128)(2,1)S(1)}, u32[]{:S(2)}, u32[]{:S(2)}) collective-permute-start(bf16[1024,128]{1,0:T(8,128)(2,1)S(1)} %get-tuple-element.58), channel_id=1, source_target_pairs={{0,96},{32,0},{64,32},{96,64},{1,97},{33,1},{65,33},{97,65},{2,98}... | collective-permute-start | bytes 786440 | tf_op jit(solution)/shard_map/slope_exchange/ppermute | solution.py:453
  129.9 2.7 %collective-permute-start.6 = (bf16[1024,128]{1,0:T(8,128)(2,1)S(1)}, bf16[1024,128]{1,0:T(8,128)(2,1)S(1)}, u32[]{:S(2)}, u32[]{:S(2)}) collective-permute-start(bf16[1024,128]{1,0:T(8,128)(2,1)S(1)} %get-tuple-element.51), channel_id=1, source_target_pairs={{0,96},{32,0},{64,32},{96,64},{1,97},{33,1},{65,33},{97,65},{2,98}... | collective-permute-start | bytes 786440 | tf_op jit(solution)/shard_map/slope_exchange/ppermute | solution.py:453
  132.6 0.8 fusion
  134.8 1.0 copy-done.7
  136.6 1.7 collective-permute-start.13
  138.3 0.8 collective-permute-done.9
  139.9 2.0 %collective-permute-done.10 = bf16[512,128]{1,0:T(8,128)(2,1)S(1)} collective-permute-done((bf16[512,128]{1,0:T(8,128)(2,1)S(1)}, bf16[512,128]{1,0:T(8,128)(2,1)S(1)}, u32[]{:S(2)}, u32[]{:S(2)}) %collective-permute-start.10) | collective-permute-done | bytes 131104 | tf_op jit(solution)/shard_map/second_layer/ppermute | solution.py:453
  142.0 6.3 %collective-permute-start.11 = (bf16[16,80,128]{2,1,0:T(8,128)(2,1)S(1)}, bf16[16,80,128]{2,1,0:T(8,128)(2,1)S(1)}, u32[]{:S(2)}, u32[]{:S(2)}) collective-permute-start(bf16[16,80,128]{2,1,0:T(8,128)(2,1)S(1)} %get-tuple-element.61), channel_id=1, source_target_pairs={{0,1},{1,0},{2,3},{3,2},{4,5},{5,4},{6,7},{7,6},{8,9},{9,8},{10,11... | collective-permute-start | bytes 983048 | tf_op jit(solution)/shard_map/gradients/ppermute | solution.py:525
  149.1 2.8 %collective-permute-start.14 = (bf16[16,16,128]{2,1,0:T(8,128)(2,1)S(1)}, bf16[16,16,128]{2,1,0:T(8,128)(2,1)S(1)}, u32[]{:S(2)}, u32[]{:S(2)}) collective-permute-start(bf16[16,16,128]{2,1,0:T(8,128)(2,1)S(1)} %get-tuple-element.63), channel_id=1, source_target_pairs={{0,1},{1,0},{2,3},{3,2},{4,5},{5,4},{6,7},{7,6},{8,9},{9,8},{10,11... | collective-permute-start | bytes 196616 | tf_op jit(solution)/shard_map/gradients/ppermute | solution.py:525
  151.9 0.9 collective-permute-done.14.got_far
  152.9 15.3 %all_to_all.21.got_ref = bf16[16,96,128]{2,1,0:T(8,128)(2,1)S(1)} all-to-all(bf16[16,96,128]{2,1,0:T(8,128)(2,1)S(1)} %joined.1), channel_id=1, replica_groups={{0,2,4,6,8,10,12,14,16,18,20,22,24,26,28,30},{1,3,5,7,9,11,13,15,17,19,..., dimensions={0} | all-to-all | bytes 786432 | tf_op jit(solution)/shard_map/gradients/all_to_all | solution.py:528
  168.2 0.8 sum_and_spread.1
  169.0 3.6 %all-to-all-start.3 = ((bf16[16,96,128]{2,1,0:T(8,128)(2,1)}), bf16[16,96,128]{2,1,0:T(8,128)(2,1)S(1)}, u32[]{:S(2)}, u32[]{:S(2)}) async-start(bf16[16,96,128]{2,1,0:T(8,128)(2,1)} %sum_and_spread.1), calls=%async_computation.3 | async-start | bytes 786432 | tf_op jit(solution)/shard_map/gradients/all_to_all | solution.py:528
  173.8 4.1 %collective-permute-done.15 = bf16[512,128]{1,0:T(8,128)(2,1)S(1)} collective-permute-done((bf16[512,128]{1,0:T(8,128)(2,1)S(1)}, bf16[512,128]{1,0:T(8,128)(2,1)S(1)}, u32[]{:S(2)}, u32[]{:S(2)}) %collective-permute-start.15) | collective-permute-done | bytes 131104 | tf_op jit(solution)/shard_map/second_layer/ppermute | solution.py:453
  178.6 2.4 %all-to-all-done.3.mine_ref = bf16[16,96,128]{2,1,0:T(8,128)(2,1)S(1)} async-done(((bf16[16,96,128]{2,1,0:T(8,128)(2,1)}), bf16[16,96,128]{2,1,0:T(8,128)(2,1)S(1)}, u32[]{:S(2)}, u32[]{:S(2)}) %all-to-all-start.3) | async-done | bytes 393248 | tf_op jit(solution)/shard_map/gradients/all_to_all | solution.py:528
  181.0 2.6 %collective-permute-start.17 = (bf16[16,96,128]{2,1,0:T(8,128)(2,1)S(1)}, bf16[16,96,128]{2,1,0:T(8,128)(2,1)S(1)}, u32[]{:S(2)}, u32[]{:S(2)}) collective-permute-start(bf16[16,96,128]{2,1,0:T(8,128)(2,1)S(1)} %all-to-all-done.3.mine_ref), channel_id=1, source_target_pairs={{0,1},{1,0},{2,3},{3,2},{4,5},{5,4},{6,7},{7,6},{8,9},{9,8},{10,11... | collective-permute-start | bytes 1179656 | tf_op jit(solution)/shard_map/gradients/ppermute | solution.py:525
  184.9 1.8 finish.1
  (67 shorter events, 11.5 us)
Async XLA Ops:
  0.6 40.5 %copy-start = (bf16[512,512]{1,0:T(8,128)(2,1)S(1)}, bf16[512,512]{1,0:T(8,128)(2,1)}, u32[]{:S(2)}) copy-start(bf16[512,512]{1,0:T(8,128)(2,1)} %param.21) | copy-start | bytes 1572868
  32.3 5.0 %copy-start.6 = (s32[512,10]{0,1:T(8,128)S(1)}, s32[512,10]{0,1:T(8,128)}, u32[]{:S(2)}) copy-start(s32[512,10]{0,1:T(8,128)} %param.15) | copy-start | bytes 61444
  32.3 5.3 %copy-start.5 = (s32[2048,15]{0,1:T(8,128)S(1)}, s32[2048,15]{0,1:T(8,128)}, u32[]{:S(2)}) copy-start(s32[2048,15]{0,1:T(8,128)} %param.14) | copy-start | bytes 368644
  32.3 55.4 %all-to-all-start.1 = ((bf16[32,256,256]{2,1,0:T(8,128)(2,1)}), bf16[32,256,256]{2,1,0:T(8,128)(2,1)}, u32[]{:S(2)}, u32[]{:S(2)}) async-start(bf16[32,256,256]{2,1,0:T(8,128)(2,1)} %bitcast.23), calls=%async_computation.1 | async-start | bytes 8388608 | tf_op jit(solution)/shard_map/rows/all_to_all | solution.py:456
  38.1 3.1 %copy-start.3 = (bf16[128,512]{1,0:T(8,128)(2,1)S(1)}, bf16[128,512]{1,0:T(8,128)(2,1)}, u32[]{:S(2)}) copy-start(bf16[128,512]{1,0:T(8,128)(2,1)} %param.20) | copy-start | bytes 393220
  38.1 3.4 %copy-start.4 = (bf16[128,512]{1,0:T(8,128)(2,1)S(1)}, bf16[128,512]{1,0:T(8,128)(2,1)}, u32[]{:S(2)}) copy-start(bf16[128,512]{1,0:T(8,128)(2,1)} %param.19) | copy-start | bytes 393220
  41.2 1.4 copy-start.1
  87.7 22.2 %copy-start.8 = (bf16[128]{0:T(256)(128)(2,1)S(1)}, bf16[128]{0:T(256)(128)(2,1)}, u32[]{:S(2)}) copy-start(bf16[128]{0:T(256)(128)(2,1)} %param.18) | copy-start | bytes 772
  106.0 7.8 %collective-permute-start = (bf16[1024,128]{1,0:T(8,128)(2,1)}, bf16[1024,128]{1,0:T(8,128)(2,1)S(1)}, u32[]{:S(2)}, u32[]{:S(2)}) collective-permute-start(bf16[1024,128]{1,0:T(8,128)(2,1)} %get-tuple-element.45), channel_id=1, source_target_pairs={{0,32},{32,64},{64,96},{96,0},{1,33},{33,65},{65,97},{97,1},{2,34}... | collective-permute-start | bytes 786440 | tf_op jit(solution)/shard_map/pre_act_exchange/ppermute | solution.py:453
  107.7 6.2 %collective-permute-start.4 = (bf16[1024,128]{1,0:T(8,128)(2,1)}, bf16[1024,128]{1,0:T(8,128)(2,1)S(1)}, u32[]{:S(2)}, u32[]{:S(2)}) collective-permute-start(bf16[1024,128]{1,0:T(8,128)(2,1)} %get-tuple-element.55), channel_id=1, source_target_pairs={{0,96},{32,0},{64,32},{96,64},{1,97},{33,1},{65,33},{97,65},{2,98}... | collective-permute-start | bytes 786440 | tf_op jit(solution)/shard_map/pre_act_exchange/ppermute | solution.py:453
  109.9 8.1 %collective-permute-start.2 = (bf16[1024,128]{1,0:T(8,128)(2,1)S(1)}, bf16[1024,128]{1,0:T(8,128)(2,1)S(1)}, u32[]{:S(2)}, u32[]{:S(2)}) collective-permute-start(bf16[1024,128]{1,0:T(8,128)(2,1)S(1)} %get-tuple-element.46), channel_id=1, source_target_pairs={{0,96},{32,0},{64,32},{96,64},{1,97},{33,1},{65,33},{97,65},{2,98}... | collective-permute-start | bytes 786440 | tf_op jit(solution)/shard_map/pre_act_exchange/ppermute | solution.py:453
  111.3 15.6 %collective-permute-start.3 = (bf16[1024,128]{1,0:T(8,128)(2,1)S(1)}, bf16[1024,128]{1,0:T(8,128)(2,1)S(1)}, u32[]{:S(2)}, u32[]{:S(2)}) collective-permute-start(bf16[1024,128]{1,0:T(8,128)(2,1)S(1)} %get-tuple-element.53), channel_id=1, source_target_pairs={{0,32},{32,64},{64,96},{96,0},{1,33},{33,65},{65,97},{97,1},{2,34}... | collective-permute-start | bytes 786440 | tf_op jit(solution)/shard_map/pre_act_exchange/ppermute | solution.py:453
  113.8 12.6 %collective-permute-start.1 = (bf16[1024,128]{1,0:T(8,128)(2,1)S(1)}, bf16[1024,128]{1,0:T(8,128)(2,1)S(1)}, u32[]{:S(2)}, u32[]{:S(2)}) collective-permute-start(bf16[1024,128]{1,0:T(8,128)(2,1)S(1)} %added.2), channel_id=1, source_target_pairs={{0,32},{32,64},{64,96},{96,0},{1,33},{33,65},{65,97},{97,1},{2,34}... | collective-permute-start | bytes 786440 | tf_op jit(solution)/shard_map/pre_act_exchange/ppermute | solution.py:453
  114.0 12.8 %collective-permute-start.5 = (bf16[1024,128]{1,0:T(8,128)(2,1)S(1)}, bf16[1024,128]{1,0:T(8,128)(2,1)S(1)}, u32[]{:S(2)}, u32[]{:S(2)}) collective-permute-start(bf16[1024,128]{1,0:T(8,128)(2,1)S(1)} %added.3), channel_id=1, source_target_pairs={{0,96},{32,0},{64,32},{96,64},{1,97},{33,1},{65,33},{97,65},{2,98}... | collective-permute-start | bytes 786440 | tf_op jit(solution)/shard_map/pre_act_exchange/ppermute | solution.py:453
  126.4 6.1 %copy-start.2 = (bf16[512,2048]{1,0:T(8,128)(2,1)S(1)}, bf16[512,2048]{1,0:T(8,128)(2,1)}, u32[]{:S(2)}) copy-start(bf16[512,2048]{1,0:T(8,128)(2,1)} %copy-done.1) | copy-start | bytes 6291460
  126.7 11.5 %collective-permute-start.8 = (bf16[1024,128]{1,0:T(8,128)(2,1)S(1)}, bf16[1024,128]{1,0:T(8,128)(2,1)S(1)}, u32[]{:S(2)}, u32[]{:S(2)}) collective-permute-start(bf16[1024,128]{1,0:T(8,128)(2,1)S(1)} %get-tuple-element.51), channel_id=1, source_target_pairs={{0,32},{32,64},{64,96},{96,0},{1,33},{33,65},{65,97},{97,1},{2,34}... | collective-permute-start | bytes 786440 | tf_op jit(solution)/shard_map/slope_exchange/ppermute | solution.py:453
  127.2 9.4 %collective-permute-start.7 = (bf16[1024,128]{1,0:T(8,128)(2,1)S(1)}, bf16[1024,128]{1,0:T(8,128)(2,1)S(1)}, u32[]{:S(2)}, u32[]{:S(2)}) collective-permute-start(bf16[1024,128]{1,0:T(8,128)(2,1)S(1)} %get-tuple-element.58), channel_id=1, source_target_pairs={{0,96},{32,0},{64,32},{96,64},{1,97},{33,1},{65,33},{97,65},{2,98}... | collective-permute-start | bytes 786440 | tf_op jit(solution)/shard_map/slope_exchange/ppermute | solution.py:453
  129.9 9.3 %collective-permute-start.9 = (bf16[1024,128]{1,0:T(8,128)(2,1)S(1)}, bf16[1024,128]{1,0:T(8,128)(2,1)S(1)}, u32[]{:S(2)}, u32[]{:S(2)}) collective-permute-start(bf16[1024,128]{1,0:T(8,128)(2,1)S(1)} %get-tuple-element.58), channel_id=1, source_target_pairs={{0,32},{32,64},{64,96},{96,0},{1,33},{33,65},{65,97},{97,1},{2,34}... | collective-permute-start | bytes 786440 | tf_op jit(solution)/shard_map/slope_exchange/ppermute | solution.py:453
  129.9 9.3 %collective-permute-start.6 = (bf16[1024,128]{1,0:T(8,128)(2,1)S(1)}, bf16[1024,128]{1,0:T(8,128)(2,1)S(1)}, u32[]{:S(2)}, u32[]{:S(2)}) collective-permute-start(bf16[1024,128]{1,0:T(8,128)(2,1)S(1)} %get-tuple-element.51), channel_id=1, source_target_pairs={{0,96},{32,0},{64,32},{96,64},{1,97},{33,1},{65,33},{97,65},{2,98}... | collective-permute-start | bytes 786440 | tf_op jit(solution)/shard_map/slope_exchange/ppermute | solution.py:453
  134.2 1.6 copy-start.7
  134.6 7.3 %collective-permute-start.10 = (bf16[512,128]{1,0:T(8,128)(2,1)S(1)}, bf16[512,128]{1,0:T(8,128)(2,1)S(1)}, u32[]{:S(2)}, u32[]{:S(2)}) collective-permute-start(bf16[512,128]{1,0:T(8,128)(2,1)S(1)} %get-tuple-element.77), channel_id=1, source_target_pairs={{0,32},{32,64},{64,96},{96,0},{1,33},{33,65},{65,97},{97,1},{2,34}... | collective-permute-start | bytes 393224 | tf_op jit(solution)/shard_map/second_layer/ppermute | solution.py:453
  136.6 11.8 %collective-permute-start.13 = (bf16[1024,128]{1,0:T(8,128)(2,1)S(1)}, bf16[1024,128]{1,0:T(8,128)(2,1)S(1)}, u32[]{:S(2)}, u32[]{:S(2)}) collective-permute-start(bf16[1024,128]{1,0:T(8,128)(2,1)S(1)} %collective-permute-done.7), channel_id=1, source_target_pairs={{0,96},{32,0},{64,32},{96,64},{1,97},{33,1},{65,33},{97,65},{2,98}... | collective-permute-start | bytes 786440 | tf_op jit(solution)/shard_map/slope_exchange/ppermute | solution.py:453
  138.3 10.0 %collective-permute-start.12 = (bf16[1024,128]{1,0:T(8,128)(2,1)S(1)}, bf16[1024,128]{1,0:T(8,128)(2,1)S(1)}, u32[]{:S(2)}, u32[]{:S(2)}) collective-permute-start(bf16[1024,128]{1,0:T(8,128)(2,1)S(1)} %collective-permute-done.8), channel_id=1, source_target_pairs={{0,32},{32,64},{64,96},{96,0},{1,33},{33,65},{65,97},{97,1},{2,34}... | collective-permute-start | bytes 786440 | tf_op jit(solution)/shard_map/slope_exchange/ppermute | solution.py:453
  142.0 10.8 %collective-permute-start.11 = (bf16[16,80,128]{2,1,0:T(8,128)(2,1)S(1)}, bf16[16,80,128]{2,1,0:T(8,128)(2,1)S(1)}, u32[]{:S(2)}, u32[]{:S(2)}) collective-permute-start(bf16[16,80,128]{2,1,0:T(8,128)(2,1)S(1)} %get-tuple-element.61), channel_id=1, source_target_pairs={{0,1},{1,0},{2,3},{3,2},{4,5},{5,4},{6,7},{7,6},{8,9},{9,8},{10,11... | collective-permute-start | bytes 983048 | tf_op jit(solution)/shard_map/gradients/ppermute | solution.py:525
  149.1 3.7 %collective-permute-start.14 = (bf16[16,16,128]{2,1,0:T(8,128)(2,1)S(1)}, bf16[16,16,128]{2,1,0:T(8,128)(2,1)S(1)}, u32[]{:S(2)}, u32[]{:S(2)}) collective-permute-start(bf16[16,16,128]{2,1,0:T(8,128)(2,1)S(1)} %get-tuple-element.63), channel_id=1, source_target_pairs={{0,1},{1,0},{2,3},{3,2},{4,5},{5,4},{6,7},{7,6},{8,9},{9,8},{10,11... | collective-permute-start | bytes 196616 | tf_op jit(solution)/shard_map/gradients/ppermute | solution.py:525
  169.0 12.0 %all-to-all-start.3 = ((bf16[16,96,128]{2,1,0:T(8,128)(2,1)}), bf16[16,96,128]{2,1,0:T(8,128)(2,1)S(1)}, u32[]{:S(2)}, u32[]{:S(2)}) async-start(bf16[16,96,128]{2,1,0:T(8,128)(2,1)} %sum_and_spread.1), calls=%async_computation.3 | async-start | bytes 786432 | tf_op jit(solution)/shard_map/gradients/all_to_all | solution.py:528
  172.6 5.4 %collective-permute-start.15 = (bf16[512,128]{1,0:T(8,128)(2,1)S(1)}, bf16[512,128]{1,0:T(8,128)(2,1)S(1)}, u32[]{:S(2)}, u32[]{:S(2)}) collective-permute-start(bf16[512,128]{1,0:T(8,128)(2,1)S(1)} %get-tuple-element.76), channel_id=1, source_target_pairs={{0,64},{32,96},{64,0},{96,32},{1,65},{33,97},{65,1},{97,33},{2,66}... | collective-permute-start | bytes 393224 | tf_op jit(solution)/shard_map/second_layer/ppermute | solution.py:453
  173.0 5.6 %collective-permute-start.16 = (bf16[512,128]{1,0:T(8,128)(2,1)S(1)}, bf16[512,128]{1,0:T(8,128)(2,1)S(1)}, u32[]{:S(2)}, u32[]{:S(2)}) collective-permute-start(bf16[512,128]{1,0:T(8,128)(2,1)S(1)} %get-tuple-element.75), channel_id=1, source_target_pairs={{0,96},{32,0},{64,32},{96,64},{1,97},{33,1},{65,33},{97,65},{2,98}... | collective-permute-start | bytes 393224 | tf_op jit(solution)/shard_map/second_layer/ppermute | solution.py:453
  181.0 4.0 %collective-permute-start.17 = (bf16[16,96,128]{2,1,0:T(8,128)(2,1)S(1)}, bf16[16,96,128]{2,1,0:T(8,128)(2,1)S(1)}, u32[]{:S(2)}, u32[]{:S(2)}) collective-permute-start(bf16[16,96,128]{2,1,0:T(8,128)(2,1)S(1)} %all-to-all-done.3.mine_ref), channel_id=1, source_target_pairs={{0,1},{1,0},{2,3},{3,2},{4,5},{5,4},{6,7},{7,6},{8,9},{9,8},{10,11... | collective-permute-start | bytes 1179656 | tf_op jit(solution)/shard_map/gradients/ppermute | solution.py:525

commit v8 on v7

--- a/solution.py
+++ b/solution.py
@@ -501,9 +501,12 @@
         passing_up = shift(far[0], 1)
         passing_down = shift(far[1], -1)
         down_0 = shift(below[0], -1)
-        up_1 = shift(above[1], 1)
-        up_0 = shift(added(above[0], passing_up), 1)
-        down_1 = shift(added(below[1], passing_down), -1)
+        first = added(above[0], passing_up)
+        up_0 = shift(first, 1)
+        passing_down, _ = lax.optimization_barrier((passing_down, first))
+        second, after = lax.optimization_barrier((added(below[1], passing_down), above[1]))
+        down_1 = shift(second, -1)
+        up_1 = shift(after, 1)
         hiddens, slopes = [], []
         for half, (up, down) in enumerate([(up_0, down_0), (up_1, down_1)]):
             base = own[half].astype(F32) + bias_hidden.astype(F32)

time: 187 us -> 187 us (level)
  starting transfers between devices: 37.1 us -> 44.2 us
  waiting for transfers between devices: 53.4 us -> 49.3 us
  blocking collectives: 31.2 us -> 28 us
    ppermute x3, starting transfers between devices: 11.7 us -> 18 us  [swap(): return lax.ppermute(value, 'wide', [(i, i ^ 1) for i in range(peers)])]
    all_to_all x1, blocking collectives: 15.3 us -> 12.1 us  [between_chips(): lax.all_to_all(value, 'wide', split_axis=0, concat_axis=0, axis_index_gro...]
    ppermute x15, waiting for transfers between devices: 18.5 us -> 15.6 us  [shift(): lax.ppermute(value, 'blk', [(i, (i + by) % quarters) for i in range(quart...]
  transfers between devices with their start and end apart: 20 -> 20, of which waited for: 10 -> 11; matrix products, arithmetic and copies ran while one was open for 5% -> 5% of each run, Pallas kernels for 9% -> 9%
where the time goes in v8:
time: 187 us; the launch traced here: 186 us
  Pallas kernels  53.2 us (28%)
  waiting for transfers between devices  49.3 us (26%)
  starting transfers between devices  44.2 us (24%)
  blocking collectives  28 us (15%)
  matrix products  5.53 us (3%)
  local copies, waits for them, and re-layouts  3.09 us (2%)
  other arithmetic  2.07 us (1%)
    all_to_all x1, waiting for transfers between devices, exchange(): lax.all_to_all(value, 'wide', split_axis=0, concat_axis=0, tiled=True)  31.1 us
    pallas_call x1, Pallas kernels, first_layer(): pl.pallas_call(functools.partial(layer_kernel, list_width), grid_spec=plt...  18.3 us
    ppermute x3, starting transfers between devices, swap(): return lax.ppermute(value, 'wide', [(i, i ^ 1) for i in range(peers)])  18 us
    ppermute x15, starting transfers between devices, shift(): lax.ppermute(value, 'blk', [(i, (i + by) % quarters) for i in range(quart...  17.7 us
    all_to_all x1, blocking collectives, exchange(): lax.all_to_all(value, 'wide', split_axis=0, concat_axis=0, tiled=True)  16 us
    pallas_call x2, Pallas kernels, neighbour_counts(): pl.pallas_call(count_kernel, grid=(targets // 16 // block_groups,), in_sp...  15.7 us
    ppermute x15, waiting for transfers between devices, shift(): lax.ppermute(value, 'blk', [(i, (i + by) % quarters) for i in range(quart...  15.6 us
    pallas_call x1, Pallas kernels, gather_rows(): pl.pallas_call(gather_kernel, grid=(total // rows,), in_specs=[pl.BlockSp...  12.7 us
  transfers between devices with their start and end apart: 20, of which 11 were waited for; matrix products, arithmetic and copies ran while one was open for 5% of the time, Pallas kernels for 9%

profile of v8, /device:TPU:1, one launch (start us, length us, event | category | flops | bytes accessed | tf_op | source)
XLA Modules:
  0.0 186.5 jit_solution(6221137783360906292)
XLA Ops:
  0.6 2.9 %request_table.1 = (s32[32,1,256]{2,1,0:T(1,128)}, s32[32,128]{1,0:T(8,128)}) custom-call(s32[32,128]{1,0:T(8,128)} %bitcast.25, s32[32,128]{1,0:T(8,128)} %bitcast.26), custom_call_target="tpu_custom_call" | custom-call | tf_op jit(solution)/shard_map/requests/request_table/pallas_call | solution.py:66
  3.6 16.0 %all_to_all.20 = s32[32,1,256]{2,1,0:T(1,128)} all-to-all(s32[32,1,256]{2,1,0:T(1,128)} %get-tuple-element.43), channel_id=1, replica_groups=mesh['blk'=4,'wide'=32] {'wide'}, dimensions={0} | all-to-all | bytes 65536 | tf_op jit(solution)/shard_map/requests/all_to_all | solution.py:456
  19.5 12.7 %gather_rows.1 = bf16[8192,256]{1,0:T(8,128)(2,1)} custom-call(s32[8192]{0:T(1024)} %bitcast.24, bf16[8192,256]{1,0:T(8,128)(2,1)} %table_ref.1), custom_call_target="tpu_custom_call" | custom-call | tf_op jit(solution)/shard_map/rows/gather_rows/pallas_call | solution.py:200
  32.3 5.0 %all-to-all-start.1 = ((bf16[32,256,256]{2,1,0:T(8,128)(2,1)}), bf16[32,256,256]{2,1,0:T(8,128)(2,1)}, u32[]{:S(2)}, u32[]{:S(2)}) async-start(bf16[32,256,256]{2,1,0:T(8,128)(2,1)} %bitcast.23), calls=%async_computation.1 | async-start | bytes 8388608 | tf_op jit(solution)/shard_map/rows/all_to_all | solution.py:456
  38.5 2.6 %neighbour_counts.3 = bf16[512,2048]{1,0:T(8,128)(2,1)S(1)} custom-call(s32[32,256]{1,0:T(8,128)S(1)} %reshape.46.idx_ref), custom_call_target="tpu_custom_call" | custom-call | flops 536870912 | bytes 2097152 | tf_op jit(solution)/shard_map/beside_rows/neighbour_counts/pallas_call | solution.py:112
  43.3 13.1 %neighbour_counts.2.counts_ref = bf16[2048,4096]{1,0:T(8,128)(2,1)} custom-call(s32[128,256]{1,0:T(8,128)S(1)} %reshape.45.idx_ref), custom_call_target="tpu_custom_call" | custom-call | flops 4294967296 | bytes 16777216 | tf_op jit(solution)/shard_map/beside_rows/neighbour_counts/pallas_call | solution.py:112
  56.5 31.1 %all-to-all-done.1 = bf16[32,256,256]{2,1,0:T(8,128)(2,1)} async-done(((bf16[32,256,256]{2,1,0:T(8,128)(2,1)}), bf16[32,256,256]{2,1,0:T(8,128)(2,1)}, u32[]{:S(2)}, u32[]{:S(2)}) %all-to-all-start.1) | async-done | bytes 4194336 | tf_op jit(solution)/shard_map/rows/all_to_all | solution.py:456
  87.7 18.3 %first_layer.1 = (bf16[1024,128]{1,0:T(8,128)(2,1)}, bf16[1024,128]{1,0:T(8,128)(2,1)}, bf16[1024,128]{1,0:T(8,128)(2,1)S(1)}, bf16[1024,128]{1,0:T(8,128)(2,1)S...) custom-call(s32[4096]{0:T(1024)} %bitcast.27, ...), custom_call_target="tpu_custom_call" | custom-call | tf_op jit(solution)/shard_map/first_layer/first_layer/pallas_call | solution.py:274
  106.0 1.7 collective-permute-start
  107.7 2.2 %collective-permute-start.3 = (bf16[1024,128]{1,0:T(8,128)(2,1)}, bf16[1024,128]{1,0:T(8,128)(2,1)S(1)}, u32[]{:S(2)}, u32[]{:S(2)}) collective-permute-start(bf16[1024,128]{1,0:T(8,128)(2,1)} %get-tuple-element.57), channel_id=1, source_target_pairs={{0,96},{32,0},{64,32},{96,64},{1,97},{33,1},{65,33},{97,65},{2,98}... | collective-permute-start | bytes 786440 | tf_op jit(solution)/shard_map/pre_act_exchange/ppermute | solution.py:453
  109.9 1.4 collective-permute-start.2
  111.3 2.5 %collective-permute-done.right = bf16[1024,128]{1,0:T(8,128)(2,1)S(1)} collective-permute-done((bf16[1024,128]{1,0:T(8,128)(2,1)}, bf16[1024,128]{1,0:T(8,128)(2,1)S(1)}, u32[]{:S(2)}, u32[]{:S(2)}) %collective-permute-start) | collective-permute-done | bytes 262176 | tf_op jit(solution)/shard_map/pre_act_exchange/ppermute | solution.py:453
  114.0 1.2 collective-permute-start.4
  115.2 1.8 collective-permute-start.5
  117.0 1.1 convert_add_fusion.1
  118.1 2.2 %collective-permute-done.1.up = bf16[1024,128]{1,0:T(8,128)(2,1)S(1)} collective-permute-done((bf16[1024,128]{1,0:T(8,128)(2,1)S(1)}, bf16[1024,128]{1,0:T(8,128)(2,1)S(1)}, u32[]{:S(2)}, u32[]{:S(2)}) %collective-permute-start.1) | collective-permute-done | bytes 262176 | tf_op jit(solution)/shard_map/pre_act_exchange/ppermute | solution.py:453
  120.7 3.2 %collective-permute-done.4.up = bf16[1024,128]{1,0:T(8,128)(2,1)S(1)} collective-permute-done((bf16[1024,128]{1,0:T(8,128)(2,1)S(1)}, bf16[1024,128]{1,0:T(8,128)(2,1)S(1)}, u32[]{:S(2)}, u32[]{:S(2)}) %collective-permute-start.4) | collective-permute-done | bytes 262176 | tf_op jit(solution)/shard_map/pre_act_exchange/ppermute | solution.py:453
  124.3 2.9 %collective-permute-start.7 = (bf16[1024,128]{1,0:T(8,128)(2,1)S(1)}, bf16[1024,128]{1,0:T(8,128)(2,1)S(1)}, u32[]{:S(2)}, u32[]{:S(2)}) collective-permute-start(bf16[1024,128]{1,0:T(8,128)(2,1)S(1)} %get-tuple-element.64), channel_id=1, source_target_pairs={{0,96},{32,0},{64,32},{96,64},{1,97},{33,1},{65,33},{97,65},{2,98}... | collective-permute-start | bytes 786440 | tf_op jit(solution)/shard_map/slope_exchange/ppermute | solution.py:453
  127.2 2.7 %collective-permute-start.6 = (bf16[1024,128]{1,0:T(8,128)(2,1)S(1)}, bf16[1024,128]{1,0:T(8,128)(2,1)S(1)}, u32[]{:S(2)}, u32[]{:S(2)}) collective-permute-start(bf16[1024,128]{1,0:T(8,128)(2,1)S(1)} %get-tuple-element.54), channel_id=1, source_target_pairs={{0,96},{32,0},{64,32},{96,64},{1,97},{33,1},{65,33},{97,65},{2,98}... | collective-permute-start | bytes 786440 | tf_op jit(solution)/shard_map/slope_exchange/ppermute | solution.py:453
  132.1 1.0 copy-done.7
  133.9 1.7 collective-permute-start.13
  137.1 1.5 collective-permute-done.10
  138.7 9.9 %collective-permute-start.11 = (bf16[16,80,128]{2,1,0:T(8,128)(2,1)S(1)}, bf16[16,80,128]{2,1,0:T(8,128)(2,1)S(1)}, u32[]{:S(2)}, u32[]{:S(2)}) collective-permute-start(bf16[16,80,128]{2,1,0:T(8,128)(2,1)S(1)} %get-tuple-element.67), channel_id=1, source_target_pairs={{0,1},{1,0},{2,3},{3,2},{4,5},{5,4},{6,7},{7,6},{8,9},{9,8},{10,11... | collective-permute-start | bytes 983048 | tf_op jit(solution)/shard_map/gradients/ppermute | solution.py:528
  149.4 5.5 %collective-permute-start.14 = (bf16[16,16,128]{2,1,0:T(8,128)(2,1)S(1)}, bf16[16,16,128]{2,1,0:T(8,128)(2,1)S(1)}, u32[]{:S(2)}, u32[]{:S(2)}) collective-permute-start(bf16[16,16,128]{2,1,0:T(8,128)(2,1)S(1)} %get-tuple-element.69), channel_id=1, source_target_pairs={{0,1},{1,0},{2,3},{3,2},{4,5},{5,4},{6,7},{7,6},{8,9},{9,8},{10,11... | collective-permute-start | bytes 196616 | tf_op jit(solution)/shard_map/gradients/ppermute | solution.py:528
  155.9 12.1 %all_to_all.21.got_ref = bf16[16,96,128]{2,1,0:T(8,128)(2,1)S(1)} all-to-all(bf16[16,96,128]{2,1,0:T(8,128)(2,1)S(1)} %joined.1), channel_id=1, replica_groups={{0,2,4,6,8,10,12,14,16,18,20,22,24,26,28,30},{1,3,5,7,9,11,13,15,17,19,..., dimensions={0} | all-to-all | bytes 786432 | tf_op jit(solution)/shard_map/gradients/all_to_all | solution.py:531
  168.8 3.6 %all-to-all-start.3 = ((bf16[16,96,128]{2,1,0:T(8,128)(2,1)}), bf16[16,96,128]{2,1,0:T(8,128)(2,1)S(1)}, u32[]{:S(2)}, u32[]{:S(2)}) async-start(bf16[16,96,128]{2,1,0:T(8,128)(2,1)} %sum_and_spread.1), calls=%async_computation.3 | async-start | bytes 786432 | tf_op jit(solution)/shard_map/gradients/all_to_all | solution.py:531
  172.8 1.4 collective-permute-start.16
  174.2 3.5 %collective-permute-done.15 = bf16[512,128]{1,0:T(8,128)(2,1)S(1)} collective-permute-done((bf16[512,128]{1,0:T(8,128)(2,1)S(1)}, bf16[512,128]{1,0:T(8,128)(2,1)S(1)}, u32[]{:S(2)}, u32[]{:S(2)}) %collective-permute-start.15) | collective-permute-done | bytes 131104 | tf_op jit(solution)/shard_map/second_layer/ppermute | solution.py:453
  177.7 1.8 collective-permute-done.16
  179.5 1.2 all-to-all-done.3.mine_ref
  180.7 2.6 %collective-permute-start.17 = (bf16[16,96,128]{2,1,0:T(8,128)(2,1)S(1)}, bf16[16,96,128]{2,1,0:T(8,128)(2,1)S(1)}, u32[]{:S(2)}, u32[]{:S(2)}) collective-permute-start(bf16[16,96,128]{2,1,0:T(8,128)(2,1)S(1)} %all-to-all-done.3.mine_ref), channel_id=1, source_target_pairs={{0,1},{1,0},{2,3},{3,2},{4,5},{5,4},{6,7},{7,6},{8,9},{9,8},{10,11... | collective-permute-start | bytes 1179656 | tf_op jit(solution)/shard_map/gradients/ppermute | solution.py:528
  184.7 1.8 finish.1
  (67 shorter events, 13.2 us)
Async XLA Ops:
  0.6 40.5 %copy-start = (bf16[512,512]{1,0:T(8,128)(2,1)S(1)}, bf16[512,512]{1,0:T(8,128)(2,1)}, u32[]{:S(2)}) copy-start(bf16[512,512]{1,0:T(8,128)(2,1)} %param.21) | copy-start | bytes 1572868
  32.3 5.0 %copy-start.6 = (s32[512,10]{0,1:T(8,128)S(1)}, s32[512,10]{0,1:T(8,128)}, u32[]{:S(2)}) copy-start(s32[512,10]{0,1:T(8,128)} %param.15) | copy-start | bytes 61444
  32.3 5.3 %copy-start.5 = (s32[2048,15]{0,1:T(8,128)S(1)}, s32[2048,15]{0,1:T(8,128)}, u32[]{:S(2)}) copy-start(s32[2048,15]{0,1:T(8,128)} %param.14) | copy-start | bytes 368644
  32.3 55.4 %all-to-all-start.1 = ((bf16[32,256,256]{2,1,0:T(8,128)(2,1)}), bf16[32,256,256]{2,1,0:T(8,128)(2,1)}, u32[]{:S(2)}, u32[]{:S(2)}) async-start(bf16[32,256,256]{2,1,0:T(8,128)(2,1)} %bitcast.23), calls=%async_computation.1 | async-start | bytes 8388608 | tf_op jit(solution)/shard_map/rows/all_to_all | solution.py:456
  38.1 3.1 %copy-start.3 = (bf16[128,512]{1,0:T(8,128)(2,1)S(1)}, bf16[128,512]{1,0:T(8,128)(2,1)}, u32[]{:S(2)}) copy-start(bf16[128,512]{1,0:T(8,128)(2,1)} %param.20) | copy-start | bytes 393220
  38.1 3.4 %copy-start.4 = (bf16[128,512]{1,0:T(8,128)(2,1)S(1)}, bf16[128,512]{1,0:T(8,128)(2,1)}, u32[]{:S(2)}) copy-start(bf16[128,512]{1,0:T(8,128)(2,1)} %param.19) | copy-start | bytes 393220
  41.2 1.4 copy-start.1
  87.7 22.2 %copy-start.8 = (bf16[128]{0:T(256)(128)(2,1)S(1)}, bf16[128]{0:T(256)(128)(2,1)}, u32[]{:S(2)}) copy-start(bf16[128]{0:T(256)(128)(2,1)} %param.18) | copy-start | bytes 772
  106.0 7.8 %collective-permute-start = (bf16[1024,128]{1,0:T(8,128)(2,1)}, bf16[1024,128]{1,0:T(8,128)(2,1)S(1)}, u32[]{:S(2)}, u32[]{:S(2)}) collective-permute-start(bf16[1024,128]{1,0:T(8,128)(2,1)} %get-tuple-element.48), channel_id=1, source_target_pairs={{0,32},{32,64},{64,96},{96,0},{1,33},{33,65},{65,97},{97,1},{2,34}... | collective-permute-start | bytes 786440 | tf_op jit(solution)/shard_map/pre_act_exchange/ppermute | solution.py:453
  107.7 6.2 %collective-permute-start.3 = (bf16[1024,128]{1,0:T(8,128)(2,1)}, bf16[1024,128]{1,0:T(8,128)(2,1)S(1)}, u32[]{:S(2)}, u32[]{:S(2)}) collective-permute-start(bf16[1024,128]{1,0:T(8,128)(2,1)} %get-tuple-element.57), channel_id=1, source_target_pairs={{0,96},{32,0},{64,32},{96,64},{1,97},{33,1},{65,33},{97,65},{2,98}... | collective-permute-start | bytes 786440 | tf_op jit(solution)/shard_map/pre_act_exchange/ppermute | solution.py:453
  109.9 8.2 %collective-permute-start.2 = (bf16[1024,128]{1,0:T(8,128)(2,1)S(1)}, bf16[1024,128]{1,0:T(8,128)(2,1)S(1)}, u32[]{:S(2)}, u32[]{:S(2)}) collective-permute-start(bf16[1024,128]{1,0:T(8,128)(2,1)S(1)} %get-tuple-element.49), channel_id=1, source_target_pairs={{0,96},{32,0},{64,32},{96,64},{1,97},{33,1},{65,33},{97,65},{2,98}... | collective-permute-start | bytes 786440 | tf_op jit(solution)/shard_map/pre_act_exchange/ppermute | solution.py:453
  113.8 6.5 %collective-permute-start.1 = (bf16[1024,128]{1,0:T(8,128)(2,1)S(1)}, bf16[1024,128]{1,0:T(8,128)(2,1)S(1)}, u32[]{:S(2)}, u32[]{:S(2)}) collective-permute-start(bf16[1024,128]{1,0:T(8,128)(2,1)S(1)} %added.2), channel_id=1, source_target_pairs={{0,32},{32,64},{64,96},{96,0},{1,33},{33,65},{65,97},{97,1},{2,34}... | collective-permute-start | bytes 786440 | tf_op jit(solution)/shard_map/pre_act_exchange/ppermute | solution.py:453
  114.0 10.0 %collective-permute-start.4 = (bf16[1024,128]{1,0:T(8,128)(2,1)S(1)}, bf16[1024,128]{1,0:T(8,128)(2,1)S(1)}, u32[]{:S(2)}, u32[]{:S(2)}) collective-permute-start(bf16[1024,128]{1,0:T(8,128)(2,1)S(1)} %get-tuple-element.60), channel_id=1, source_target_pairs={{0,32},{32,64},{64,96},{96,0},{1,33},{33,65},{65,97},{97,1},{2,34}... | collective-permute-start | bytes 786440 | tf_op jit(solution)/shard_map/pre_act_exchange/ppermute | solution.py:453
  115.2 8.8 %collective-permute-start.5 = (bf16[1024,128]{1,0:T(8,128)(2,1)S(1)}, bf16[1024,128]{1,0:T(8,128)(2,1)S(1)}, u32[]{:S(2)}, u32[]{:S(2)}) collective-permute-start(bf16[1024,128]{1,0:T(8,128)(2,1)S(1)} %added.3), channel_id=1, source_target_pairs={{0,96},{32,0},{64,32},{96,64},{1,97},{33,1},{65,33},{97,65},{2,98}... | collective-permute-start | bytes 786440 | tf_op jit(solution)/shard_map/pre_act_exchange/ppermute | solution.py:453
  120.3 9.5 %copy-start.2 = (bf16[512,2048]{1,0:T(8,128)(2,1)S(1)}, bf16[512,2048]{1,0:T(8,128)(2,1)}, u32[]{:S(2)}) copy-start(bf16[512,2048]{1,0:T(8,128)(2,1)} %copy-done.1) | copy-start | bytes 6291460
  120.7 15.0 %collective-permute-start.8 = (bf16[1024,128]{1,0:T(8,128)(2,1)S(1)}, bf16[1024,128]{1,0:T(8,128)(2,1)S(1)}, u32[]{:S(2)}, u32[]{:S(2)}) collective-permute-start(bf16[1024,128]{1,0:T(8,128)(2,1)S(1)} %get-tuple-element.54), channel_id=1, source_target_pairs={{0,32},{32,64},{64,96},{96,0},{1,33},{33,65},{65,97},{97,1},{2,34}... | collective-permute-start | bytes 786440 | tf_op jit(solution)/shard_map/slope_exchange/ppermute | solution.py:453
  124.3 9.6 %collective-permute-start.7 = (bf16[1024,128]{1,0:T(8,128)(2,1)S(1)}, bf16[1024,128]{1,0:T(8,128)(2,1)S(1)}, u32[]{:S(2)}, u32[]{:S(2)}) collective-permute-start(bf16[1024,128]{1,0:T(8,128)(2,1)S(1)} %get-tuple-element.64), channel_id=1, source_target_pairs={{0,96},{32,0},{64,32},{96,64},{1,97},{33,1},{65,33},{97,65},{2,98}... | collective-permute-start | bytes 786440 | tf_op jit(solution)/shard_map/slope_exchange/ppermute | solution.py:453
  127.2 9.1 %collective-permute-start.9 = (bf16[1024,128]{1,0:T(8,128)(2,1)S(1)}, bf16[1024,128]{1,0:T(8,128)(2,1)S(1)}, u32[]{:S(2)}, u32[]{:S(2)}) collective-permute-start(bf16[1024,128]{1,0:T(8,128)(2,1)S(1)} %get-tuple-element.64), channel_id=1, source_target_pairs={{0,32},{32,64},{64,96},{96,0},{1,33},{33,65},{65,97},{97,1},{2,34}... | collective-permute-start | bytes 786440 | tf_op jit(solution)/shard_map/slope_exchange/ppermute | solution.py:453
  127.2 9.1 %collective-permute-start.6 = (bf16[1024,128]{1,0:T(8,128)(2,1)S(1)}, bf16[1024,128]{1,0:T(8,128)(2,1)S(1)}, u32[]{:S(2)}, u32[]{:S(2)}) collective-permute-start(bf16[1024,128]{1,0:T(8,128)(2,1)S(1)} %get-tuple-element.54), channel_id=1, source_target_pairs={{0,96},{32,0},{64,32},{96,64},{1,97},{33,1},{65,33},{97,65},{2,98}... | collective-permute-start | bytes 786440 | tf_op jit(solution)/shard_map/slope_exchange/ppermute | solution.py:453
  131.5 1.6 copy-start.7
  132.0 6.7 %collective-permute-start.10 = (bf16[512,128]{1,0:T(8,128)(2,1)S(1)}, bf16[512,128]{1,0:T(8,128)(2,1)S(1)}, u32[]{:S(2)}, u32[]{:S(2)}) collective-permute-start(bf16[512,128]{1,0:T(8,128)(2,1)S(1)} %get-tuple-element.83), channel_id=1, source_target_pairs={{0,32},{32,64},{64,96},{96,0},{1,33},{33,65},{65,97},{97,1},{2,34}... | collective-permute-start | bytes 393224 | tf_op jit(solution)/shard_map/second_layer/ppermute | solution.py:453
  133.9 14.7 %collective-permute-start.13 = (bf16[1024,128]{1,0:T(8,128)(2,1)S(1)}, bf16[1024,128]{1,0:T(8,128)(2,1)S(1)}, u32[]{:S(2)}, u32[]{:S(2)}) collective-permute-start(bf16[1024,128]{1,0:T(8,128)(2,1)S(1)} %collective-permute-done.7), channel_id=1, source_target_pairs={{0,96},{32,0},{64,32},{96,64},{1,97},{33,1},{65,33},{97,65},{2,98}... | collective-permute-start | bytes 786440 | tf_op jit(solution)/shard_map/slope_exchange/ppermute | solution.py:453
  135.6 13.0 %collective-permute-start.12 = (bf16[1024,128]{1,0:T(8,128)(2,1)S(1)}, bf16[1024,128]{1,0:T(8,128)(2,1)S(1)}, u32[]{:S(2)}, u32[]{:S(2)}) collective-permute-start(bf16[1024,128]{1,0:T(8,128)(2,1)S(1)} %collective-permute-done.8), channel_id=1, source_target_pairs={{0,32},{32,64},{64,96},{96,0},{1,33},{33,65},{65,97},{97,1},{2,34}... | collective-permute-start | bytes 786440 | tf_op jit(solution)/shard_map/slope_exchange/ppermute | solution.py:453
  138.7 17.1 %collective-permute-start.11 = (bf16[16,80,128]{2,1,0:T(8,128)(2,1)S(1)}, bf16[16,80,128]{2,1,0:T(8,128)(2,1)S(1)}, u32[]{:S(2)}, u32[]{:S(2)}) collective-permute-start(bf16[16,80,128]{2,1,0:T(8,128)(2,1)S(1)} %get-tuple-element.67), channel_id=1, source_target_pairs={{0,1},{1,0},{2,3},{3,2},{4,5},{5,4},{6,7},{7,6},{8,9},{9,8},{10,11... | collective-permute-start | bytes 983048 | tf_op jit(solution)/shard_map/gradients/ppermute | solution.py:528
  149.4 6.4 %collective-permute-start.14 = (bf16[16,16,128]{2,1,0:T(8,128)(2,1)S(1)}, bf16[16,16,128]{2,1,0:T(8,128)(2,1)S(1)}, u32[]{:S(2)}, u32[]{:S(2)}) collective-permute-start(bf16[16,16,128]{2,1,0:T(8,128)(2,1)S(1)} %get-tuple-element.69), channel_id=1, source_target_pairs={{0,1},{1,0},{2,3},{3,2},{4,5},{5,4},{6,7},{7,6},{8,9},{9,8},{10,11... | collective-permute-start | bytes 196616 | tf_op jit(solution)/shard_map/gradients/ppermute | solution.py:528
  168.8 11.9 %all-to-all-start.3 = ((bf16[16,96,128]{2,1,0:T(8,128)(2,1)}), bf16[16,96,128]{2,1,0:T(8,128)(2,1)S(1)}, u32[]{:S(2)}, u32[]{:S(2)}) async-start(bf16[16,96,128]{2,1,0:T(8,128)(2,1)} %sum_and_spread.1), calls=%async_computation.3 | async-start | bytes 786432 | tf_op jit(solution)/shard_map/gradients/all_to_all | solution.py:531
  172.3 5.4 %collective-permute-start.15 = (bf16[512,128]{1,0:T(8,128)(2,1)S(1)}, bf16[512,128]{1,0:T(8,128)(2,1)S(1)}, u32[]{:S(2)}, u32[]{:S(2)}) collective-permute-start(bf16[512,128]{1,0:T(8,128)(2,1)S(1)} %get-tuple-element.82), channel_id=1, source_target_pairs={{0,64},{32,96},{64,0},{96,32},{1,65},{33,97},{65,1},{97,33},{2,66}... | collective-permute-start | bytes 393224 | tf_op jit(solution)/shard_map/second_layer/ppermute | solution.py:453
  172.8 6.8 %collective-permute-start.16 = (bf16[512,128]{1,0:T(8,128)(2,1)S(1)}, bf16[512,128]{1,0:T(8,128)(2,1)S(1)}, u32[]{:S(2)}, u32[]{:S(2)}) collective-permute-start(bf16[512,128]{1,0:T(8,128)(2,1)S(1)} %get-tuple-element.81), channel_id=1, source_target_pairs={{0,96},{32,0},{64,32},{96,64},{1,97},{33,1},{65,33},{97,65},{2,98}... | collective-permute-start | bytes 393224 | tf_op jit(solution)/shard_map/second_layer/ppermute | solution.py:453
  180.7 4.0 %collective-permute-start.17 = (bf16[16,96,128]{2,1,0:T(8,128)(2,1)S(1)}, bf16[16,96,128]{2,1,0:T(8,128)(2,1)S(1)}, u32[]{:S(2)}, u32[]{:S(2)}) collective-permute-start(bf16[16,96,128]{2,1,0:T(8,128)(2,1)S(1)} %all-to-all-done.3.mine_ref), channel_id=1, source_target_pairs={{0,1},{1,0},{2,3},{3,2},{4,5},{5,4},{6,7},{7,6},{8,9},{9,8},{10,11... | collective-permute-start | bytes 1179656 | tf_op jit(solution)/shard_map/gradients/ppermute | solution.py:528

commit v9 on v8

--- a/solution.py
+++ b/solution.py
@@ -194,7 +194,7 @@
     pick_rows(idx_ref, step * rows, rows, low, high, out_ref)
 
 
-def gather_rows(table, idx, rows=1024):
+def gather_rows(table, idx, rows=2048):
     total = idx.shape[0]
     own_rows, width = table.shape
     return pl.pallas_call(

time: 187 us -> 187 us (level)
  no operation moved by 1% of the time
where the time goes in v9:
time: 187 us
  Pallas kernels  53.3 us (29%)
  waiting for transfers between devices  49.4 us (26%)
  starting transfers between devices  44.2 us (24%)
  blocking collectives  28 us (15%)
  matrix products  5.53 us (3%)
  local copies, waits for them, and re-layouts  3.09 us (2%)
  other arithmetic  2.07 us (1%)
    all_to_all x1, waiting for transfers between devices, exchange(): lax.all_to_all(value, 'wide', split_axis=0, concat_axis=0, tiled=True)  31.1 us
    pallas_call x1, Pallas kernels, first_layer(): pl.pallas_call(functools.partial(layer_kernel, list_width), grid_spec=plt...  18.3 us
    ppermute x3, starting transfers between devices, swap(): return lax.ppermute(value, 'wide', [(i, i ^ 1) for i in range(peers)])  18 us
    ppermute x15, starting transfers between devices, shift(): lax.ppermute(value, 'blk', [(i, (i + by) % quarters) for i in range(quart...  17.6 us
    all_to_all x1, blocking collectives, exchange(): lax.all_to_all(value, 'wide', split_axis=0, concat_axis=0, tiled=True)  16 us
    pallas_call x2, Pallas kernels, neighbour_counts(): pl.pallas_call(count_kernel, grid=(targets // 16 // block_groups,), in_sp...  15.7 us
    ppermute x15, waiting for transfers between devices, shift(): lax.ppermute(value, 'blk', [(i, (i + by) % quarters) for i in range(quart...  15.6 us
    pallas_call x1, Pallas kernels, gather_rows(): pl.pallas_call(gather_kernel, grid=(total // rows,), in_specs=[pl.BlockSp...  12.9 us
  transfers between devices with their start and end apart: 20, of which 11 were waited for; matrix products, arithmetic and copies ran while one was open for 5% of the time, Pallas kernels for 9%

profile of v9, /device:TPU:1, one launch (start us, length us, event | category | flops | bytes accessed | tf_op | source)
XLA Modules:
  0.0 186.6 jit_solution(16198988367673839994)
XLA Ops:
  0.6 2.9 %request_table.1 = (s32[32,1,256]{2,1,0:T(1,128)}, s32[32,128]{1,0:T(8,128)}) custom-call(s32[32,128]{1,0:T(8,128)} %bitcast.25, s32[32,128]{1,0:T(8,128)} %bitcast.26), custom_call_target="tpu_custom_call" | custom-call | tf_op jit(solution)/shard_map/requests/request_table/pallas_call | solution.py:66
  3.6 16.0 %all_to_all.20 = s32[32,1,256]{2,1,0:T(1,128)} all-to-all(s32[32,1,256]{2,1,0:T(1,128)} %get-tuple-element.43), channel_id=1, replica_groups=mesh['blk'=4,'wide'=32] {'wide'}, dimensions={0} | all-to-all | bytes 65536 | tf_op jit(solution)/shard_map/requests/all_to_all | solution.py:456
  19.5 12.9 %gather_rows.1 = bf16[8192,256]{1,0:T(8,128)(2,1)} custom-call(s32[8192]{0:T(1024)} %bitcast.24, bf16[8192,256]{1,0:T(8,128)(2,1)} %table_ref.1), custom_call_target="tpu_custom_call" | custom-call | tf_op jit(solution)/shard_map/rows/gather_rows/pallas_call | solution.py:200
  32.5 5.0 %all-to-all-start.1 = ((bf16[32,256,256]{2,1,0:T(8,128)(2,1)}), bf16[32,256,256]{2,1,0:T(8,128)(2,1)}, u32[]{:S(2)}, u32[]{:S(2)}) async-start(bf16[32,256,256]{2,1,0:T(8,128)(2,1)} %bitcast.23), calls=%async_computation.1 | async-start | bytes 8388608 | tf_op jit(solution)/shard_map/rows/all_to_all | solution.py:456
  38.7 2.6 %neighbour_counts.3 = bf16[512,2048]{1,0:T(8,128)(2,1)S(1)} custom-call(s32[32,256]{1,0:T(8,128)S(1)} %reshape.46.idx_ref), custom_call_target="tpu_custom_call" | custom-call | flops 536870912 | bytes 2097152 | tf_op jit(solution)/shard_map/beside_rows/neighbour_counts/pallas_call | solution.py:112
  43.5 13.1 %neighbour_counts.2.counts_ref = bf16[2048,4096]{1,0:T(8,128)(2,1)} custom-call(s32[128,256]{1,0:T(8,128)S(1)} %reshape.45.idx_ref), custom_call_target="tpu_custom_call" | custom-call | flops 4294967296 | bytes 16777216 | tf_op jit(solution)/shard_map/beside_rows/neighbour_counts/pallas_call | solution.py:112
  56.7 31.1 %all-to-all-done.1 = bf16[32,256,256]{2,1,0:T(8,128)(2,1)} async-done(((bf16[32,256,256]{2,1,0:T(8,128)(2,1)}), bf16[32,256,256]{2,1,0:T(8,128)(2,1)}, u32[]{:S(2)}, u32[]{:S(2)}) %all-to-all-start.1) | async-done | bytes 4194336 | tf_op jit(solution)/shard_map/rows/all_to_all | solution.py:456
  87.8 18.3 %first_layer.1 = (bf16[1024,128]{1,0:T(8,128)(2,1)}, bf16[1024,128]{1,0:T(8,128)(2,1)}, bf16[1024,128]{1,0:T(8,128)(2,1)S(1)}, bf16[1024,128]{1,0:T(8,128)(2,1)S...) custom-call(s32[4096]{0:T(1024)} %bitcast.27, ...), custom_call_target="tpu_custom_call" | custom-call | tf_op jit(solution)/shard_map/first_layer/first_layer/pallas_call | solution.py:274
  106.1 1.7 collective-permute-start
  107.8 2.2 %collective-permute-start.3 = (bf16[1024,128]{1,0:T(8,128)(2,1)}, bf16[1024,128]{1,0:T(8,128)(2,1)S(1)}, u32[]{:S(2)}, u32[]{:S(2)}) collective-permute-start(bf16[1024,128]{1,0:T(8,128)(2,1)} %get-tuple-element.57), channel_id=1, source_target_pairs={{0,96},{32,0},{64,32},{96,64},{1,97},{33,1},{65,33},{97,65},{2,98}... | collective-permute-start | bytes 786440 | tf_op jit(solution)/shard_map/pre_act_exchange/ppermute | solution.py:453
  110.1 1.4 collective-permute-start.2
  111.4 2.5 %collective-permute-done.right = bf16[1024,128]{1,0:T(8,128)(2,1)S(1)} collective-permute-done((bf16[1024,128]{1,0:T(8,128)(2,1)}, bf16[1024,128]{1,0:T(8,128)(2,1)S(1)}, u32[]{:S(2)}, u32[]{:S(2)}) %collective-permute-start) | collective-permute-done | bytes 262176 | tf_op jit(solution)/shard_map/pre_act_exchange/ppermute | solution.py:453
  114.2 1.2 collective-permute-start.4
  115.3 1.8 collective-permute-start.5
  117.1 1.1 convert_add_fusion.1
  118.3 2.2 %collective-permute-done.1.up = bf16[1024,128]{1,0:T(8,128)(2,1)S(1)} collective-permute-done((bf16[1024,128]{1,0:T(8,128)(2,1)S(1)}, bf16[1024,128]{1,0:T(8,128)(2,1)S(1)}, u32[]{:S(2)}, u32[]{:S(2)}) %collective-permute-start.1) | collective-permute-done | bytes 262176 | tf_op jit(solution)/shard_map/pre_act_exchange/ppermute | solution.py:453
  120.9 3.2 %collective-permute-done.4.up = bf16[1024,128]{1,0:T(8,128)(2,1)S(1)} collective-permute-done((bf16[1024,128]{1,0:T(8,128)(2,1)S(1)}, bf16[1024,128]{1,0:T(8,128)(2,1)S(1)}, u32[]{:S(2)}, u32[]{:S(2)}) %collective-permute-start.4) | collective-permute-done | bytes 262176 | tf_op jit(solution)/shard_map/pre_act_exchange/ppermute | solution.py:453
  124.5 2.9 %collective-permute-start.7 = (bf16[1024,128]{1,0:T(8,128)(2,1)S(1)}, bf16[1024,128]{1,0:T(8,128)(2,1)S(1)}, u32[]{:S(2)}, u32[]{:S(2)}) collective-permute-start(bf16[1024,128]{1,0:T(8,128)(2,1)S(1)} %get-tuple-element.64), channel_id=1, source_target_pairs={{0,96},{32,0},{64,32},{96,64},{1,97},{33,1},{65,33},{97,65},{2,98}... | collective-permute-start | bytes 786440 | tf_op jit(solution)/shard_map/slope_exchange/ppermute | solution.py:453
  127.4 2.7 %collective-permute-start.6 = (bf16[1024,128]{1,0:T(8,128)(2,1)S(1)}, bf16[1024,128]{1,0:T(8,128)(2,1)S(1)}, u32[]{:S(2)}, u32[]{:S(2)}) collective-permute-start(bf16[1024,128]{1,0:T(8,128)(2,1)S(1)} %get-tuple-element.54), channel_id=1, source_target_pairs={{0,96},{32,0},{64,32},{96,64},{1,97},{33,1},{65,33},{97,65},{2,98}... | collective-permute-start | bytes 786440 | tf_op jit(solution)/shard_map/slope_exchange/ppermute | solution.py:453
  132.3 1.0 copy-done.7
  134.1 1.7 collective-permute-start.13
  137.3 1.5 collective-permute-done.10
  138.9 9.9 %collective-permute-start.11 = (bf16[16,80,128]{2,1,0:T(8,128)(2,1)S(1)}, bf16[16,80,128]{2,1,0:T(8,128)(2,1)S(1)}, u32[]{:S(2)}, u32[]{:S(2)}) collective-permute-start(bf16[16,80,128]{2,1,0:T(8,128)(2,1)S(1)} %get-tuple-element.67), channel_id=1, source_target_pairs={{0,1},{1,0},{2,3},{3,2},{4,5},{5,4},{6,7},{7,6},{8,9},{9,8},{10,11... | collective-permute-start | bytes 983048 | tf_op jit(solution)/shard_map/gradients/ppermute | solution.py:528
  149.6 5.5 %collective-permute-start.14 = (bf16[16,16,128]{2,1,0:T(8,128)(2,1)S(1)}, bf16[16,16,128]{2,1,0:T(8,128)(2,1)S(1)}, u32[]{:S(2)}, u32[]{:S(2)}) collective-permute-start(bf16[16,16,128]{2,1,0:T(8,128)(2,1)S(1)} %get-tuple-element.69), channel_id=1, source_target_pairs={{0,1},{1,0},{2,3},{3,2},{4,5},{5,4},{6,7},{7,6},{8,9},{9,8},{10,11... | collective-permute-start | bytes 196616 | tf_op jit(solution)/shard_map/gradients/ppermute | solution.py:528
  156.1 12.1 %all_to_all.21.got_ref = bf16[16,96,128]{2,1,0:T(8,128)(2,1)S(1)} all-to-all(bf16[16,96,128]{2,1,0:T(8,128)(2,1)S(1)} %joined.1), channel_id=1, replica_groups={{0,2,4,6,8,10,12,14,16,18,20,22,24,26,28,30},{1,3,5,7,9,11,13,15,17,19,..., dimensions={0} | all-to-all | bytes 786432 | tf_op jit(solution)/shard_map/gradients/all_to_all | solution.py:531
  169.0 3.6 %all-to-all-start.3 = ((bf16[16,96,128]{2,1,0:T(8,128)(2,1)}), bf16[16,96,128]{2,1,0:T(8,128)(2,1)S(1)}, u32[]{:S(2)}, u32[]{:S(2)}) async-start(bf16[16,96,128]{2,1,0:T(8,128)(2,1)} %sum_and_spread.1), calls=%async_computation.3 | async-start | bytes 786432 | tf_op jit(solution)/shard_map/gradients/all_to_all | solution.py:531
  173.0 1.4 collective-permute-start.16
  174.4 3.6 %collective-permute-done.15 = bf16[512,128]{1,0:T(8,128)(2,1)S(1)} collective-permute-done((bf16[512,128]{1,0:T(8,128)(2,1)S(1)}, bf16[512,128]{1,0:T(8,128)(2,1)S(1)}, u32[]{:S(2)}, u32[]{:S(2)}) %collective-permute-start.15) | collective-permute-done | bytes 131104 | tf_op jit(solution)/shard_map/second_layer/ppermute | solution.py:453
  177.9 1.8 collective-permute-done.16
  179.7 1.2 all-to-all-done.3.mine_ref
  180.9 2.6 %collective-permute-start.17 = (bf16[16,96,128]{2,1,0:T(8,128)(2,1)S(1)}, bf16[16,96,128]{2,1,0:T(8,128)(2,1)S(1)}, u32[]{:S(2)}, u32[]{:S(2)}) collective-permute-start(bf16[16,96,128]{2,1,0:T(8,128)(2,1)S(1)} %all-to-all-done.3.mine_ref), channel_id=1, source_target_pairs={{0,1},{1,0},{2,3},{3,2},{4,5},{5,4},{6,7},{7,6},{8,9},{9,8},{10,11... | collective-permute-start | bytes 1179656 | tf_op jit(solution)/shard_map/gradients/ppermute | solution.py:528
  184.9 1.8 finish.1
  (67 shorter events, 13.1 us)
Async XLA Ops:
  0.6 40.7 %copy-start = (bf16[512,512]{1,0:T(8,128)(2,1)S(1)}, bf16[512,512]{1,0:T(8,128)(2,1)}, u32[]{:S(2)}) copy-start(bf16[512,512]{1,0:T(8,128)(2,1)} %param.21) | copy-start | bytes 1572868
  32.4 5.0 %copy-start.6 = (s32[512,10]{0,1:T(8,128)S(1)}, s32[512,10]{0,1:T(8,128)}, u32[]{:S(2)}) copy-start(s32[512,10]{0,1:T(8,128)} %param.15) | copy-start | bytes 61444
  32.4 5.3 %copy-start.5 = (s32[2048,15]{0,1:T(8,128)S(1)}, s32[2048,15]{0,1:T(8,128)}, u32[]{:S(2)}) copy-start(s32[2048,15]{0,1:T(8,128)} %param.14) | copy-start | bytes 368644
  32.5 55.4 %all-to-all-start.1 = ((bf16[32,256,256]{2,1,0:T(8,128)(2,1)}), bf16[32,256,256]{2,1,0:T(8,128)(2,1)}, u32[]{:S(2)}, u32[]{:S(2)}) async-start(bf16[32,256,256]{2,1,0:T(8,128)(2,1)} %bitcast.23), calls=%async_computation.1 | async-start | bytes 8388608 | tf_op jit(solution)/shard_map/rows/all_to_all | solution.py:456
  38.2 3.1 %copy-start.3 = (bf16[128,512]{1,0:T(8,128)(2,1)S(1)}, bf16[128,512]{1,0:T(8,128)(2,1)}, u32[]{:S(2)}) copy-start(bf16[128,512]{1,0:T(8,128)(2,1)} %param.20) | copy-start | bytes 393220
  38.2 3.4 %copy-start.4 = (bf16[128,512]{1,0:T(8,128)(2,1)S(1)}, bf16[128,512]{1,0:T(8,128)(2,1)}, u32[]{:S(2)}) copy-start(bf16[128,512]{1,0:T(8,128)(2,1)} %param.19) | copy-start | bytes 393220
  41.3 1.4 copy-start.1
  87.8 22.2 %copy-start.8 = (bf16[128]{0:T(256)(128)(2,1)S(1)}, bf16[128]{0:T(256)(128)(2,1)}, u32[]{:S(2)}) copy-start(bf16[128]{0:T(256)(128)(2,1)} %param.18) | copy-start | bytes 772
  106.1 7.8 %collective-permute-start = (bf16[1024,128]{1,0:T(8,128)(2,1)}, bf16[1024,128]{1,0:T(8,128)(2,1)S(1)}, u32[]{:S(2)}, u32[]{:S(2)}) collective-permute-start(bf16[1024,128]{1,0:T(8,128)(2,1)} %get-tuple-element.48), channel_id=1, source_target_pairs={{0,32},{32,64},{64,96},{96,0},{1,33},{33,65},{65,97},{97,1},{2,34}... | collective-permute-start | bytes 786440 | tf_op jit(solution)/shard_map/pre_act_exchange/ppermute | solution.py:453
  107.8 6.2 %collective-permute-start.3 = (bf16[1024,128]{1,0:T(8,128)(2,1)}, bf16[1024,128]{1,0:T(8,128)(2,1)S(1)}, u32[]{:S(2)}, u32[]{:S(2)}) collective-permute-start(bf16[1024,128]{1,0:T(8,128)(2,1)} %get-tuple-element.57), channel_id=1, source_target_pairs={{0,96},{32,0},{64,32},{96,64},{1,97},{33,1},{65,33},{97,65},{2,98}... | collective-permute-start | bytes 786440 | tf_op jit(solution)/shard_map/pre_act_exchange/ppermute | solution.py:453
  110.1 8.2 %collective-permute-start.2 = (bf16[1024,128]{1,0:T(8,128)(2,1)S(1)}, bf16[1024,128]{1,0:T(8,128)(2,1)S(1)}, u32[]{:S(2)}, u32[]{:S(2)}) collective-permute-start(bf16[1024,128]{1,0:T(8,128)(2,1)S(1)} %get-tuple-element.49), channel_id=1, source_target_pairs={{0,96},{32,0},{64,32},{96,64},{1,97},{33,1},{65,33},{97,65},{2,98}... | collective-permute-start | bytes 786440 | tf_op jit(solution)/shard_map/pre_act_exchange/ppermute | solution.py:453
  114.0 6.5 %collective-permute-start.1 = (bf16[1024,128]{1,0:T(8,128)(2,1)S(1)}, bf16[1024,128]{1,0:T(8,128)(2,1)S(1)}, u32[]{:S(2)}, u32[]{:S(2)}) collective-permute-start(bf16[1024,128]{1,0:T(8,128)(2,1)S(1)} %added.2), channel_id=1, source_target_pairs={{0,32},{32,64},{64,96},{96,0},{1,33},{33,65},{65,97},{97,1},{2,34}... | collective-permute-start | bytes 786440 | tf_op jit(solution)/shard_map/pre_act_exchange/ppermute | solution.py:453
  114.2 10.0 %collective-permute-start.4 = (bf16[1024,128]{1,0:T(8,128)(2,1)S(1)}, bf16[1024,128]{1,0:T(8,128)(2,1)S(1)}, u32[]{:S(2)}, u32[]{:S(2)}) collective-permute-start(bf16[1024,128]{1,0:T(8,128)(2,1)S(1)} %get-tuple-element.60), channel_id=1, source_target_pairs={{0,32},{32,64},{64,96},{96,0},{1,33},{33,65},{65,97},{97,1},{2,34}... | collective-permute-start | bytes 786440 | tf_op jit(solution)/shard_map/pre_act_exchange/ppermute | solution.py:453
  115.3 8.8 %collective-permute-start.5 = (bf16[1024,128]{1,0:T(8,128)(2,1)S(1)}, bf16[1024,128]{1,0:T(8,128)(2,1)S(1)}, u32[]{:S(2)}, u32[]{:S(2)}) collective-permute-start(bf16[1024,128]{1,0:T(8,128)(2,1)S(1)} %added.3), channel_id=1, source_target_pairs={{0,96},{32,0},{64,32},{96,64},{1,97},{33,1},{65,33},{97,65},{2,98}... | collective-permute-start | bytes 786440 | tf_op jit(solution)/shard_map/pre_act_exchange/ppermute | solution.py:453
  120.5 9.5 %copy-start.2 = (bf16[512,2048]{1,0:T(8,128)(2,1)S(1)}, bf16[512,2048]{1,0:T(8,128)(2,1)}, u32[]{:S(2)}) copy-start(bf16[512,2048]{1,0:T(8,128)(2,1)} %copy-done.1) | copy-start | bytes 6291460
  120.8 15.0 %collective-permute-start.8 = (bf16[1024,128]{1,0:T(8,128)(2,1)S(1)}, bf16[1024,128]{1,0:T(8,128)(2,1)S(1)}, u32[]{:S(2)}, u32[]{:S(2)}) collective-permute-start(bf16[1024,128]{1,0:T(8,128)(2,1)S(1)} %get-tuple-element.54), channel_id=1, source_target_pairs={{0,32},{32,64},{64,96},{96,0},{1,33},{33,65},{65,97},{97,1},{2,34}... | collective-permute-start | bytes 786440 | tf_op jit(solution)/shard_map/slope_exchange/ppermute | solution.py:453
  124.5 9.6 %collective-permute-start.7 = (bf16[1024,128]{1,0:T(8,128)(2,1)S(1)}, bf16[1024,128]{1,0:T(8,128)(2,1)S(1)}, u32[]{:S(2)}, u32[]{:S(2)}) collective-permute-start(bf16[1024,128]{1,0:T(8,128)(2,1)S(1)} %get-tuple-element.64), channel_id=1, source_target_pairs={{0,96},{32,0},{64,32},{96,64},{1,97},{33,1},{65,33},{97,65},{2,98}... | collective-permute-start | bytes 786440 | tf_op jit(solution)/shard_map/slope_exchange/ppermute | solution.py:453
  127.4 9.1 %collective-permute-start.9 = (bf16[1024,128]{1,0:T(8,128)(2,1)S(1)}, bf16[1024,128]{1,0:T(8,128)(2,1)S(1)}, u32[]{:S(2)}, u32[]{:S(2)}) collective-permute-start(bf16[1024,128]{1,0:T(8,128)(2,1)S(1)} %get-tuple-element.64), channel_id=1, source_target_pairs={{0,32},{32,64},{64,96},{96,0},{1,33},{33,65},{65,97},{97,1},{2,34}... | collective-permute-start | bytes 786440 | tf_op jit(solution)/shard_map/slope_exchange/ppermute | solution.py:453
  127.4 9.1 %collective-permute-start.6 = (bf16[1024,128]{1,0:T(8,128)(2,1)S(1)}, bf16[1024,128]{1,0:T(8,128)(2,1)S(1)}, u32[]{:S(2)}, u32[]{:S(2)}) collective-permute-start(bf16[1024,128]{1,0:T(8,128)(2,1)S(1)} %get-tuple-element.54), channel_id=1, source_target_pairs={{0,96},{32,0},{64,32},{96,64},{1,97},{33,1},{65,33},{97,65},{2,98}... | collective-permute-start | bytes 786440 | tf_op jit(solution)/shard_map/slope_exchange/ppermute | solution.py:453
  131.7 1.6 copy-start.7
  132.1 6.7 %collective-permute-start.10 = (bf16[512,128]{1,0:T(8,128)(2,1)S(1)}, bf16[512,128]{1,0:T(8,128)(2,1)S(1)}, u32[]{:S(2)}, u32[]{:S(2)}) collective-permute-start(bf16[512,128]{1,0:T(8,128)(2,1)S(1)} %get-tuple-element.83), channel_id=1, source_target_pairs={{0,32},{32,64},{64,96},{96,0},{1,33},{33,65},{65,97},{97,1},{2,34}... | collective-permute-start | bytes 393224 | tf_op jit(solution)/shard_map/second_layer/ppermute | solution.py:453
  134.1 14.7 %collective-permute-start.13 = (bf16[1024,128]{1,0:T(8,128)(2,1)S(1)}, bf16[1024,128]{1,0:T(8,128)(2,1)S(1)}, u32[]{:S(2)}, u32[]{:S(2)}) collective-permute-start(bf16[1024,128]{1,0:T(8,128)(2,1)S(1)} %collective-permute-done.7), channel_id=1, source_target_pairs={{0,96},{32,0},{64,32},{96,64},{1,97},{33,1},{65,33},{97,65},{2,98}... | collective-permute-start | bytes 786440 | tf_op jit(solution)/shard_map/slope_exchange/ppermute | solution.py:453
  135.8 13.0 %collective-permute-start.12 = (bf16[1024,128]{1,0:T(8,128)(2,1)S(1)}, bf16[1024,128]{1,0:T(8,128)(2,1)S(1)}, u32[]{:S(2)}, u32[]{:S(2)}) collective-permute-start(bf16[1024,128]{1,0:T(8,128)(2,1)S(1)} %collective-permute-done.8), channel_id=1, source_target_pairs={{0,32},{32,64},{64,96},{96,0},{1,33},{33,65},{65,97},{97,1},{2,34}... | collective-permute-start | bytes 786440 | tf_op jit(solution)/shard_map/slope_exchange/ppermute | solution.py:453
  138.9 17.1 %collective-permute-start.11 = (bf16[16,80,128]{2,1,0:T(8,128)(2,1)S(1)}, bf16[16,80,128]{2,1,0:T(8,128)(2,1)S(1)}, u32[]{:S(2)}, u32[]{:S(2)}) collective-permute-start(bf16[16,80,128]{2,1,0:T(8,128)(2,1)S(1)} %get-tuple-element.67), channel_id=1, source_target_pairs={{0,1},{1,0},{2,3},{3,2},{4,5},{5,4},{6,7},{7,6},{8,9},{9,8},{10,11... | collective-permute-start | bytes 983048 | tf_op jit(solution)/shard_map/gradients/ppermute | solution.py:528
  149.6 6.4 %collective-permute-start.14 = (bf16[16,16,128]{2,1,0:T(8,128)(2,1)S(1)}, bf16[16,16,128]{2,1,0:T(8,128)(2,1)S(1)}, u32[]{:S(2)}, u32[]{:S(2)}) collective-permute-start(bf16[16,16,128]{2,1,0:T(8,128)(2,1)S(1)} %get-tuple-element.69), channel_id=1, source_target_pairs={{0,1},{1,0},{2,3},{3,2},{4,5},{5,4},{6,7},{7,6},{8,9},{9,8},{10,11... | collective-permute-start | bytes 196616 | tf_op jit(solution)/shard_map/gradients/ppermute | solution.py:528
  169.0 11.9 %all-to-all-start.3 = ((bf16[16,96,128]{2,1,0:T(8,128)(2,1)}), bf16[16,96,128]{2,1,0:T(8,128)(2,1)S(1)}, u32[]{:S(2)}, u32[]{:S(2)}) async-start(bf16[16,96,128]{2,1,0:T(8,128)(2,1)} %sum_and_spread.1), calls=%async_computation.3 | async-start | bytes 786432 | tf_op jit(solution)/shard_map/gradients/all_to_all | solution.py:531
  172.5 5.4 %collective-permute-start.15 = (bf16[512,128]{1,0:T(8,128)(2,1)S(1)}, bf16[512,128]{1,0:T(8,128)(2,1)S(1)}, u32[]{:S(2)}, u32[]{:S(2)}) collective-permute-start(bf16[512,128]{1,0:T(8,128)(2,1)S(1)} %get-tuple-element.82), channel_id=1, source_target_pairs={{0,64},{32,96},{64,0},{96,32},{1,65},{33,97},{65,1},{97,33},{2,66}... | collective-permute-start | bytes 393224 | tf_op jit(solution)/shard_map/second_layer/ppermute | solution.py:453
  173.0 6.8 %collective-permute-start.16 = (bf16[512,128]{1,0:T(8,128)(2,1)S(1)}, bf16[512,128]{1,0:T(8,128)(2,1)S(1)}, u32[]{:S(2)}, u32[]{:S(2)}) collective-permute-start(bf16[512,128]{1,0:T(8,128)(2,1)S(1)} %get-tuple-element.81), channel_id=1, source_target_pairs={{0,96},{32,0},{64,32},{96,64},{1,97},{33,1},{65,33},{97,65},{2,98}... | collective-permute-start | bytes 393224 | tf_op jit(solution)/shard_map/second_layer/ppermute | solution.py:453
  180.9 4.0 %collective-permute-start.17 = (bf16[16,96,128]{2,1,0:T(8,128)(2,1)S(1)}, bf16[16,96,128]{2,1,0:T(8,128)(2,1)S(1)}, u32[]{:S(2)}, u32[]{:S(2)}) collective-permute-start(bf16[16,96,128]{2,1,0:T(8,128)(2,1)S(1)} %all-to-all-done.3.mine_ref), channel_id=1, source_target_pairs={{0,1},{1,0},{2,3},{3,2},{4,5},{5,4},{6,7},{7,6},{8,9},{9,8},{10,11... | collective-permute-start | bytes 1179656 | tf_op jit(solution)/shard_map/gradients/ppermute | solution.py:528
